TPU v7x, 32 devices: a whole 2x2x4 slice. The times are simulated.
32 devices in a mesh: section: 4 (over y, x), dp: 4 (over z), seq: 2 (over core).
Axes of the slice: x: 2, y: 2, z: 4, core: 2. Of those that a mesh axis runs over, the one named last changes fastest.
Arguments:
- tokens: bfloat16 [8, 1024, 1024], P('dp', 'seq'), may hold values from -6 to 6
- section_in: bfloat16 [4, 1024, 5504], P('section'), may hold values from -0.1875 to 0.1875
- section_out: bfloat16 [4, 2752, 1024], P('section')
- gains: float32 [4, 1024], P('section'), may hold values from 0.25 to 1.75
- bounds: int32 [8, 4], P('dp'), may hold values from 1 to 1023, as said below
- cotangent: bfloat16 [8, 1024, 1024], P('dp', 'seq'), may hold values from -6 to 6
Outputs:
- block_out: bfloat16 [8, 1024, 1024], P('dp', 'seq', 'section')
- grad_tokens: bfloat16 [8, 1024, 1024], P('dp', 'seq', 'section')
- grad_in: float32 [4, 1024, 5504], P('section', ('dp', 'seq'))
- grad_out: float32 [4, 2752, 1024], P('section', ('dp', 'seq'))
- grad_gains: float32 [4, 1024], P('section', ('dp', 'seq'))
Inputs may be any that keep to these rules, and one draw needn't show every extreme that they name: `bounds`: each row's four start positions rise strictly; in every row one document runs from the first block of 512 positions into the last.
All inputs are finite; a program needn't handle non-finite values.
Results may differ from a plain program's by a relative error of at most 0.04.
Values may be sent and summed in bfloat16 or wider, within the bound.
No kernel may reach another device: no remote copies, remote signals or barrier semaphores. Data moves between devices by JAX's collectives and lax.ppermute only.
A program may use at most 320 MiB of HBM per device.

v0:
```python
import math

import jax
import jax.numpy as jnp
from jax import lax
from jax.sharding import PartitionSpec as P

HEADS = 16
FEAT_DIM = 16
WINDOW = 64


highest = lax.Precision.HIGHEST
epsilon = 1e-06


def prefix(value, axis, join, neutral, backward):
    count = lax.axis_size(axis)
    place = lax.axis_index(axis)
    ahead = count - 1 - place if backward else place
    gathered = jax.tree.map(
        lambda a, kind: lax.all_gather(a.astype(kind), axis),
        value,
        jax.tree.map(lambda a: jnp.bfloat16 if a.dtype == jnp.float32 else a.dtype, value),
    )
    state = jax.tree.map(lambda a, e: jnp.zeros_like(a) + jnp.asarray(e, a.dtype), value, neutral)

    def one(hop, state):
        source = count - 1 - hop if backward else hop
        return join(
            state,
            jax.tree.map(
                lambda a, own: lax.dynamic_index_in_dim(a, source, 0, False).astype(own.dtype),
                gathered,
                value,
            ),
        )

    return lax.fori_loop(0, ahead, one, state)


def shortened(value):

    def short(part):
        return part.astype(jnp.bfloat16) if part.dtype == jnp.float32 else part

    return jax.tree.map(short, value)


def passed_along(value, axis, by):
    length = lax.axis_size(axis)
    pairs = [(i, i + by) for i in range(length) if 0 <= i + by < length]
    return lax.ppermute(value, axis, pairs)


def matmul(left_side, right_side):
    return jnp.dot(left_side, right_side, preferred_element_type=jnp.float32)


def inner_rows(left_side, right_side):
    return lax.dot_general(
        left_side, right_side, (((0,), (0,)), ((), ())), preferred_element_type=jnp.float32
    )


def inner_cols(left_side, right_side):
    return lax.dot_general(
        left_side, right_side, (((1,), (1,)), ((), ())), preferred_element_type=jnp.float32
    )


def widen_columns(block_rows, full_size):
    return jnp.pad(block_rows, ((0, 0), (0, full_size - block_rows.shape[1])))


def widen_rows(block_rows, full_size):
    return jnp.pad(block_rows, ((0, full_size - block_rows.shape[0]), (0, 0)))


def rms_forward(inputs, gain_row):
    inverse = lax.rsqrt(jnp.mean(inputs * inputs, axis=-1, keepdims=True) + epsilon)
    return (inputs * inverse * gain_row, inverse)


def rms_backward(inputs, gain_row, inverse, grad_normed):
    scaled = grad_normed * gain_row
    grad_inputs = inverse * scaled - inputs * inverse**3 * jnp.mean(
        scaled * inputs, axis=-1, keepdims=True
    )
    grad_gain = jnp.sum(grad_normed * inputs * inverse, axis=0)
    return (grad_inputs, grad_gain)


def doc_numbers(starts, positions):
    return jnp.sum((starts[None, :] <= positions[:, None]).astype(jnp.int32), axis=1)


def feature_total():
    return 1 + FEAT_DIM + FEAT_DIM * FEAT_DIM


def block_docs(starts, seq_index, block_len):
    offset = seq_index * block_len
    positions = offset + jnp.arange(block_len, dtype=jnp.int32)
    doc_ids = doc_numbers(starts, positions)
    before = doc_numbers(starts, jnp.reshape(offset - 1, (1,)))[0]
    return (offset, positions, doc_ids, before)


def taylor_features(vectors):
    row_count, head_count, feat_width = vectors.shape
    square = (vectors[:, :, :, None] * vectors[:, :, None, :]).reshape(
        row_count, head_count, feat_width * feat_width
    )
    constant = jnp.ones((row_count, head_count, 1), jnp.float32)
    return jnp.concatenate(
        [constant, vectors / feat_width**0.25, square / math.sqrt(2.0 * feat_width)], axis=2
    )


def taylor_features_back(vectors, grad_feat):
    row_count, head_count, feat_width = vectors.shape
    linear = grad_feat[:, :, 1 : 1 + feat_width] / feat_width**0.25
    square = grad_feat[:, :, 1 + feat_width :].reshape(
        row_count, head_count, feat_width, feat_width
    ) / math.sqrt(2.0 * feat_width)
    return (
        linear
        + jnp.einsum("thij,thj->thi", square, vectors, precision=highest)
        + jnp.einsum("thji,thj->thi", square, vectors, precision=highest)
    )


def carry_state(earlier, latter):
    carried = 1.0 - latter[2]
    return (
        latter[0] + carried * earlier[0],
        latter[1] + carried * earlier[1],
        jnp.maximum(earlier[2], latter[2]),
    )


def state_identity(feature_count, model_width):
    return (
        jnp.zeros((feature_count, model_width), jnp.float32),
        jnp.zeros((feature_count, HEADS), jnp.float32),
        jnp.zeros((), jnp.float32),
    )


def forward_links(state, halo):
    feature_count, model_width = state[0].shape
    incoming = prefix(state, "seq", carry_state, state_identity(feature_count, model_width), False)
    halo_rows = jax.tree.map(
        lambda part, own: part.astype(own.dtype), passed_along(shortened(halo), "seq", 1), halo
    )
    return (incoming, halo_rows)


def backward_links(state, halo):
    feature_count, model_width = state[0].shape
    outgoing = prefix(state, "seq", carry_state, state_identity(feature_count, model_width), True)
    sent_back = jax.tree.map(
        lambda part, own: part.astype(own.dtype), passed_along(shortened(halo), "seq", -1), halo
    )
    return (outgoing, sent_back)


def key_tail(keys_rows, values, doc_ids, block_len):
    key_feat = taylor_features(keys_rows.astype(jnp.float32))
    tail_mask = (doc_ids == doc_ids[block_len - 1]).astype(jnp.float32)[:, None, None]
    return (key_feat * tail_mask, tail_mask, values.astype(jnp.float32))


def taylor_front(section_entry, gain_row, pack_in, starts, seq_index):
    block_len, model_width = section_entry.shape
    qk_cols = HEADS * FEAT_DIM
    value_dim = model_width // HEADS
    feature_count = feature_total()
    offset, positions, doc_ids, before = block_docs(starts, seq_index, block_len)
    normed, inverse = rms_forward(section_entry.astype(jnp.float32), gain_row)
    projected = matmul(normed.astype(jnp.bfloat16), pack_in[:, : 2 * qk_cols + model_width]).astype(
        jnp.bfloat16
    )
    keys_rows = projected[:, qk_cols : 2 * qk_cols].reshape(block_len, HEADS, FEAT_DIM)
    values = projected[:, 2 * qk_cols :].reshape(block_len, HEADS, value_dim)
    tail_feat, tail_mask, values_wide = key_tail(keys_rows, values, doc_ids, block_len)
    state_vals = jnp.einsum("thf,thc->fhc", tail_feat, values_wide, precision=highest).reshape(
        feature_count, model_width
    )
    state_norm = jnp.sum(tail_feat, axis=0).T
    opened = (doc_ids[block_len - 1] != before).astype(jnp.float32)
    return (
        widen_columns(projected, 3 * model_width),
        (state_vals, state_norm, opened),
        jnp.zeros((WINDOW, 2 * model_width), jnp.bfloat16),
    )


def window_front(section_entry, gain_row, pack_in):
    block_len, model_width = section_entry.shape
    normed, inverse = rms_forward(section_entry.astype(jnp.float32), gain_row)
    projected = matmul(normed.astype(jnp.bfloat16), pack_in[:, : 3 * model_width]).astype(
        jnp.bfloat16
    )
    return (
        projected,
        state_identity(feature_total(), model_width),
        projected[block_len - WINDOW :, model_width:],
    )


def quiet_front(block_len, model_width):
    return (
        jnp.zeros((block_len, 3 * model_width), jnp.bfloat16),
        state_identity(feature_total(), model_width),
        jnp.zeros((WINDOW, 2 * model_width), jnp.bfloat16),
    )


def taylor_rest(
    section_entry, gain_row, pack_in, pack_out, starts, seq_index, projected_wide, incoming
):
    block_len, model_width = section_entry.shape
    qk_cols = HEADS * FEAT_DIM
    value_dim = model_width // HEADS
    feature_count = feature_total()
    offset, positions, doc_ids, before = block_docs(starts, seq_index, block_len)
    inputs = section_entry.astype(jnp.float32)
    normed, inverse = rms_forward(inputs, gain_row)
    normed_low = normed.astype(jnp.bfloat16)
    used_cols = pack_in[:, : 2 * qk_cols + model_width]
    projected = projected_wide[:, : 2 * qk_cols + model_width]
    queries = projected[:, :qk_cols].reshape(block_len, HEADS, FEAT_DIM)
    keys_rows = projected[:, qk_cols : 2 * qk_cols].reshape(block_len, HEADS, FEAT_DIM)
    values = projected[:, 2 * qk_cols :].reshape(block_len, HEADS, value_dim)
    scores = jnp.einsum(
        "thf,shf->hts", queries, keys_rows, preferred_element_type=jnp.float32
    ) / math.sqrt(FEAT_DIM)
    allowed = ((positions[None, :] <= positions[:, None]) & (doc_ids[None, :] == doc_ids[:, None]))[
        None
    ]
    weights = jnp.where(allowed, 1.0 + scores + 0.5 * scores * scores, 0.0)
    weights_low = weights.astype(jnp.bfloat16)
    numer_in = jnp.einsum("hts,shc->thc", weights_low, values, preferred_element_type=jnp.float32)
    denom_in = jnp.sum(weights, axis=2).T
    query_feat = taylor_features(queries.astype(jnp.float32))
    tail_feat, tail_mask, values_wide = key_tail(keys_rows, values, doc_ids, block_len)
    opened = (doc_ids[block_len - 1] != before).astype(jnp.float32)
    head_mask = (doc_ids == before).astype(jnp.float32)
    in_vals = incoming[0].reshape(feature_count, HEADS, value_dim)
    in_norm = incoming[1]
    numer_out = (
        jnp.einsum("thf,fhc->thc", query_feat, in_vals, precision=highest)
        * head_mask[:, None, None]
    )
    denom_out = (
        jnp.einsum("thf,fh->th", query_feat, in_norm, precision=highest) * head_mask[:, None]
    )
    denominator = denom_in + denom_out
    ratios = (numer_in + numer_out) / denominator[:, :, None]
    mixture = ratios.reshape(block_len, model_width).astype(jnp.bfloat16)
    output = inputs + matmul(mixture, pack_out[:model_width])
    kept_parts = (
        inputs,
        normed_low,
        inverse,
        used_cols,
        queries,
        keys_rows,
        values,
        scores,
        allowed,
        weights_low,
        query_feat,
        tail_mask,
        values_wide,
        tail_feat,
        opened,
        head_mask,
        in_vals,
        in_norm,
        denominator,
        ratios,
        mixture,
    )
    return (output, kept_parts)


def taylor_mid(
    section_entry,
    upstream,
    gain_row,
    pack_in,
    pack_out,
    starts,
    seq_index,
    projected_wide,
    incoming,
):
    output, kept_parts = taylor_rest(
        section_entry, gain_row, pack_in, pack_out, starts, seq_index, projected_wide, incoming
    )
    (
        inputs,
        normed_low,
        inverse,
        used_cols,
        queries,
        keys_rows,
        values,
        scores,
        allowed,
        weights_low,
        query_feat,
        tail_mask,
        values_wide,
        tail_feat,
        opened,
        head_mask,
        in_vals,
        in_norm,
        denominator,
        ratios,
        mixture,
    ) = kept_parts
    block_len, model_width = section_entry.shape
    value_dim = model_width // HEADS
    feature_count = feature_total()
    root_scale = math.sqrt(FEAT_DIM)
    grad_pack_out = inner_rows(mixture, upstream)
    grad_mixture = (
        inner_cols(upstream, pack_out[:model_width])
        .astype(jnp.bfloat16)
        .reshape(block_len, HEADS, value_dim)
    )
    grad_mixture_wide = grad_mixture.astype(jnp.float32)
    grad_numer = (grad_mixture_wide / denominator[:, :, None]).astype(jnp.bfloat16)
    grad_denom = -jnp.sum(grad_mixture_wide * ratios, axis=2) / denominator
    grad_weights = (
        jnp.einsum("thc,shc->hts", grad_numer, values, preferred_element_type=jnp.float32)
        + grad_denom.T[:, :, None]
    )
    grad_scores = jnp.where(allowed, grad_weights * (1.0 + scores), 0.0).astype(jnp.bfloat16)
    grad_queries = (
        jnp.einsum("hts,shf->thf", grad_scores, keys_rows, preferred_element_type=jnp.float32)
        / root_scale
    )
    grad_keys = (
        jnp.einsum("hts,thf->shf", grad_scores, queries, preferred_element_type=jnp.float32)
        / root_scale
    )
    grad_values = jnp.einsum(
        "hts,thc->shc", weights_low, grad_numer, preferred_element_type=jnp.float32
    )
    numer_back = grad_numer.astype(jnp.float32) * head_mask[:, None, None]
    denom_back = grad_denom * head_mask[:, None]
    back_vals = jnp.einsum("thf,thc->fhc", query_feat, numer_back, precision=highest).reshape(
        feature_count, model_width
    )
    back_norm = jnp.einsum("thf,th->fh", query_feat, denom_back, precision=highest)
    grad_query_feat = (
        jnp.einsum("thc,fhc->thf", numer_back, in_vals, precision=highest)
        + denom_back[:, :, None] * in_norm.T[None]
    )
    grad_queries = grad_queries + taylor_features_back(queries.astype(jnp.float32), grad_query_feat)
    grad_part = jnp.concatenate(
        [
            grad_queries.reshape(block_len, -1),
            grad_keys.reshape(block_len, -1),
            grad_values.reshape(block_len, model_width),
        ],
        axis=1,
    )
    return (
        (back_vals, back_norm, opened),
        jnp.zeros((WINDOW, 2 * model_width), jnp.float32),
        widen_columns(grad_part, 3 * model_width),
        widen_rows(grad_pack_out, pack_out.shape[0]),
    )


def taylor_tail(
    section_entry,
    upstream,
    gain_row,
    pack_in,
    starts,
    seq_index,
    projected_wide,
    grad_part,
    grad_pack_out,
    outgoing,
):
    block_len, model_width = section_entry.shape
    qk_cols = HEADS * FEAT_DIM
    value_dim = model_width // HEADS
    feature_count = feature_total()
    offset, positions, doc_ids, before = block_docs(starts, seq_index, block_len)
    inputs = section_entry.astype(jnp.float32)
    normed, inverse = rms_forward(inputs, gain_row)
    normed_low = normed.astype(jnp.bfloat16)
    used_cols = pack_in[:, : 2 * qk_cols + model_width]
    keys_rows = projected_wide[:, qk_cols : 2 * qk_cols].reshape(block_len, HEADS, FEAT_DIM)
    values = projected_wide[:, 2 * qk_cols : 2 * qk_cols + model_width].reshape(
        block_len, HEADS, value_dim
    )
    tail_feat, tail_mask, values_wide = key_tail(keys_rows, values, doc_ids, block_len)
    out_vals = outgoing[0].reshape(feature_count, HEADS, value_dim)
    grad_key_feat = (
        jnp.einsum("fhc,thc->thf", out_vals, values_wide, precision=highest) + outgoing[1].T[None]
    ) * tail_mask
    grad_keys = grad_part[:, qk_cols : 2 * qk_cols].reshape(
        block_len, HEADS, FEAT_DIM
    ) + taylor_features_back(keys_rows.astype(jnp.float32), grad_key_feat)
    grad_values = grad_part[:, 2 * qk_cols : 2 * qk_cols + model_width].reshape(
        block_len, HEADS, value_dim
    ) + jnp.einsum("thf,fhc->thc", tail_feat, out_vals, precision=highest)
    grad_projected = jnp.concatenate(
        [
            grad_part[:, :qk_cols],
            grad_keys.reshape(block_len, -1),
            grad_values.reshape(block_len, model_width),
        ],
        axis=1,
    ).astype(jnp.bfloat16)
    grad_used = inner_rows(normed_low, grad_projected)
    grad_normed = inner_cols(grad_projected, used_cols)
    grad_inputs, grad_gain = rms_backward(inputs, gain_row, inverse, grad_normed)
    return (
        upstream.astype(jnp.float32) + grad_inputs,
        widen_columns(grad_used, pack_in.shape[1]),
        grad_pack_out,
        grad_gain,
    )


def dense_pass(section_entry, gain_row, pack_in, pack_out):
    hidden_dim = pack_out.shape[0]
    inputs = section_entry.astype(jnp.float32)
    normed, inverse = rms_forward(inputs, gain_row)
    normed_low = normed.astype(jnp.bfloat16)
    gate_up = matmul(normed_low, pack_in)
    gate_rows = gate_up[:, :hidden_dim]
    up_rows = gate_up[:, hidden_dim:]
    sigmoid_gate = jax.nn.sigmoid(gate_rows)
    hidden = (gate_rows * sigmoid_gate * up_rows).astype(jnp.bfloat16)
    output = inputs + matmul(hidden, pack_out)
    return (output, (inputs, normed_low, inverse, gate_rows, up_rows, sigmoid_gate, hidden))


def dense_back(section_entry, upstream, gain_row, pack_in, pack_out):
    output, kept_parts = dense_pass(section_entry, gain_row, pack_in, pack_out)
    inputs, normed_low, inverse, gate_rows, up_rows, sigmoid_gate, hidden = kept_parts
    grad_hidden = inner_cols(upstream, pack_out)
    grad_gate = (
        grad_hidden * up_rows * sigmoid_gate * (1.0 + gate_rows * (1.0 - sigmoid_gate))
    ).astype(jnp.bfloat16)
    grad_up = (grad_hidden * gate_rows * sigmoid_gate).astype(jnp.bfloat16)
    grad_gate_up = jnp.concatenate([grad_gate, grad_up], axis=1)
    grad_pack_in = inner_rows(normed_low, grad_gate_up)
    grad_pack_out = inner_rows(hidden, upstream)
    grad_normed = inner_cols(grad_gate_up, pack_in)
    grad_inputs, grad_gain = rms_backward(inputs, gain_row, inverse, grad_normed)
    return (upstream.astype(jnp.float32) + grad_inputs, grad_pack_in, grad_pack_out, grad_gain)


def quiet_mid(block_len, model_width, hidden_dim):
    return (
        state_identity(feature_total(), model_width),
        jnp.zeros((WINDOW, 2 * model_width), jnp.float32),
        jnp.zeros((block_len, 3 * model_width), jnp.float32),
        jnp.zeros((hidden_dim, model_width), jnp.float32),
    )


def window_rest(
    section_entry, gain_row, pack_in, pack_out, starts, seq_index, projected, halo_rows
):
    block_len, model_width = section_entry.shape
    head_dim = model_width // HEADS
    offset = seq_index * block_len
    positions = offset + jnp.arange(block_len, dtype=jnp.int32)
    key_positions = offset - WINDOW + jnp.arange(block_len + WINDOW, dtype=jnp.int32)
    doc_ids = doc_numbers(starts, positions)
    key_docs = doc_numbers(starts, key_positions)
    inputs = section_entry.astype(jnp.float32)
    normed, inverse = rms_forward(inputs, gain_row)
    normed_low = normed.astype(jnp.bfloat16)
    used_cols = pack_in[:, : 3 * model_width]
    key_vals = projected[:, model_width:]
    joined = jnp.concatenate([halo_rows, key_vals], axis=0)
    queries = projected[:, :model_width].reshape(block_len, HEADS, head_dim)
    keys_rows = joined[:, :model_width].reshape(-1, HEADS, head_dim)
    values = joined[:, model_width:].reshape(-1, HEADS, head_dim)
    distance = positions[:, None] - key_positions[None, :]
    allowed = (
        (distance >= 0)
        & (distance < WINDOW)
        & (doc_ids[:, None] == key_docs[None, :])
        & (key_positions[None, :] >= 0)
    )[None]
    scores = jnp.einsum(
        "thd,shd->hts", queries, keys_rows, preferred_element_type=jnp.float32
    ) / math.sqrt(head_dim)
    masked = jnp.where(allowed, scores, -1e30)
    highest_score = jnp.max(masked, axis=2, keepdims=True)
    powered = jnp.where(allowed, jnp.exp(masked - highest_score), 0.0)
    soft_weights = powered / jnp.sum(powered, axis=2, keepdims=True)
    soft_low = soft_weights.astype(jnp.bfloat16)
    mixture = (
        jnp.einsum("hts,shd->thd", soft_low, values, preferred_element_type=jnp.float32)
        .reshape(block_len, model_width)
        .astype(jnp.bfloat16)
    )
    output = inputs + matmul(mixture, pack_out[:model_width])
    return (
        output,
        (
            inputs,
            normed_low,
            inverse,
            used_cols,
            queries,
            keys_rows,
            values,
            soft_weights,
            soft_low,
            mixture,
        ),
    )


def window_mid(
    section_entry, upstream, gain_row, pack_in, pack_out, starts, seq_index, projected, halo_rows
):
    output, kept_parts = window_rest(
        section_entry, gain_row, pack_in, pack_out, starts, seq_index, projected, halo_rows
    )
    (
        inputs,
        normed_low,
        inverse,
        used_cols,
        queries,
        keys_rows,
        values,
        soft_weights,
        soft_low,
        mixture,
    ) = kept_parts
    block_len, model_width = section_entry.shape
    head_dim = model_width // HEADS
    root_scale = math.sqrt(head_dim)
    grad_pack_out = inner_rows(mixture, upstream)
    grad_mixture = (
        inner_cols(upstream, pack_out[:model_width])
        .astype(jnp.bfloat16)
        .reshape(block_len, HEADS, head_dim)
    )
    grad_soft = jnp.einsum("thd,shd->hts", grad_mixture, values, preferred_element_type=jnp.float32)
    grad_scores = (
        soft_weights * (grad_soft - jnp.sum(soft_weights * grad_soft, axis=2, keepdims=True))
    ).astype(jnp.bfloat16)
    grad_queries = (
        jnp.einsum("hts,shd->thd", grad_scores, keys_rows, preferred_element_type=jnp.float32)
        / root_scale
    )
    grad_keys = (
        jnp.einsum("hts,thd->shd", grad_scores, queries, preferred_element_type=jnp.float32)
        / root_scale
    )
    grad_values = jnp.einsum(
        "hts,thd->shd", soft_low, grad_mixture, preferred_element_type=jnp.float32
    )
    grad_joined = jnp.concatenate(
        [grad_keys.reshape(-1, model_width), grad_values.reshape(-1, model_width)], axis=1
    )
    grad_part = jnp.concatenate(
        [grad_queries.reshape(block_len, model_width), grad_joined[WINDOW:]], axis=1
    )
    return (
        state_identity(feature_total(), model_width),
        grad_joined[:WINDOW],
        grad_part,
        widen_rows(grad_pack_out, pack_out.shape[0]),
    )


def window_tail(section_entry, upstream, gain_row, pack_in, grad_part, grad_pack_out, sent_back):
    block_len, model_width = section_entry.shape
    inputs = section_entry.astype(jnp.float32)
    normed, inverse = rms_forward(inputs, gain_row)
    normed_low = normed.astype(jnp.bfloat16)
    used_cols = pack_in[:, : 3 * model_width]
    grad_key_vals = grad_part[:, model_width:] + jnp.pad(
        sent_back, ((block_len - WINDOW, 0), (0, 0))
    )
    grad_projected = jnp.concatenate([grad_part[:, :model_width], grad_key_vals], axis=1).astype(
        jnp.bfloat16
    )
    grad_used = inner_rows(normed_low, grad_projected)
    grad_normed = inner_cols(grad_projected, used_cols)
    grad_inputs, grad_gain = rms_backward(inputs, gain_row, inverse, grad_normed)
    return (
        upstream.astype(jnp.float32) + grad_inputs,
        widen_columns(grad_used, pack_in.shape[1]),
        grad_pack_out,
        grad_gain,
    )


def local(tokens, section_in, section_out, gains, bounds, cotangent):
    section_count = lax.axis_size("section")
    section_index = lax.axis_index("section")
    seq_index = lax.axis_index("seq")
    pack_in = section_in[0]
    pack_out = section_out[0]
    gain_row = gains[0]
    micro_count, block_len, model_width = tokens.shape
    hidden_dim = pack_out.shape[0]
    last_section = section_count - 1
    turn_count = micro_count + section_count - 1

    def fronts(section_entry, starts):
        return lax.switch(
            section_index,
            [
                lambda: taylor_front(section_entry, gain_row, pack_in, starts, seq_index),
                lambda: quiet_front(block_len, model_width),
                lambda: window_front(section_entry, gain_row, pack_in),
                lambda: quiet_front(block_len, model_width),
            ],
        )

    def forward_turn(turn_index, carry):
        arrived, kept_inputs, finals = carry
        micro_index = turn_index - section_index
        is_live = (micro_index >= 0) & (micro_index < micro_count)
        slot_index = jnp.clip(micro_index, 0, micro_count - 1)
        starts = lax.dynamic_index_in_dim(bounds, slot_index, 0, keepdims=False)
        section_entry = jnp.where(
            section_index == 0,
            lax.dynamic_index_in_dim(tokens, slot_index, 0, keepdims=False),
            arrived,
        )
        projected, state, halo = fronts(section_entry, starts)
        incoming, halo_rows = forward_links(state, halo)
        output = lax.switch(
            section_index,
            [
                lambda: taylor_rest(
                    section_entry,
                    gain_row,
                    pack_in,
                    pack_out,
                    starts,
                    seq_index,
                    projected,
                    incoming,
                )[0],
                lambda: dense_pass(section_entry, gain_row, pack_in, pack_out)[0],
                lambda: window_rest(
                    section_entry,
                    gain_row,
                    pack_in,
                    pack_out,
                    starts,
                    seq_index,
                    projected,
                    halo_rows,
                )[0],
                lambda: dense_pass(section_entry, gain_row, pack_in, pack_out)[0],
            ],
        )
        output_low = output.astype(jnp.bfloat16)
        kept_inputs = jnp.where(
            is_live,
            lax.dynamic_update_index_in_dim(kept_inputs, section_entry, slot_index, 0),
            kept_inputs,
        )
        finals = jnp.where(
            is_live & (section_index == last_section),
            lax.dynamic_update_index_in_dim(finals, output_low, slot_index, 0),
            finals,
        )
        arrived = passed_along(output_low, "section", 1)
        return (arrived, kept_inputs, finals)

    start_forward = (
        jnp.zeros((block_len, model_width), jnp.bfloat16),
        jnp.zeros((micro_count, block_len, model_width), jnp.bfloat16),
        jnp.zeros((micro_count, block_len, model_width), jnp.bfloat16),
    )
    arrived, kept_inputs, finals = lax.fori_loop(0, turn_count, forward_turn, start_forward)
    totals = (
        jnp.zeros(pack_in.shape, jnp.float32),
        jnp.zeros(pack_out.shape, jnp.float32),
        jnp.zeros((model_width,), jnp.float32),
    )

    def backward_turn(turn_index, carry):
        arrived, returned, totals = carry
        micro_index = turn_index - (last_section - section_index)
        is_live = (micro_index >= 0) & (micro_index < micro_count)
        slot_index = jnp.clip(micro_index, 0, micro_count - 1)
        starts = lax.dynamic_index_in_dim(bounds, slot_index, 0, keepdims=False)
        upstream = jnp.where(
            section_index == last_section,
            lax.dynamic_index_in_dim(cotangent, slot_index, 0, keepdims=False),
            arrived,
        )
        section_entry = lax.dynamic_index_in_dim(kept_inputs, slot_index, 0, keepdims=False)
        projected, state, halo = fronts(section_entry, starts)
        incoming, halo_rows = forward_links(state, halo)
        back_state, back_halo, grad_part, grad_pack_out = lax.switch(
            section_index,
            [
                lambda: taylor_mid(
                    section_entry,
                    upstream,
                    gain_row,
                    pack_in,
                    pack_out,
                    starts,
                    seq_index,
                    projected,
                    incoming,
                ),
                lambda: quiet_mid(block_len, model_width, hidden_dim),
                lambda: window_mid(
                    section_entry,
                    upstream,
                    gain_row,
                    pack_in,
                    pack_out,
                    starts,
                    seq_index,
                    projected,
                    halo_rows,
                ),
                lambda: quiet_mid(block_len, model_width, hidden_dim),
            ],
        )
        outgoing, sent_back = backward_links(back_state, back_halo)
        results = lax.switch(
            section_index,
            [
                lambda: taylor_tail(
                    section_entry,
                    upstream,
                    gain_row,
                    pack_in,
                    starts,
                    seq_index,
                    projected,
                    grad_part,
                    grad_pack_out,
                    outgoing,
                ),
                lambda: dense_back(section_entry, upstream, gain_row, pack_in, pack_out),
                lambda: window_tail(
                    section_entry, upstream, gain_row, pack_in, grad_part, grad_pack_out, sent_back
                ),
                lambda: dense_back(section_entry, upstream, gain_row, pack_in, pack_out),
            ],
        )
        grad_entry = results[0].astype(jnp.bfloat16)
        returned = jnp.where(
            is_live & (section_index == 0),
            lax.dynamic_update_index_in_dim(returned, grad_entry, slot_index, 0),
            returned,
        )
        increments = tuple((jnp.where(is_live, member, 0.0) for member in results[1:]))
        totals = jax.tree.map(jnp.add, totals, increments)
        arrived = passed_along(grad_entry, "section", -1)
        return (arrived, returned, totals)

    start_backward = (
        jnp.zeros((block_len, model_width), jnp.bfloat16),
        jnp.zeros((micro_count, block_len, model_width), jnp.bfloat16),
        totals,
    )
    arrived, returned, totals = lax.fori_loop(0, turn_count, backward_turn, start_backward)
    totals = (
        lax.psum_scatter(totals[0], ("dp", "seq"), scatter_dimension=0, tiled=True),
        lax.psum_scatter(totals[1], ("dp", "seq"), scatter_dimension=0, tiled=True),
        lax.psum_scatter(totals[2], ("dp", "seq"), scatter_dimension=0, tiled=True),
    )
    section_outputs = (
        lax.psum_scatter(
            finals.astype(jnp.float32).astype(jnp.bfloat16),
            "section",
            scatter_dimension=2,
            tiled=True,
        ).astype(jnp.float32),
        lax.psum_scatter(
            returned.astype(jnp.float32).astype(jnp.bfloat16),
            "section",
            scatter_dimension=2,
            tiled=True,
        ).astype(jnp.float32),
    )
    return (
        section_outputs[0].astype(jnp.bfloat16),
        section_outputs[1].astype(jnp.bfloat16),
        totals[0][None],
        totals[1][None],
        totals[2][None],
    )


def solution(mesh):
    placed = (
        P("dp", "seq", None),
        P("section", None, None),
        P("section", None, None),
        P("section", None),
        P("dp", None),
        P("dp", "seq", None),
    )
    return jax.shard_map(
        local,
        mesh=mesh,
        in_specs=placed,
        out_specs=(
            P("dp", "seq", "section"),
            P("dp", "seq", "section"),
            P("section", ("dp", "seq"), None),
            P("section", ("dp", "seq"), None),
            P("section", ("dp", "seq")),
        ),
        check_vma=False,
    )
```

profile of v0, /device:TPU:0, one launch (start us, length us, event | category | flops | bytes accessed | tf_op | source)
XLA Modules:
  0.0 2770.0 jit_solution(3333784698384214157)
XLA Ops:
  11.4 642.3 %while.152 = (s32[]{:T(128)}, bf16[512,1024]{1,0:T(8,128)(2,1)S(1)}, bf16[2,512,1024]{2,1,0:T(8,128)(2,1)}, bf16[2,512,1024]{2,1,0:T(8,128)(2,1)}, s32[]{:T(128)...) while((s32[]{:T(128)}, bf16[512,1024]{1,0:T(8,128)(2,1)S(1)}, ...), condition=%wide.region_25.26_spmd, body=%wide.region_0.25_spmd.sunk | while | flops 12025916416 | bytes 219922208 | solution.py:695
  15.6 27.9 %conditional.22 = (bf16[512,3072]{1,0:T(8,128)(2,1)}, bf16[273,1024]{0,1:T(8,128)(2,1)}, bf16[273,16]{0,1:T(8,128)(2,1)S(1)}, f32[]{:T(128)}, bf16[64,2048]{1,0:T(8,128)(2,1)S(1)}) conditional(s32[]{:T(128)} %get-tuple-element.2283, (bf16[512,1024]{1,0:T(8,128)(2,1)S(1)}, f32[1,1024]{1,0:T(1,128)}, ...), branch_computations={%region_1.5_spmd, %region_6.6_spmd, %region_7.8_spmd, %region_9.9_... | conditional | flops 3352751360 | bytes 87105472 | solution.py:626
  56.7 58.7 %conditional.23 = (bf16[512,1024]{1,0:T(8,128)(2,1)}, bf16[1,512,1024]{2,1,0:T(8,128)(2,1)S(1)}) conditional(s32[]{:T(128)} %get-tuple-element.2283, (bf16[512,1024]{1,0:T(8,128)(2,1)S(1)}, s32[]{:T(128)}, s32[4]{0:T(128)S(1)}, bf16[512,3072]{1,0:T(8,128)(2,1)}, f32[273,1024]{1,0:T(8,128)S(1)}, ...), branch_computations={%region_12.15_spmd, %region_16.17_spmd, %region_18.22_spmd, %regio... | conditional | flops 8670740480 | bytes 107399584
  86.0 12.3 fusion.34
  119.6 19.3 collective-permute-done.4
  143.2 27.9 %conditional.22 = (bf16[512,3072]{1,0:T(8,128)(2,1)}, bf16[273,1024]{0,1:T(8,128)(2,1)}, bf16[273,16]{0,1:T(8,128)(2,1)S(1)}, f32[]{:T(128)}, bf16[64,2048]{1,0:T(8,128)(2,1)S(1)}) conditional(s32[]{:T(128)} %get-tuple-element.2283, (bf16[512,1024]{1,0:T(8,128)(2,1)S(1)}, f32[1,1024]{1,0:T(1,128)}, ...), branch_computations={%region_1.5_spmd, %region_6.6_spmd, %region_7.8_spmd, %region_9.9_... | conditional | flops 3352751360 | bytes 87105472 | solution.py:626
  185.3 58.8 %conditional.23 = (bf16[512,1024]{1,0:T(8,128)(2,1)}, bf16[1,512,1024]{2,1,0:T(8,128)(2,1)S(1)}) conditional(s32[]{:T(128)} %get-tuple-element.2283, (bf16[512,1024]{1,0:T(8,128)(2,1)S(1)}, s32[]{:T(128)}, s32[4]{0:T(128)S(1)}, bf16[512,3072]{1,0:T(8,128)(2,1)}, f32[273,1024]{1,0:T(8,128)S(1)}, ...), branch_computations={%region_12.15_spmd, %region_16.17_spmd, %region_18.22_spmd, %regio... | conditional | flops 8670740480 | bytes 107399584
  214.5 12.2 fusion.34
  248.0 19.4 collective-permute-done.4
  271.7 27.9 %conditional.22 = (bf16[512,3072]{1,0:T(8,128)(2,1)}, bf16[273,1024]{0,1:T(8,128)(2,1)}, bf16[273,16]{0,1:T(8,128)(2,1)S(1)}, f32[]{:T(128)}, bf16[64,2048]{1,0:T(8,128)(2,1)S(1)}) conditional(s32[]{:T(128)} %get-tuple-element.2283, (bf16[512,1024]{1,0:T(8,128)(2,1)S(1)}, f32[1,1024]{1,0:T(1,128)}, ...), branch_computations={%region_1.5_spmd, %region_6.6_spmd, %region_7.8_spmd, %region_9.9_... | conditional | flops 3352751360 | bytes 87105472 | solution.py:626
  313.4 58.7 %conditional.23 = (bf16[512,1024]{1,0:T(8,128)(2,1)}, bf16[1,512,1024]{2,1,0:T(8,128)(2,1)S(1)}) conditional(s32[]{:T(128)} %get-tuple-element.2283, (bf16[512,1024]{1,0:T(8,128)(2,1)S(1)}, s32[]{:T(128)}, s32[4]{0:T(128)S(1)}, bf16[512,3072]{1,0:T(8,128)(2,1)}, f32[273,1024]{1,0:T(8,128)S(1)}, ...), branch_computations={%region_12.15_spmd, %region_16.17_spmd, %region_18.22_spmd, %regio... | conditional | flops 8670740480 | bytes 107399584
  342.7 12.3 fusion.34
  376.1 19.5 collective-permute-done.4
  399.9 27.9 %conditional.22 = (bf16[512,3072]{1,0:T(8,128)(2,1)}, bf16[273,1024]{0,1:T(8,128)(2,1)}, bf16[273,16]{0,1:T(8,128)(2,1)S(1)}, f32[]{:T(128)}, bf16[64,2048]{1,0:T(8,128)(2,1)S(1)}) conditional(s32[]{:T(128)} %get-tuple-element.2283, (bf16[512,1024]{1,0:T(8,128)(2,1)S(1)}, f32[1,1024]{1,0:T(1,128)}, ...), branch_computations={%region_1.5_spmd, %region_6.6_spmd, %region_7.8_spmd, %region_9.9_... | conditional | flops 3352751360 | bytes 87105472 | solution.py:626
  441.9 58.8 %conditional.23 = (bf16[512,1024]{1,0:T(8,128)(2,1)}, bf16[1,512,1024]{2,1,0:T(8,128)(2,1)S(1)}) conditional(s32[]{:T(128)} %get-tuple-element.2283, (bf16[512,1024]{1,0:T(8,128)(2,1)S(1)}, s32[]{:T(128)}, s32[4]{0:T(128)S(1)}, bf16[512,3072]{1,0:T(8,128)(2,1)}, f32[273,1024]{1,0:T(8,128)S(1)}, ...), branch_computations={%region_12.15_spmd, %region_16.17_spmd, %region_18.22_spmd, %regio... | conditional | flops 8670740480 | bytes 107399584
  471.1 12.2 fusion.34
  504.7 19.4 collective-permute-done.4
  528.3 27.9 %conditional.22 = (bf16[512,3072]{1,0:T(8,128)(2,1)}, bf16[273,1024]{0,1:T(8,128)(2,1)}, bf16[273,16]{0,1:T(8,128)(2,1)S(1)}, f32[]{:T(128)}, bf16[64,2048]{1,0:T(8,128)(2,1)S(1)}) conditional(s32[]{:T(128)} %get-tuple-element.2283, (bf16[512,1024]{1,0:T(8,128)(2,1)S(1)}, f32[1,1024]{1,0:T(1,128)}, ...), branch_computations={%region_1.5_spmd, %region_6.6_spmd, %region_7.8_spmd, %region_9.9_... | conditional | flops 3352751360 | bytes 87105472 | solution.py:626
  570.1 58.7 %conditional.23 = (bf16[512,1024]{1,0:T(8,128)(2,1)}, bf16[1,512,1024]{2,1,0:T(8,128)(2,1)S(1)}) conditional(s32[]{:T(128)} %get-tuple-element.2283, (bf16[512,1024]{1,0:T(8,128)(2,1)S(1)}, s32[]{:T(128)}, s32[4]{0:T(128)S(1)}, bf16[512,3072]{1,0:T(8,128)(2,1)}, f32[273,1024]{1,0:T(8,128)S(1)}, ...), branch_computations={%region_12.15_spmd, %region_16.17_spmd, %region_18.22_spmd, %regio... | conditional | flops 8670740480 | bytes 107399584
  599.4 12.3 fusion.34
  632.8 19.5 collective-permute-done.4
  656.4 1685.6 %while.155 = (s32[]{:T(128)}, bf16[512,1024]{1,0:T(8,128)(2,1)}, bf16[2,512,1024]{2,1,0:T(8,128)(2,1)}, f32[1024,5504]{1,0:T(8,128)}, f32[2752,1024]{1,0:T(8,128...) while((s32[]{:T(128)}, bf16[512,1024]{1,0:T(8,128)(2,1)}, ...), condition=%wide.region_71.72_spmd.clone, body=%wide.region_27.71_spmd.clone.sunk | while | flops 36067979264 | bytes 870966016 | solution.py:784
  665.2 28.5 %conditional.34 = (bf16[512,3072]{1,0:T(8,128)(2,1)}, bf16[273,1024]{0,1:T(8,128)(2,1)S(1)}, bf16[273,16]{0,1:T(8,128)(2,1)S(1)}, f32[]{:T(128)}, bf16[64,2048]{1,0:T(8,128)(2,1)S(1)}) conditional(s32[]{:T(128)} %get-tuple-element.2376, (bf16[512,1024]{1,0:T(8,128)(2,1)}, f32[1,1024]{1,0:T(1,128)}, ...), branch_computations={%region_28.32_spmd, %region_33.33_spmd, %region_34.35_spmd, %regio... | conditional | flops 3352751360 | bytes 85008320 | solution.py:626
  707.5 153.7 %conditional.35 = (bf16[273,1024]{0,1:T(8,128)(2,1)}, bf16[273,16]{0,1:T(8,128)(2,1)S(1)}, f32[]{:T(128)}, bf16[64,2048]{1,0:T(8,128)(2,1)S(1)}, f32[512,3072]{0,1:T(8,128)}, /*index=5*/f32[2752,1024]{1,0:T(8,128)}) conditional(s32[]{:T(128)} %get-tuple-element.2376, (bf16[2752,1024]{1,0:T(8,128)(2,1)}, ...), branch_computations={%region_39.43_spmd, %region_44.44_spmd, %region_45.50_spmd, %regio... | conditional | flops 9538059264 | bytes 378140544 | solution.py:716
  741.3 10.4 fusion.202
  753.4 11.4 fusion.227
  877.8 89.4 %conditional.36 = (f32[1024,5504]{1,0:T(8,128)}, f32[2752,1024]{1,0:T(8,128)}, f32[1024]{0:T(1024)S(1)}, bf16[512,1024]{1,0:T(8,128)(2,1)}, bf16[1,512,1024]{2,1,0:T(8,128)(2,1)S(1)}) conditional(s32[]{:T(128)} %get-tuple-element.2376, (bf16[512,1024]{1,0:T(8,128)(2,1)}, f32[1,1024]{1,0:T(1,128)S(1)}, ...), branch_computations={%region_54.58_spmd, %region_59.62_spmd, %region_63.66_spmd, %regio... | conditional | flops 23148920832 | bytes 167950464
  925.3 11.8 pad.27
  968.5 11.4 select_add_fusion.6
  996.6 28.5 %conditional.34 = (bf16[512,3072]{1,0:T(8,128)(2,1)}, bf16[273,1024]{0,1:T(8,128)(2,1)S(1)}, bf16[273,16]{0,1:T(8,128)(2,1)S(1)}, f32[]{:T(128)}, bf16[64,2048]{1,0:T(8,128)(2,1)S(1)}) conditional(s32[]{:T(128)} %get-tuple-element.2376, (bf16[512,1024]{1,0:T(8,128)(2,1)}, f32[1,1024]{1,0:T(1,128)}, ...), branch_computations={%region_28.32_spmd, %region_33.33_spmd, %region_34.35_spmd, %regio... | conditional | flops 3352751360 | bytes 85008320 | solution.py:626
  1036.6 153.5 %conditional.35 = (bf16[273,1024]{0,1:T(8,128)(2,1)}, bf16[273,16]{0,1:T(8,128)(2,1)S(1)}, f32[]{:T(128)}, bf16[64,2048]{1,0:T(8,128)(2,1)S(1)}, f32[512,3072]{0,1:T(8,128)}, /*index=5*/f32[2752,1024]{1,0:T(8,128)}) conditional(s32[]{:T(128)} %get-tuple-element.2376, (bf16[2752,1024]{1,0:T(8,128)(2,1)}, ...), branch_computations={%region_39.43_spmd, %region_44.44_spmd, %region_45.50_spmd, %regio... | conditional | flops 9538059264 | bytes 378140544 | solution.py:716
  1070.2 10.4 fusion.202
  1082.3 11.4 fusion.227
  1095.2 10.1 fusion.262
  1206.9 89.5 %conditional.36 = (f32[1024,5504]{1,0:T(8,128)}, f32[2752,1024]{1,0:T(8,128)}, f32[1024]{0:T(1024)S(1)}, bf16[512,1024]{1,0:T(8,128)(2,1)}, bf16[1,512,1024]{2,1,0:T(8,128)(2,1)S(1)}) conditional(s32[]{:T(128)} %get-tuple-element.2376, (bf16[512,1024]{1,0:T(8,128)(2,1)}, f32[1,1024]{1,0:T(1,128)S(1)}, ...), branch_computations={%region_54.58_spmd, %region_59.62_spmd, %region_63.66_spmd, %regio... | conditional | flops 23148920832 | bytes 167950464
  1254.5 11.8 pad.27
  1297.7 18.4 select_add_fusion.6
  1328.2 28.5 %conditional.34 = (bf16[512,3072]{1,0:T(8,128)(2,1)}, bf16[273,1024]{0,1:T(8,128)(2,1)S(1)}, bf16[273,16]{0,1:T(8,128)(2,1)S(1)}, f32[]{:T(128)}, bf16[64,2048]{1,0:T(8,128)(2,1)S(1)}) conditional(s32[]{:T(128)} %get-tuple-element.2376, (bf16[512,1024]{1,0:T(8,128)(2,1)}, f32[1,1024]{1,0:T(1,128)}, ...), branch_computations={%region_28.32_spmd, %region_33.33_spmd, %region_34.35_spmd, %regio... | conditional | flops 3352751360 | bytes 85008320 | solution.py:626
  1368.2 153.5 %conditional.35 = (bf16[273,1024]{0,1:T(8,128)(2,1)}, bf16[273,16]{0,1:T(8,128)(2,1)S(1)}, f32[]{:T(128)}, bf16[64,2048]{1,0:T(8,128)(2,1)S(1)}, f32[512,3072]{0,1:T(8,128)}, /*index=5*/f32[2752,1024]{1,0:T(8,128)}) conditional(s32[]{:T(128)} %get-tuple-element.2376, (bf16[2752,1024]{1,0:T(8,128)(2,1)}, ...), branch_computations={%region_39.43_spmd, %region_44.44_spmd, %region_45.50_spmd, %regio... | conditional | flops 9538059264 | bytes 378140544 | solution.py:716
  1401.8 10.4 fusion.202
  1413.9 11.4 fusion.227
  1426.8 10.1 fusion.262
  1538.4 89.5 %conditional.36 = (f32[1024,5504]{1,0:T(8,128)}, f32[2752,1024]{1,0:T(8,128)}, f32[1024]{0:T(1024)S(1)}, bf16[512,1024]{1,0:T(8,128)(2,1)}, bf16[1,512,1024]{2,1,0:T(8,128)(2,1)S(1)}) conditional(s32[]{:T(128)} %get-tuple-element.2376, (bf16[512,1024]{1,0:T(8,128)(2,1)}, f32[1,1024]{1,0:T(1,128)S(1)}, ...), branch_computations={%region_54.58_spmd, %region_59.62_spmd, %region_63.66_spmd, %regio... | conditional | flops 23148920832 | bytes 167950464
  1585.9 11.8 pad.27
  1629.2 18.4 select_add_fusion.6
  1659.7 28.5 %conditional.34 = (bf16[512,3072]{1,0:T(8,128)(2,1)}, bf16[273,1024]{0,1:T(8,128)(2,1)S(1)}, bf16[273,16]{0,1:T(8,128)(2,1)S(1)}, f32[]{:T(128)}, bf16[64,2048]{1,0:T(8,128)(2,1)S(1)}) conditional(s32[]{:T(128)} %get-tuple-element.2376, (bf16[512,1024]{1,0:T(8,128)(2,1)}, f32[1,1024]{1,0:T(1,128)}, ...), branch_computations={%region_28.32_spmd, %region_33.33_spmd, %region_34.35_spmd, %regio... | conditional | flops 3352751360 | bytes 85008320 | solution.py:626
  1699.7 153.5 %conditional.35 = (bf16[273,1024]{0,1:T(8,128)(2,1)}, bf16[273,16]{0,1:T(8,128)(2,1)S(1)}, f32[]{:T(128)}, bf16[64,2048]{1,0:T(8,128)(2,1)S(1)}, f32[512,3072]{0,1:T(8,128)}, /*index=5*/f32[2752,1024]{1,0:T(8,128)}) conditional(s32[]{:T(128)} %get-tuple-element.2376, (bf16[2752,1024]{1,0:T(8,128)(2,1)}, ...), branch_computations={%region_39.43_spmd, %region_44.44_spmd, %region_45.50_spmd, %regio... | conditional | flops 9538059264 | bytes 378140544 | solution.py:716
  1733.3 10.4 fusion.202
  1745.4 11.4 fusion.227
  1869.8 89.5 %conditional.36 = (f32[1024,5504]{1,0:T(8,128)}, f32[2752,1024]{1,0:T(8,128)}, f32[1024]{0:T(1024)S(1)}, bf16[512,1024]{1,0:T(8,128)(2,1)}, bf16[1,512,1024]{2,1,0:T(8,128)(2,1)S(1)}) conditional(s32[]{:T(128)} %get-tuple-element.2376, (bf16[512,1024]{1,0:T(8,128)(2,1)}, f32[1,1024]{1,0:T(1,128)S(1)}, ...), branch_computations={%region_54.58_spmd, %region_59.62_spmd, %region_63.66_spmd, %regio... | conditional | flops 23148920832 | bytes 167950464
  1917.4 11.8 pad.27
  1960.7 23.8 select_add_fusion.6
  2001.8 28.5 %conditional.34 = (bf16[512,3072]{1,0:T(8,128)(2,1)}, bf16[273,1024]{0,1:T(8,128)(2,1)S(1)}, bf16[273,16]{0,1:T(8,128)(2,1)S(1)}, f32[]{:T(128)}, bf16[64,2048]{1,0:T(8,128)(2,1)S(1)}) conditional(s32[]{:T(128)} %get-tuple-element.2376, (bf16[512,1024]{1,0:T(8,128)(2,1)}, f32[1,1024]{1,0:T(1,128)}, ...), branch_computations={%region_28.32_spmd, %region_33.33_spmd, %region_34.35_spmd, %regio... | conditional | flops 3352751360 | bytes 85008320 | solution.py:626
  2041.7 153.5 %conditional.35 = (bf16[273,1024]{0,1:T(8,128)(2,1)}, bf16[273,16]{0,1:T(8,128)(2,1)S(1)}, f32[]{:T(128)}, bf16[64,2048]{1,0:T(8,128)(2,1)S(1)}, f32[512,3072]{0,1:T(8,128)}, /*index=5*/f32[2752,1024]{1,0:T(8,128)}) conditional(s32[]{:T(128)} %get-tuple-element.2376, (bf16[2752,1024]{1,0:T(8,128)(2,1)}, ...), branch_computations={%region_39.43_spmd, %region_44.44_spmd, %region_45.50_spmd, %regio... | conditional | flops 9538059264 | bytes 378140544 | solution.py:716
  2075.4 10.4 fusion.202
  2087.5 11.4 fusion.227
  2211.9 89.5 %conditional.36 = (f32[1024,5504]{1,0:T(8,128)}, f32[2752,1024]{1,0:T(8,128)}, f32[1024]{0:T(1024)S(1)}, bf16[512,1024]{1,0:T(8,128)(2,1)}, bf16[1,512,1024]{2,1,0:T(8,128)(2,1)S(1)}) conditional(s32[]{:T(128)} %get-tuple-element.2376, (bf16[512,1024]{1,0:T(8,128)(2,1)}, f32[1,1024]{1,0:T(1,128)S(1)}, ...), branch_computations={%region_54.58_spmd, %region_59.62_spmd, %region_63.66_spmd, %regio... | conditional | flops 23148920832 | bytes 167950464
  2259.5 11.8 pad.27
  2302.7 23.8 select_add_fusion.6
  2345.7 14.9 all-reduce.13
  2361.2 19.2 reduce-scatter.5.cloned.1.call-done
  2380.4 38.8 %reduce-scatter.7.cloned.1.call-done = bf16[2,512,256]{2,1,0:T(8,128)(2,1)} async-done(((bf16[2,512,1024]{2,1,0:T(8,128)(2,1)}), bf16[2,512,256]{2,1,0:T(8,128)(2,1)}) %reduce-scatter.7.cloned.1.call-update) | async-done | bytes 524304 | tf_op jit(solution)/shard_map/reduce_scatter | solution.py:797
  2419.1 119.4 %reduce-scatter.11.cloned.1.call-done = f32[344,1024]{1,0:T(8,128)} async-done(((f32[2752,1024]{1,0:T(8,128)}), f32[344,1024]{1,0:T(8,128)}) %reduce-scatter.11.cloned.1.call-update) | async-done | bytes 1409040 | tf_op jit(solution)/shard_map/reduce_scatter | solution.py:787
  2538.6 223.8 %reduce-scatter.9.cloned.1.call-done = f32[128,5504]{1,0:T(8,128)} async-done(((f32[1024,5504]{1,0:T(8,128)}), f32[128,5504]{1,0:T(8,128)}) %reduce-scatter.9.cloned.1.call-update) | async-done | bytes 2818064 | tf_op jit(solution)/shard_map/reduce_scatter | solution.py:786
  (1415 shorter events, 1592.9 us)
Async XLA Ops:
  11.6 44.3 %all-gather.32.cloned.1.call-start = ((), (), s32[]{:S(2)}) async-start(), calls=%async_computation.8 | async-start | bytes 1720320 | tf_op jit(solution)/shard_map/while/body/eval_jaxpr/all_gather | solution.py:22
  15.6 32.9 %copy-start.54 = (u32[32]{0:T(128)S(1)}, u32[32]{0:T(128)}, u32[]{:S(2)}) copy-start(u32[32]{0:T(128)} %get-tuple-element.2292) | copy-start | bytes 388 | tf_op jit(solution)/shard_map/while
  46.0 8.2 collective-permute-start.3
  115.5 23.4 collective-permute-start.4
  139.1 44.5 %all-gather.32.cloned.1.call-start = ((), (), s32[]{:S(2)}) async-start(), calls=%async_computation.8 | async-start | bytes 1720320 | tf_op jit(solution)/shard_map/while/body/eval_jaxpr/all_gather | solution.py:22
  143.2 34.3 %copy-start.54 = (u32[32]{0:T(128)S(1)}, u32[32]{0:T(128)}, u32[]{:S(2)}) copy-start(u32[32]{0:T(128)} %get-tuple-element.2292) | copy-start | bytes 388 | tf_op jit(solution)/shard_map/while
  173.6 10.0 collective-permute-start.3
  244.1 23.4 collective-permute-start.4
  267.6 44.5 %all-gather.32.cloned.1.call-start = ((), (), s32[]{:S(2)}) async-start(), calls=%async_computation.8 | async-start | bytes 1720320 | tf_op jit(solution)/shard_map/while/body/eval_jaxpr/all_gather | solution.py:22
  271.7 34.3 %copy-start.54 = (u32[32]{0:T(128)S(1)}, u32[32]{0:T(128)}, u32[]{:S(2)}) copy-start(u32[32]{0:T(128)} %get-tuple-element.2292) | copy-start | bytes 388 | tf_op jit(solution)/shard_map/while
  302.1 9.7 collective-permute-start.3
  372.2 23.4 collective-permute-start.4
  395.8 44.5 %all-gather.32.cloned.1.call-start = ((), (), s32[]{:S(2)}) async-start(), calls=%async_computation.8 | async-start | bytes 1720320 | tf_op jit(solution)/shard_map/while/body/eval_jaxpr/all_gather | solution.py:22
  399.9 34.2 %copy-start.54 = (u32[32]{0:T(128)S(1)}, u32[32]{0:T(128)}, u32[]{:S(2)}) copy-start(u32[32]{0:T(128)} %get-tuple-element.2292) | copy-start | bytes 388 | tf_op jit(solution)/shard_map/while
  430.3 10.0 collective-permute-start.3
  500.7 23.4 collective-permute-start.4
  524.3 44.5 %all-gather.32.cloned.1.call-start = ((), (), s32[]{:S(2)}) async-start(), calls=%async_computation.8 | async-start | bytes 1720320 | tf_op jit(solution)/shard_map/while/body/eval_jaxpr/all_gather | solution.py:22
  528.3 34.3 %copy-start.54 = (u32[32]{0:T(128)S(1)}, u32[32]{0:T(128)}, u32[]{:S(2)}) copy-start(u32[32]{0:T(128)} %get-tuple-element.2292) | copy-start | bytes 388 | tf_op jit(solution)/shard_map/while
  558.8 9.7 collective-permute-start.3
  628.8 23.4 collective-permute-start.4
  662.2 44.3 %all-gather.34.cloned.1.call-start = ((), (), s32[]{:S(2)}) async-start(), calls=%async_computation.9 | async-start | bytes 1720320 | tf_op jit(solution)/shard_map/while/body/eval_jaxpr/all_gather | solution.py:22
  665.2 29.9 %copy-start.55 = (u32[32]{0:T(128)S(1)}, u32[32]{0:T(128)}, u32[]{:S(2)}) copy-start(u32[32]{0:T(128)} %get-tuple-element.2386) | copy-start | bytes 388 | tf_op jit(solution)/shard_map/while
  694.8 180.0 %all-gather.36.cloned.1.call-start = ((), (), s32[]{:S(2)}) async-start(), calls=%async_computation.10 | async-start | bytes 1720320 | tf_op jit(solution)/shard_map/while/body/eval_jaxpr/all_gather | solution.py:22
  696.8 9.7 collective-permute-start
  863.5 9.0 collective-permute-start.1
  967.2 25.2 collective-permute-start.2
  993.6 42.1 %all-gather.34.cloned.1.call-start = ((), (), s32[]{:S(2)}) async-start(), calls=%async_computation.9 | async-start | bytes 1720320 | tf_op jit(solution)/shard_map/while/body/eval_jaxpr/all_gather | solution.py:22
  996.6 29.9 %copy-start.55 = (u32[32]{0:T(128)S(1)}, u32[32]{0:T(128)}, u32[]{:S(2)}) copy-start(u32[32]{0:T(128)} %get-tuple-element.2386) | copy-start | bytes 388 | tf_op jit(solution)/shard_map/while
  1026.2 177.7 %all-gather.36.cloned.1.call-start = ((), (), s32[]{:S(2)}) async-start(), calls=%async_computation.10 | async-start | bytes 1720320 | tf_op jit(solution)/shard_map/while/body/eval_jaxpr/all_gather | solution.py:22
  1028.4 7.3 collective-permute-start
  1192.5 9.0 collective-permute-start.1
  1296.4 25.2 collective-permute-start.2
  1325.2 42.1 %all-gather.34.cloned.1.call-start = ((), (), s32[]{:S(2)}) async-start(), calls=%async_computation.9 | async-start | bytes 1720320 | tf_op jit(solution)/shard_map/while/body/eval_jaxpr/all_gather | solution.py:22
  1328.2 29.9 %copy-start.55 = (u32[32]{0:T(128)S(1)}, u32[32]{0:T(128)}, u32[]{:S(2)}) copy-start(u32[32]{0:T(128)} %get-tuple-element.2386) | copy-start | bytes 388 | tf_op jit(solution)/shard_map/while
  1357.8 177.6 %all-gather.36.cloned.1.call-start = ((), (), s32[]{:S(2)}) async-start(), calls=%async_computation.10 | async-start | bytes 1720320 | tf_op jit(solution)/shard_map/while/body/eval_jaxpr/all_gather | solution.py:22
  1360.0 7.3 collective-permute-start
  1524.1 9.0 collective-permute-start.1
  1627.8 25.2 collective-permute-start.2
  1656.7 42.1 %all-gather.34.cloned.1.call-start = ((), (), s32[]{:S(2)}) async-start(), calls=%async_computation.9 | async-start | bytes 1720320 | tf_op jit(solution)/shard_map/while/body/eval_jaxpr/all_gather | solution.py:22
  1659.7 29.9 %copy-start.55 = (u32[32]{0:T(128)S(1)}, u32[32]{0:T(128)}, u32[]{:S(2)}) copy-start(u32[32]{0:T(128)} %get-tuple-element.2386) | copy-start | bytes 388 | tf_op jit(solution)/shard_map/while
  1689.3 177.6 %all-gather.36.cloned.1.call-start = ((), (), s32[]{:S(2)}) async-start(), calls=%async_computation.10 | async-start | bytes 1720320 | tf_op jit(solution)/shard_map/while/body/eval_jaxpr/all_gather | solution.py:22
  1691.5 7.3 collective-permute-start
  1855.5 9.0 collective-permute-start.1
  1959.3 34.5 %collective-permute-start.2 = (bf16[512,1024]{1,0:T(8,128)(2,1)}, bf16[512,1024]{1,0:T(8,128)(2,1)S(1)}, u32[]{:S(2)}, u32[]{:S(2)}) collective-permute-start(bf16[512,1024]{1,0:T(8,128)(2,1)} %get-tuple-element.2002), channel_id=1, source_target_pairs={{8,0},{16,8},{24,16},{9,1},{17,9},{25,17},{10,2},{18,10},{26,18},{... | collective-permute-start | bytes 3145736 | tf_op jit(solution)/shard_map/while/body/eval_jaxpr/ppermute | solution.py:53
  1960.6 24.4 slice-start.2
  1960.6 23.9 copy-start.47
  1960.6 23.9 copy-start.20
  1960.6 25.1 slice-start.3
  1960.7 26.7 slice-start.4
  1998.7 42.1 %all-gather.34.cloned.1.call-start = ((), (), s32[]{:S(2)}) async-start(), calls=%async_computation.9 | async-start | bytes 1720320 | tf_op jit(solution)/shard_map/while/body/eval_jaxpr/all_gather | solution.py:22
  2001.7 29.9 %copy-start.55 = (u32[32]{0:T(128)S(1)}, u32[32]{0:T(128)}, u32[]{:S(2)}) copy-start(u32[32]{0:T(128)} %get-tuple-element.2386) | copy-start | bytes 388 | tf_op jit(solution)/shard_map/while
  2031.3 177.6 %all-gather.36.cloned.1.call-start = ((), (), s32[]{:S(2)}) async-start(), calls=%async_computation.10 | async-start | bytes 1720320 | tf_op jit(solution)/shard_map/while/body/eval_jaxpr/all_gather | solution.py:22
  2033.5 7.3 collective-permute-start
  2197.6 9.0 collective-permute-start.1
  2301.4 34.5 %collective-permute-start.2 = (bf16[512,1024]{1,0:T(8,128)(2,1)}, bf16[512,1024]{1,0:T(8,128)(2,1)S(1)}, u32[]{:S(2)}, u32[]{:S(2)}) collective-permute-start(bf16[512,1024]{1,0:T(8,128)(2,1)} %get-tuple-element.2002), channel_id=1, source_target_pairs={{8,0},{16,8},{24,16},{9,1},{17,9},{25,17},{10,2},{18,10},{26,18},{... | collective-permute-start | bytes 3145736 | tf_op jit(solution)/shard_map/while/body/eval_jaxpr/ppermute | solution.py:53
  2302.7 24.4 slice-start.2
  2302.7 23.9 copy-start.47
  2302.7 23.9 copy-start.20
  2302.7 25.1 slice-start.3
  2302.7 26.7 slice-start.4
  2342.0 38.4 %reduce-scatter.5.cloned.1.call-start = ((), (), s32[]{:S(2)}) async-start(), calls=%async_computation.4 | async-start | bytes 2621440 | tf_op jit(solution)/shard_map/reduce_scatter | solution.py:791
  2342.5 76.6 %reduce-scatter.7.cloned.1.call-start = ((), (), s32[]{:S(2)}) async-start(), calls=%async_computation.5 | async-start | bytes 2621440 | tf_op jit(solution)/shard_map/reduce_scatter | solution.py:797
  2343.1 195.4 %reduce-scatter.11.cloned.1.call-start = ((), (), s32[]{:S(2)}) async-start(), calls=%async_computation.7 | async-start | bytes 12681216 | tf_op jit(solution)/shard_map/reduce_scatter | solution.py:787
  2343.7 418.6 %reduce-scatter.9.cloned.1.call-start = ((), (), s32[]{:S(2)}) async-start(), calls=%async_computation.6 | async-start | bytes 25362432 | tf_op jit(solution)/shard_map/reduce_scatter | solution.py:786
  (232 other events, 1792.3 us)
Sparse Core Ops, SparseCore 0:
  45.9 9.9 all-gather.31
  173.5 10.0 all-gather.31
  301.9 10.0 all-gather.31
  430.2 10.0 all-gather.31
  558.6 10.0 all-gather.31
  695.0 10.0 all-gather.33
  863.6 11.1 all-gather.35
  1026.3 8.6 all-gather.33
  1192.6 11.2 all-gather.35
  1357.9 8.5 all-gather.33
  1524.2 11.1 all-gather.35
  1689.4 8.5 all-gather.33
  1855.6 11.1 all-gather.35
  2031.5 8.5 all-gather.33
  2197.7 11.1 all-gather.35
Sparse Core Ops, SparseCore 1:
  2346.0 34.4 reduce-scatter.4
  2384.1 35.0 reduce-scatter.6
  2421.9 116.6 reduce-scatter.10
  2541.5 220.7 reduce-scatter.8
where the time goes:
time: 2780 us; the launch traced here: 2770 us
  matrix products  872 us (31%)
  waiting for transfers between devices  525 us (19%)
  other arithmetic  467 us (17%)
  local copies, waits for them, and re-layouts  433 us (16%)
  loops' own time  316 us (11%)
  blocking collectives  94 us (3%)
  starting transfers between devices  47.2 us (2%)
    reduce_scatter x1, waiting for transfers between devices, local(): lax.psum_scatter(totals[0], ('dp', 'seq'), scatter_dimension=0, tiled=True)  224 us
    unnamed x10, loops' own time  170 us
    another operation x140, local copies, waits for them, and re-layouts  132 us
    add x15, other arithmetic, backward_turn(): totals = jax.tree.map(jnp.add, totals, increments)  120 us
    reduce_scatter x1, waiting for transfers between devices, local(): lax.psum_scatter(totals[1], ('dp', 'seq'), scatter_dimension=0, tiled=True)  119 us
    dot_general x10, matrix products, taylor_rest(): jnp.einsum('thf,fhc->thc', query_feat, in_vals, precision=highest)  118 us
    another operation x5, loops' own time, backward_turn(): lax.switch(section_index, [lambda: taylor_mid(section_entry, upstream, ga...  115 us
    ppermute x25, waiting for transfers between devices, passed_along(): return lax.ppermute(value, axis, pairs)  107 us
  transfers between devices with their start and end apart: 44, of which 20 were waited for; matrix products, arithmetic and copies ran while one was open for 6% of the time, Pallas kernels for 0%

commit v1 on v0

v1 whole, which is shorter than its diff:
```python
import functools

import jax
import jax.numpy as jnp
from jax import lax
from jax.experimental import pallas as pl
from jax.experimental.pallas import tpu as pltpu
from jax.sharding import PartitionSpec as P

HEADS = 16
FEAT_DIM = 16
WINDOW = 64
CHUNKS = 4
LAG = 1
PAIRS = HEADS // 2
epsilon = 1e-06

F32 = jnp.float32
BF16 = jnp.bfloat16


def nn(a, b):
    return jnp.dot(a, b, preferred_element_type=F32)


def nt(a, b):
    return lax.dot_general(a, b, (((1,), (1,)), ((), ())), preferred_element_type=F32)


def tn(a, b):
    return lax.dot_general(a, b, (((0,), (0,)), ((), ())), preferred_element_type=F32)


def lanes(rows, width):
    return lax.broadcasted_iota(jnp.int32, (rows, width), 1)


def call(kernel, grid, in_specs, out_specs, out_shape, scratch, flops):
    return pl.pallas_call(
        kernel,
        grid=grid,
        in_specs=in_specs,
        out_specs=out_specs,
        out_shape=out_shape,
        scratch_shapes=scratch,
        compiler_params=pltpu.CompilerParams(
            vmem_limit_bytes=40 * 1024 * 1024, dimension_semantics=("arbitrary",)
        ),
        cost_estimate=pl.CostEstimate(flops=flops, bytes_accessed=flops // 512, transcendentals=0),
    )


def whole(shape):
    return pl.BlockSpec(shape, lambda p: (0,) * len(shape))


def columns(rows, start=0, row=0):
    return pl.BlockSpec((rows, 128), lambda p: (row, start + p))


def taylor_mask(doc_t, doc_s, j, m, t_axis):
    same = doc_t == doc_s
    if j == m:
        t = lax.broadcasted_iota(jnp.int32, same.shape, t_axis)
        s = lax.broadcasted_iota(jnp.int32, same.shape, 1 - t_axis)
        same = same & (s <= t)
    return jnp.where(same, 1.0, 0.0).astype(F32)


def taylor_forward_kernel(m, size, *refs):
    docc, docr, q_ref = refs[:3]
    ks, vs = refs[3 : 4 + m], refs[4 + m : 5 + 2 * m]
    mix_ref, den_ref, mask = refs[5 + 2 * m :]
    pair = pl.program_id(0)

    @pl.when(pair == 0)
    def _():
        for j in range(m + 1):
            mask[j] = taylor_mask(
                docc[m * size : (m + 1) * size, :], docr[:, j * size : (j + 1) * size], j, m, 0
            )
        den_ref[...] = jnp.zeros_like(den_ref)

    q = q_ref[...]
    wide = lanes(size, 2 * 128) // FEAT_DIM
    lane = lanes(size, 128)
    ratios = []
    dens = den_ref[...]
    for i in range(2):
        head = 2 * pair + i
        q_head = jnp.where(wide == head, q * jnp.asarray(0.25, BF16), jnp.zeros_like(q))
        numer = jnp.zeros((size, 128), F32)
        denom = jnp.zeros((size, 1), F32)
        for j in range(m + 1):
            a = nt(q_head, ks[j][...])
            w = (1.0 + a * (1.0 + 0.5 * a)) * mask[j]
            denom += jnp.sum(w, axis=1, keepdims=True)
            numer += nn(w.astype(BF16), vs[j][...])
        ratios.append(numer / denom)
        dens = jnp.where(lane == head, denom, dens)
    den_ref[...] = dens
    mix_ref[...] = jnp.where(lane < 64, ratios[0], ratios[1]).astype(BF16)


def taylor_forward(m, docs, kept):
    size = kept[0].shape[0]
    docc, docr = docs
    return call(
        functools.partial(taylor_forward_kernel, m, size),
        (PAIRS,),
        [whole(docc.shape), whole(docr.shape), whole((size, 256))]
        + [pl.BlockSpec((size, 256), lambda p: (0, 1))] * (m + 1)
        + [columns(size, 4)] * (m + 1),
        [columns(size), whole((size, 128))],
        [
            jax.ShapeDtypeStruct((size, HEADS * 64), BF16),
            jax.ShapeDtypeStruct((size, 128), F32),
        ],
        [pltpu.VMEM((m + 1, size, size), F32)],
        2 * HEADS * (m + 1) * size * size * 512,
    )(docc, docr, kept[m], *kept, *kept)


def taylor_backward_kernel(m, size, later, *refs):
    docc, docr, q_ref = refs[:3]
    refs = refs[3:]
    ks, vs = refs[: m + 1], refs[m + 1 : 2 * m + 2]
    dmix_ref, mix_ref, den_ref = refs[2 * m + 2 : 2 * m + 5]
    refs = refs[2 * m + 5 :]
    if later:
        dk_in, dv_in = refs[:2]
        refs = refs[2:]
    dq_ref, dk_ref, dv_ref, mask, k_turned, dq_turned = refs
    pair = pl.program_id(0)

    @pl.when(pair == 0)
    def _():
        for j in range(m + 1):
            mask[j] = taylor_mask(
                docr[:, m * size : (m + 1) * size], docc[j * size : (j + 1) * size, :], j, m, 1
            )
            k_turned[j] = (ks[j][...].astype(F32) * 0.25).T.astype(BF16)
        dk_ref[...] = dk_in[...] if later else jnp.zeros_like(dk_ref)

    q = q_ref[...]
    wide = lanes(size, 2 * 128) // FEAT_DIM
    lane = lanes(size, 128)
    dm = dmix_ref[...].astype(F32)
    both = dm * mix_ref[...].astype(F32)
    den = den_ref[...]
    for i in range(2):
        head = 2 * pair + i
        inside = lane // 64 == i
        spare = 64 * (1 - i)
        turn = 1.0 / jnp.sum(jnp.where(lane == head, den, 0.0), axis=1, keepdims=True)
        dden = -jnp.sum(jnp.where(inside, both, 0.0), axis=1, keepdims=True) * turn
        dden_high = dden.astype(BF16).astype(F32)
        dnum = jnp.where(inside, dm * turn, 0.0)
        dnum_low = dnum.astype(BF16)
        dnum_more = jnp.where(
            lane == spare, dden_high, jnp.where(lane == spare + 1, dden - dden_high, dnum)
        ).astype(BF16)
        q_head = jnp.where(wide == head, q * jnp.asarray(0.25, BF16), jnp.zeros_like(q))
        own = pl.ds(pl.multiple_of(head * FEAT_DIM, FEAT_DIM), FEAT_DIM)
        dq_head = jnp.zeros((FEAT_DIM, size), F32)
        for j in range(m + 1):
            rows = pl.ds(j * size, size)
            v = vs[j][...]
            v_more = jnp.where(
                inside,
                v,
                jnp.where((lane == spare) | (lane == spare + 1), jnp.ones_like(v), jnp.zeros_like(v)),
            )
            a = nt(ks[j][...], q_head)
            w = (1.0 + a * (1.0 + 0.5 * a)) * mask[j]
            dw = nt(v_more, dnum_more)
            da = (dw * (1.0 + a) * mask[j]).astype(BF16)
            dv = nn(w.astype(BF16), dnum_low)
            if i == 0:
                dv_ref[rows, :] = dv_in[rows, :] + dv if later else dv
            else:
                dv_ref[rows, :] += dv
            dk_ref[rows, :] += nn(da, q_head)
            dq_head += nn(k_turned[j, own, :], da)
        dq_turned[own, :] = dq_head

    @pl.when(pair == PAIRS - 1)
    def _():
        dq_ref[...] = dq_turned[...].T


def taylor_backward(m, docs, kept, dmix, mix_at, den, later):
    size = kept[0].shape[0]
    docc, docr = docs
    rows = (m + 1) * size
    return call(
        functools.partial(taylor_backward_kernel, m, size, later is not None),
        (PAIRS,),
        [whole(docc.shape), whole(docr.shape), whole((size, 256))]
        + [pl.BlockSpec((size, 256), lambda p: (0, 1))] * (m + 1)
        + [columns(size, 4)] * (m + 1)
        + [columns(size), columns(size, mix_at), whole((size, 128))]
        + ([whole((rows, 256)), columns(rows)] if later is not None else []),
        [whole((size, 256)), whole((rows, 256)), columns(rows)],
        [
            jax.ShapeDtypeStruct((size, 256), F32),
            jax.ShapeDtypeStruct((rows, 256), F32),
            jax.ShapeDtypeStruct((rows, HEADS * 64), F32),
        ],
        [
            pltpu.VMEM((m + 1, size, size), F32),
            pltpu.VMEM((m + 1, 256, size), BF16),
            pltpu.VMEM((256, size), F32),
        ],
        5 * HEADS * (m + 1) * size * size * 512,
    )(docc, docr, kept[m], *kept, *kept, dmix, kept[m], den, *(later or ()))


STEP = 128


def window_spans(m, size):
    lead = STEP if m > 0 else 0
    for b in range(size // STEP):
        first = max(b * STEP + lead - STEP, 0)
        yield b * STEP, first, b * STEP + lead + STEP - first, lead


def window_mask(doc_t, doc_s, lead_rows, t_axis):
    t = lax.broadcasted_iota(jnp.int32, (doc_t == doc_s).shape, t_axis)
    s = lax.broadcasted_iota(jnp.int32, (doc_t == doc_s).shape, 1 - t_axis)
    distance = t + lead_rows - s
    return (distance >= 0) & (distance < WINDOW) & (doc_t == doc_s)


def joined(before, own):
    return jnp.concatenate([before[...], own[...]], axis=0) if before is not None else own[...]


def window_forward_kernel(m, size, *refs):
    docc, docr, q_ref, k_ref, v_ref = refs[:5]
    before_k, before_v = refs[5:7] if m > 0 else (None, None)
    mix_ref = refs[-1]
    k_all, v_all = joined(before_k, k_ref), joined(before_v, v_ref)
    lane = lanes(STEP, 128)
    for row, first, count, lead in window_spans(m, size):
        at = m * size - lead + first
        q = q_ref[row : row + STEP, :]
        k, v = k_all[first : first + count], v_all[first : first + count]
        mask = window_mask(
            docc[m * size + row : m * size + row + STEP, :],
            docr[:, at : at + count],
            row + lead - first,
            0,
        )
        mixes = []
        for i in range(2):
            q_head = jnp.where(lane // 64 == i, q * jnp.asarray(0.125, BF16), jnp.zeros_like(q))
            a = jnp.where(mask, nt(q_head, k), -1e30)
            p = jnp.exp(a - jnp.max(a, axis=1, keepdims=True))
            p = p * (1.0 / jnp.sum(p, axis=1, keepdims=True))
            mixes.append(nn(p.astype(BF16), v))
        mix_ref[row : row + STEP, :] = jnp.where(lane < 64, mixes[0], mixes[1]).astype(BF16)


def window_sources(m, size, kept, kept_before):
    last = size // STEP - 1
    specs = [columns(size), columns(size, 8), columns(size, 16)]
    arrays = [kept] * 3
    if m > 0:
        specs += [columns(STEP, 8, last), columns(STEP, 16, last)]
        arrays += [kept_before] * 2
    return specs, arrays


def window_forward(m, docs, kept, kept_before):
    size = kept.shape[0]
    docc, docr = docs
    specs, arrays = window_sources(m, size, kept, kept_before)
    return call(
        functools.partial(window_forward_kernel, m, size),
        (PAIRS,),
        [whole(docc.shape), whole(docr.shape)] + specs,
        columns(size),
        jax.ShapeDtypeStruct((size, HEADS * 64), BF16),
        [],
        2 * HEADS * size * 256 * 512,
    )(docc, docr, *arrays)


def window_backward_kernel(m, size, later, *refs):
    docc, docr, q_ref, k_ref, v_ref = refs[:5]
    refs = refs[5:]
    before_k, before_v = None, None
    if m > 0:
        before_k, before_v = refs[:2]
        refs = refs[2:]
    dmix_ref = refs[0]
    refs = refs[1:]
    if later:
        dk_in, dv_in = refs[:2]
        refs = refs[2:]
    dq_ref, dk_ref, dv_ref = refs[:3]
    refs = refs[3:]
    if m > 0:
        dk_out, dv_out = refs[:2]
        refs = refs[2:]
    dk_sum, dv_sum = refs
    lead = STEP if m > 0 else 0
    rows = size + lead
    dk_sum[...] = jnp.zeros_like(dk_sum)
    dv_sum[...] = jnp.zeros_like(dv_sum)
    if later:
        dk_sum[rows - STEP : rows, :] = dk_in[...]
        dv_sum[rows - STEP : rows, :] = dv_in[...]
    k_all, v_all = joined(before_k, k_ref), joined(before_v, v_ref)
    lane = lanes(STEP, 128)
    for row, first, count, _ in window_spans(m, size):
        at = m * size - lead + first
        q, dm = q_ref[row : row + STEP, :], dmix_ref[row : row + STEP, :]
        k, v = k_all[first : first + count], v_all[first : first + count]
        mask = window_mask(
            docr[:, m * size + row : m * size + row + STEP],
            docc[at : at + count, :],
            row + lead - first,
            1,
        )
        dq = jnp.zeros((STEP, 128), F32)
        dk = jnp.zeros((count, 128), F32)
        dv = jnp.zeros((count, 128), F32)
        for i in range(2):
            inside = lane // 64 == i
            q_head = jnp.where(inside, q * jnp.asarray(0.125, BF16), jnp.zeros_like(q))
            dm_head = jnp.where(inside, dm, jnp.zeros_like(dm))
            k_head = jnp.where(
                lanes(count, 128) // 64 == i, k * jnp.asarray(0.125, BF16), jnp.zeros_like(k)
            )
            a = jnp.where(mask, nt(k, q_head), -1e30)
            p = jnp.exp(a - jnp.max(a, axis=0, keepdims=True))
            p = p * (1.0 / jnp.sum(p, axis=0, keepdims=True))
            dp = nt(v, dm_head)
            da = (p * (dp - jnp.sum(p * dp, axis=0, keepdims=True))).astype(BF16)
            dk += nn(da, q_head)
            dv += nn(p.astype(BF16), dm_head)
            dq += tn(da, k_head)
        dq_ref[row : row + STEP, :] = dq.astype(BF16)
        dk_sum[first : first + count, :] += dk
        dv_sum[first : first + count, :] += dv
    dk_ref[...] = dk_sum[lead:rows, :].astype(BF16)
    dv_ref[...] = dv_sum[lead:rows, :].astype(BF16)
    if m > 0:
        dk_out[...] = dk_sum[:STEP, :]
        dv_out[...] = dv_sum[:STEP, :]


def window_backward(m, docs, kept, kept_before, dmix, later):
    size = kept.shape[0]
    docc, docr = docs
    specs, arrays = window_sources(m, size, kept, kept_before)
    rows = size + (STEP if m > 0 else 0)
    low = jax.ShapeDtypeStruct((size, HEADS * 64), BF16)
    edge = jax.ShapeDtypeStruct((STEP, HEADS * 64), F32)
    return call(
        functools.partial(window_backward_kernel, m, size, later is not None),
        (PAIRS,),
        [whole(docc.shape), whole(docr.shape)]
        + specs
        + [columns(size)]
        + ([columns(STEP)] * 2 if later is not None else []),
        [columns(size)] * 3 + ([columns(STEP)] * 2 if m > 0 else []),
        [low] * 3 + ([edge] * 2 if m > 0 else []),
        [pltpu.VMEM((rows, 128), F32), pltpu.VMEM((rows, 128), F32)],
        5 * HEADS * size * 256 * 512,
    )(docc, docr, *arrays, dmix, *(later or ()))


def rms_forward(inputs, gain_row):
    inverse = lax.rsqrt(jnp.mean(inputs * inputs, axis=-1, keepdims=True) + epsilon)
    return ((inputs * inverse * gain_row).astype(BF16), inverse)


def rms_backward(entry, gain_row, upstream, grad_normed):
    inputs = entry.astype(F32)
    inverse = lax.rsqrt(jnp.mean(inputs * inputs, axis=-1, keepdims=True) + epsilon)
    scaled = grad_normed * gain_row
    grad_inputs = inverse * scaled - inputs * inverse**3 * jnp.mean(
        scaled * inputs, axis=-1, keepdims=True
    )
    grad_gain = jnp.sum(grad_normed * inputs * inverse, axis=0)
    return ((upstream.astype(F32) + grad_inputs).astype(BF16), grad_gain)


def local(tokens, section_in, section_out, gains, bounds, cotangent):
    section = lax.axis_index("section")
    seq = lax.axis_index("seq")
    sections = lax.axis_size("section")
    pack_in = section_in[0]
    pack_out = section_out[0]
    gain_row = gains[0]
    _, block, width = tokens.shape
    hidden_dim = pack_out.shape[0]
    both = 2 * hidden_dim
    length = 2 * block
    size = length // CHUNKS
    last = sections - 1
    taylor_cols = 2 * HEADS * FEAT_DIM + width
    window_cols = 3 * width

    def swapped(two):
        away = lax.dynamic_index_in_dim(two, 1 - seq, 0, keepdims=False)
        own = lax.dynamic_index_in_dim(two, seq, 0, keepdims=False)
        came = lax.ppermute(away, "seq", [(0, 1), (1, 0)])
        return jnp.where(seq == 0, jnp.stack([own, came]), jnp.stack([came, own]))

    starts = lax.dynamic_index_in_dim(bounds, seq, 0, keepdims=False)
    positions = jnp.arange(length, dtype=jnp.int32)
    docs = jnp.sum((starts[None, :] <= positions[:, None]).astype(jnp.int32), axis=1)
    docs = (docs[:, None], docs[None, :])

    feed = swapped(jnp.where(section == 0, tokens, cotangent)).reshape(CHUNKS, size, width)

    turns = CHUNKS + LAG * last
    entries, kepts, denoms, finals = [], [], [], [None] * CHUNKS

    def forward_branch(s, t, entry):
        m = t - LAG * s
        if m < 0 or m >= CHUNKS:
            return lambda: (
                jnp.zeros((size, width), BF16),
                jnp.zeros((size, both), BF16),
                jnp.zeros((size, 128), F32),
            )

        def padded(parts):
            used = sum(part.shape[1] for part in parts)
            return jnp.concatenate(list(parts) + [jnp.zeros((size, both - used), BF16)], axis=1)

        def taylor():
            inputs = entry.astype(F32)
            normed, _ = rms_forward(inputs, gain_row)
            projected = nn(normed, pack_in[:, :taylor_cols]).astype(BF16)
            mix, den = taylor_forward(m, docs, kepts[t - m :] + [projected])
            output = inputs + nn(mix, pack_out[:width])
            return output.astype(BF16), padded([projected, mix]), den

        def window():
            inputs = entry.astype(F32)
            normed, _ = rms_forward(inputs, gain_row)
            projected = nn(normed, pack_in[:, :window_cols]).astype(BF16)
            mix = window_forward(m, docs, projected, kepts[t - 1] if m > 0 else None)
            output = inputs + nn(mix, pack_out[:width])
            return output.astype(BF16), padded([projected, mix]), jnp.zeros((size, 128), F32)

        def dense():
            inputs = entry.astype(F32)
            normed, _ = rms_forward(inputs, gain_row)
            gate_up = nn(normed, pack_in)
            gate, up = gate_up[:, :hidden_dim], gate_up[:, hidden_dim:]
            hidden = (gate * jax.nn.sigmoid(gate) * up).astype(BF16)
            output = inputs + nn(hidden, pack_out)
            return output.astype(BF16), gate_up.astype(BF16), jnp.zeros((size, 128), F32)

        return (taylor, dense, window, dense)[s]

    sent = []
    for t in range(turns):
        entry = feed[min(t, CHUNKS - 1)]
        if t >= LAG:
            arrived = sent[t - LAG]
            entry = jnp.where(section == 0, entry, arrived) if t < CHUNKS else arrived
        output, kept, den = lax.switch(
            section, [forward_branch(s, t, entry) for s in range(sections)]
        )
        entries.append(entry)
        kepts.append(kept)
        denoms.append(den)
        if 0 <= t - LAG * last < CHUNKS:
            finals[t - LAG * last] = output
        if t < turns - LAG:
            sent.append(lax.ppermute(output, "section", [(i, i + 1) for i in range(last)]))

    grads_low, hiddens, upstreams = [], [], []
    gain_total = jnp.zeros((width,), F32)
    returned = [None] * CHUNKS
    taylor_later = [None] * (turns + 1)
    window_later = [None] * (turns + 1)

    def backward_branch(s, t, upstream):
        f = turns - 1 - t
        m = CHUNKS - 1 - (t - LAG * (last - s))
        taylor_m = CHUNKS - 1 - (t - LAG * last)
        window_m = CHUNKS - 1 - (t - LAG * (last - 2))
        entry, kept = entries[f], kepts[f]

        def carry_zeros():
            t_rows = max(taylor_m, 0) * size if taylor_m < CHUNKS else 0
            w_rows = STEP if 0 < window_m < CHUNKS else 0
            return (
                [jnp.zeros((t_rows, 256), F32), jnp.zeros((t_rows, width), F32)] if t_rows else [],
                [jnp.zeros((w_rows, width), F32)] * 2 if w_rows else [],
            )

        if m < 0 or m >= CHUNKS:
            return lambda: (
                jnp.zeros((size, width), BF16),
                jnp.zeros((size, both), BF16),
                jnp.zeros((size, hidden_dim), BF16),
                jnp.zeros((width,), F32),
                *carry_zeros(),
            )

        def widened(parts):
            used = sum(part.shape[1] for part in parts)
            return jnp.concatenate(list(parts) + [jnp.zeros((size, both - used), BF16)], axis=1)

        def taylor():
            dmix = nt(upstream, pack_out[:width]).astype(BF16)
            dq, dk, dv = taylor_backward(
                m,
                docs,
                kepts[f - m : f + 1],
                dmix,
                taylor_cols // 128,
                denoms[f],
                taylor_later[t],
            )
            own = slice(m * size, (m + 1) * size)
            grad = [dq.astype(BF16), dk[own].astype(BF16), dv[own].astype(BF16)]
            grad_normed = nt(jnp.concatenate(grad, axis=1), pack_in[:, :taylor_cols])
            g, grad_gain = rms_backward(entry, gain_row, upstream, grad_normed)
            carry = [dk[: m * size], dv[: m * size]] if m > 0 else []
            return g, widened(grad), jnp.zeros((size, hidden_dim), BF16), grad_gain, carry, carry_zeros()[1]

        def window():
            dmix = nt(upstream, pack_out[:width]).astype(BF16)
            results = window_backward(
                m, docs, kept, kepts[f - 1] if m > 0 else None, dmix, window_later[t]
            )
            grad = list(results[:3])
            grad_normed = nt(jnp.concatenate(grad, axis=1), pack_in[:, :window_cols])
            g, grad_gain = rms_backward(entry, gain_row, upstream, grad_normed)
            return (
                g,
                widened(grad),
                jnp.zeros((size, hidden_dim), BF16),
                grad_gain,
                carry_zeros()[0],
                list(results[3:]),
            )

        def dense():
            gate = kept[:, :hidden_dim].astype(F32)
            up = kept[:, hidden_dim:].astype(F32)
            sg = jax.nn.sigmoid(gate)
            hidden = (gate * sg * up).astype(BF16)
            grad_hidden = nt(upstream, pack_out)
            grad_gate = (grad_hidden * up * sg * (1.0 + gate * (1.0 - sg))).astype(BF16)
            grad_up = (grad_hidden * gate * sg).astype(BF16)
            grad = jnp.concatenate([grad_gate, grad_up], axis=1)
            grad_normed = nt(grad, pack_in)
            g, grad_gain = rms_backward(entry, gain_row, upstream, grad_normed)
            return g, grad, hidden, grad_gain, *carry_zeros()

        return (taylor, dense, window, dense)[s]

    sent = []
    for t in range(turns):
        m_last = CHUNKS - 1 - t
        upstream = feed[max(m_last, 0)]
        if t >= LAG:
            arrived = sent[t - LAG]
            upstream = jnp.where(section == last, upstream, arrived) if m_last >= 0 else arrived
        g, grad, hidden, grad_gain, t_carry, w_carry = lax.switch(
            section, [backward_branch(s, t, upstream) for s in range(sections)]
        )
        taylor_later[t + 1] = tuple(t_carry) or None
        window_later[t + 1] = tuple(w_carry) or None
        grads_low.append(grad)
        hiddens.append(hidden)
        upstreams.append(upstream)
        gain_total = gain_total + grad_gain
        m_first = CHUNKS - 1 - (t - LAG * last)
        if 0 <= m_first < CHUNKS:
            returned[m_first] = g
        if t < turns - LAG:
            sent.append(lax.ppermute(g, "section", [(i + 1, i) for i in range(last)]))

    def weight_branch(s):
        first = LAG * (last - s)
        picks = range(first, first + CHUNKS)

        def joined_turns(parts):
            return jnp.concatenate(parts, axis=0)

        def branch():
            entry = joined_turns([entries[turns - 1 - t] for t in picks]).astype(F32)
            normed, _ = rms_forward(entry, gain_row)
            upstream = joined_turns([upstreams[t] for t in picks])
            used = (taylor_cols, both, window_cols, both)[s]
            grad = joined_turns([grads_low[t][:, :used] for t in picks])
            if s % 2 == 1:
                hidden = joined_turns([hiddens[t] for t in picks])
            else:
                hidden = joined_turns(
                    [kepts[turns - 1 - t][:, used : used + width] for t in picks]
                )
            grad_in = tn(normed, grad).astype(BF16)
            grad_out = tn(hidden, upstream).astype(BF16)
            if s % 2 == 0:
                grad_in = jnp.pad(grad_in, ((0, 0), (0, both - used)))
                grad_out = jnp.pad(grad_out, ((0, hidden_dim - width), (0, 0)))
            return grad_in, grad_out

        return branch

    grad_in, grad_out = lax.switch(section, [weight_branch(s) for s in range(sections)])
    axes = ("dp", "seq")
    grad_in = lax.psum_scatter(grad_in, axes, scatter_dimension=0, tiled=True)
    grad_out = lax.psum_scatter(grad_out, axes, scatter_dimension=0, tiled=True)
    grad_gain = lax.psum_scatter(gain_total, axes, scatter_dimension=0, tiled=True)

    def spread(parts, source):
        two = swapped(jnp.concatenate(parts, axis=0).reshape(2, block, width))
        share = width // sections
        mine = two[:, :, source * share : (source + 1) * share]
        for target in range(sections):
            if target != source:
                piece = two[:, :, target * share : (target + 1) * share]
                came = lax.ppermute(piece, "section", [(source, target)])
                mine = jnp.where(section == target, came, mine)
        return mine

    return (
        spread(finals, last),
        spread(returned, 0),
        grad_in.astype(F32)[None],
        grad_out.astype(F32)[None],
        grad_gain[None],
    )


def solution(mesh):
    placed = (
        P("dp", "seq", None),
        P("section", None, None),
        P("section", None, None),
        P("section", None),
        P("dp", None),
        P("dp", "seq", None),
    )
    return jax.shard_map(
        local,
        mesh=mesh,
        in_specs=placed,
        out_specs=(
            P("dp", "seq", "section"),
            P("dp", "seq", "section"),
            P("section", ("dp", "seq"), None),
            P("section", ("dp", "seq"), None),
            P("section", ("dp", "seq")),
        ),
        check_vma=False,
    )
```

time: 2780 us -> 811 us (0.29)
  matrix products: 872 us -> 58 us
  other arithmetic: 467 us -> 66 us
  local copies, waits for them, and re-layouts: 433 us -> 77.1 us
  loops' own time: 316 us -> 78.8 us
  waiting for transfers between devices: 525 us -> 342 us
  Pallas kernels: 0 us -> 85.8 us
  blocking collectives: 94 us -> 17.2 us
    dot_general x130 -> x18, matrix products: 872 us -> 58 us  [the longest x8 24.7 us: nt(): lax.dot_general(a, b, (((1,), (1,)), ((), ())), preferred_element_type=F32)]
    reduce_scatter x4 -> x2, waiting for transfers between devices: 401 us -> 130 us  [the longest x1 115 us: local(): grad_in = lax.psum_scatter(grad_in, axes, scatter_dimension=0, tiled=True)]
    unnamed x10 -> x2, loops' own time: 170 us -> 17.5 us
    add x65 -> x2, other arithmetic: 142 us -> 1.77 us  [the longest x1 1.76 us: rms_backward(): return ((upstream.astype(F32) + grad_inputs).astype(BF16), grad_gain)]
    ppermute x25 -> x21, waiting for transfers between devices: 107 us -> 212 us  [the longest x6 143 us: local(): sent.append(lax.ppermute(g, 'section', [(i + 1, i) for i in range(last)]))]
    div x60 -> x0, other arithmetic: 103 us -> none  [the longest x20 61.2 us: taylor_features(): square / math.sqrt(2.0 * feat_width)]
    another operation x140 -> x45, local copies, waits for them, and re-layouts: 132 us -> 32 us
    pad x20 -> x2, local copies, waits for them, and re-layouts: 108 us -> 7.92 us  [the longest x1 4.82 us: branch(): grad_in = jnp.pad(grad_in, ((0, 0), (0, both - used)))]
  transfers between devices with their start and end apart: 44 -> 23, of which waited for: 20 -> 16; matrix products, arithmetic and copies ran while one was open for 6% -> 2% of each run, Pallas kernels for 0% -> 0%
where the time goes in v1:
time: 811 us; the launch traced here: 807 us
  waiting for transfers between devices  342 us (42%)
  Pallas kernels  85.8 us (11%)
  loops' own time  78.8 us (10%)
  local copies, waits for them, and re-layouts  77.1 us (10%)
  starting transfers between devices  66.1 us (8%)
  other arithmetic  66 us (8%)
  matrix products  58 us (7%)
  blocking collectives  17.2 us (2%)
  between operations  15.6 us (2%)
    ppermute x6, waiting for transfers between devices, local(): sent.append(lax.ppermute(g, 'section', [(i + 1, i) for i in range(last)]))  143 us
    reduce_scatter x1, waiting for transfers between devices, local(): grad_in = lax.psum_scatter(grad_in, axes, scatter_dimension=0, tiled=True)  115 us
    ppermute x6, waiting for transfers between devices, local(): lax.ppermute(output, 'section', [(i, i + 1) for i in range(last)])  59.1 us
    pallas_call x4, Pallas kernels, taylor_backward(): call(functools.partial(taylor_backward_kernel, m, size, later is not None...  53.7 us
    ppermute x6, starting transfers between devices, local(): lax.ppermute(output, 'section', [(i, i + 1) for i in range(last)])  50.1 us
    another operation x6, loops' own time, local(): lax.switch(section, [backward_branch(s, t, upstream) for s in range(secti...  34.1 us
    pallas_call x4, Pallas kernels, taylor_forward(): call(functools.partial(taylor_forward_kernel, m, size), (PAIRS,), [whole(...  32.1 us
    another operation x45, local copies, waits for them, and re-layouts  32 us
  transfers between devices with their start and end apart: 23, of which 16 were waited for; matrix products, arithmetic and copies ran while one was open for 2% of the time, Pallas kernels for 0%

profile of v1, /device:TPU:0, one launch (start us, length us, event | category | flops | bytes accessed | tf_op | source)
XLA Modules:
  0.0 806.6 jit_solution(17588369222663882875)
XLA Ops:
  14.1 12.4 %conditional.19 = (bf16[256,1024]{1,0:T(8,128)(2,1)S(1)}, bf16[256,5504]{1,0:T(8,128)(2,1)S(1)}, f32[256,128]{1,0:T(8,128)S(1)}) conditional(s32[]{:T(128)} %clamp.2, (bf16[256,1024]{1,0:T(8,128)(2,1)}, f32[1,1024]{1,0:T(1,128)S(1)}, bf16[1024,5504]{1,0:T(8,128)(2,1)}, s32[1024,1]{0,1:T(1,128)S(1)}, ...), branch_computations={%region_1.3_spmd, %region_3.4_spmd, %region_4.5_spmd, %region_5.6_... | conditional | flops 2427388160 | bytes 14926876 | solution.py:471
  15.5 3.1 fusion.2.refs_2_.refs_3_.refs_4_
  18.7 5.1 branch_0_fun.9
  28.5 12.0 %collective-permute-done.1 = bf16[256,1024]{1,0:T(8,128)(2,1)S(1)} collective-permute-done((bf16[256,1024]{1,0:T(8,128)(2,1)S(1)}, bf16[256,1024]{1,0:T(8,128)(2,1)S(1)}, u32[]{:S(2)}, u32[]{:S(2)}) %collective-permute-start.1) | collective-permute-done | bytes 524320 | tf_op jit(solution)/shard_map/ppermute | solution.py:480
  42.3 15.0 %conditional.20 = (bf16[256,1024]{1,0:T(8,128)(2,1)S(1)}, bf16[256,5504]{1,0:T(8,128)(2,1)}, f32[256,128]{1,0:T(8,128)S(1)}) conditional(s32[]{:T(128)} %clamp.2, (bf16[256,1024]{1,0:T(8,128)(2,1)}, f32[1,1024]{1,0:T(1,128)S(1)}, bf16[1024,5504]{1,0:T(8,128)(2,1)}, s32[1024,1]{0,1:T(1,128)S(1)}, ...), branch_computations={%region_6.8_spmd, %region_8.10_spmd, %region_10.11_spmd, %region_1... | conditional | flops 4336779264 | bytes 50274380 | solution.py:471
  43.8 3.1 fusion.20.refs_2_.refs_4_.refs_6_
  47.0 6.1 branch_0_fun.10
  57.4 15.2 %collective-permute-start.2 = (bf16[256,1024]{1,0:T(8,128)(2,1)S(1)}, bf16[256,1024]{1,0:T(8,128)(2,1)S(1)}, u32[]{:S(2)}, u32[]{:S(2)}) collective-permute-start(bf16[256,1024]{1,0:T(8,128)(2,1)S(1)} %get-tuple-element.1105), channel_id=1, source_target_pairs={{0,8},{8,16},{16,24},{1,9},{9,17},{17,25},{2,10},{10,18},{18,26},{... | collective-permute-start | bytes 1572872 | tf_op jit(solution)/shard_map/ppermute | solution.py:480
  72.6 11.1 %collective-permute-done.2 = bf16[256,1024]{1,0:T(8,128)(2,1)S(1)} collective-permute-done((bf16[256,1024]{1,0:T(8,128)(2,1)S(1)}, bf16[256,1024]{1,0:T(8,128)(2,1)S(1)}, u32[]{:S(2)}, u32[]{:S(2)}) %collective-permute-start.2) | collective-permute-done | bytes 524320 | tf_op jit(solution)/shard_map/ppermute | solution.py:480
  85.7 18.8 %conditional.21 = (bf16[256,1024]{1,0:T(8,128)(2,1)S(1)}, bf16[256,5504]{1,0:T(8,128)(2,1)}, f32[256,128]{1,0:T(8,128)S(1)}) conditional(s32[]{:T(128)} %clamp.2, (bf16[256,1024]{1,0:T(8,128)(2,1)}, f32[1,1024]{1,0:T(1,128)S(1)}, bf16[1024,5504]{1,0:T(8,128)(2,1)}, s32[1024,1]{0,1:T(1,128)S(1)}, ...), branch_computations={%region_12.14_spmd, %region_14.16_spmd, %region_16.18_spmd, %regio... | conditional | flops 4574871552 | bytes 50274380 | solution.py:471
  87.2 3.1 fusion.54.refs_2_.refs_5_.refs_8_
  90.3 9.8 %branch_0_fun.11 = (bf16[256,1024]{1,0:T(8,128)(2,1)S(1)}, f32[256,128]{1,0:T(8,128)S(1)}) custom-call(s32[1024,1]{1,0:T(8,128)S(1)} %copy.194.refs_0_, s32[1,1024]{1,0:T(1,128)S(1)} %get-tuple-element.727.refs_1_, bf16[256,1536]{1,0:T(8,128)(2,1)S(1)} %fusion.54.refs_2_.refs_5_.refs_8_, bf16[256,5504]{1,0:T(8,128)(2,1)S(1)} %get-tuple-element.730.refs_3_.refs_6_, ...), custom_call_target="tpu_custom_call" | custom-call | flops 3221225472 | bytes 6291456 | tf_op jit(solution)/shard_map/cond/branch_0_fun/pallas_call | solution.py:108
  105.8 10.5 %collective-permute-done.3 = bf16[256,1024]{1,0:T(8,128)(2,1)S(1)} collective-permute-done((bf16[256,1024]{1,0:T(8,128)(2,1)S(1)}, bf16[256,1024]{1,0:T(8,128)(2,1)S(1)}, u32[]{:S(2)}, u32[]{:S(2)}) %collective-permute-start.3) | collective-permute-done | bytes 524320 | tf_op jit(solution)/shard_map/ppermute | solution.py:480
  118.2 18.7 %conditional.58 = (bf16[256,5504]{1,0:T(8,128)(2,1)S(1)}, f32[256,128]{1,0:T(8,128)S(1)}, bf16[256,1024]{1,0:T(8,128)(2,1)S(1)}) conditional(s32[]{:T(128)} %clamp.2, (bf16[256,1024]{1,0:T(8,128)(2,1)}, f32[1,1024]{1,0:T(1,128)S(1)}, bf16[1024,5504]{1,0:T(8,128)(2,1)}, s32[1024,1]{0,1:T(1,128)S(1)}, ...), branch_computations={%region_19.21_spmd, %region_21.23_spmd, %region_23.25_spmd, %regio... | conditional | flops 5648613376 | bytes 50274380
  119.7 3.1 fusion.106.refs_2_.refs_6_.refs_10_
  122.8 11.1 %branch_0_fun.12 = (bf16[256,1024]{1,0:T(8,128)(2,1)S(1)}, f32[256,128]{1,0:T(8,128)S(1)}) custom-call(s32[1024,1]{1,0:T(8,128)S(1)} %copy.196.refs_0_, s32[1,1024]{1,0:T(1,128)S(1)} %get-tuple-element.749.refs_1_, bf16[256,1536]{1,0:T(8,128)(2,1)S(1)} %fusion.106.refs_2_.refs_6_.refs_10_, bf16[256,5504]{1,0:T(8,128)(2,1)S(1)} %get-tuple-element.750.refs_3_.refs_7_, ...), custom_call_target="tpu_custom_call" | custom-call | flops 4294967296 | bytes 8388608 | tf_op jit(solution)/shard_map/cond/branch_0_fun/pallas_call | solution.py:108
  133.9 2.4 fusion.113
  137.0 3.5 collective-permute-start.4
  140.5 8.8 %collective-permute-done.4 = bf16[256,1024]{1,0:T(8,128)(2,1)} collective-permute-done((bf16[256,1024]{1,0:T(8,128)(2,1)S(1)}, bf16[256,1024]{1,0:T(8,128)(2,1)}, u32[]{:S(2)}, u32[]{:S(2)}) %collective-permute-start.4) | collective-permute-done | bytes 524320 | tf_op jit(solution)/shard_map/ppermute | solution.py:480
  149.3 10.5 %conditional.23 = (bf16[256,1024]{1,0:T(8,128)(2,1)S(1)}, bf16[256,5504]{1,0:T(8,128)(2,1)}) conditional(s32[]{:T(128)} %clamp.2, () %tuple.308, (bf16[256,1024]{1,0:T(8,128)(2,1)}, f32[1,1024]{1,0:T(1,128)S(1)}, bf16[1024,5504]{1,0:T(8,128)(2,1)}, bf16[2752,1024]{1,0:T(8,128)(2,1)}) %tuple.754, ...), branch_computations={%region_27.28_spmd, %region_28.30_spmd, %region_30.32_spmd, %regio... | conditional | flops 4336779264 | bytes 50143296 | solution.py:471
  159.8 24.4 %collective-permute-start.5 = (bf16[256,1024]{1,0:T(8,128)(2,1)S(1)}, bf16[256,1024]{1,0:T(8,128)(2,1)S(1)}, u32[]{:S(2)}, u32[]{:S(2)}) collective-permute-start(bf16[256,1024]{1,0:T(8,128)(2,1)S(1)} %get-tuple-element.1111), channel_id=1, source_target_pairs={{0,8},{8,16},{16,24},{1,9},{9,17},{17,25},{2,10},{10,18},{18,26},{... | collective-permute-start | bytes 1572872 | tf_op jit(solution)/shard_map/ppermute | solution.py:480
  184.1 8.7 %collective-permute-done.5 = bf16[256,1024]{1,0:T(8,128)(2,1)S(1)} collective-permute-done((bf16[256,1024]{1,0:T(8,128)(2,1)S(1)}, bf16[256,1024]{1,0:T(8,128)(2,1)S(1)}, u32[]{:S(2)}, u32[]{:S(2)}) %collective-permute-start.5) | collective-permute-done | bytes 524320 | tf_op jit(solution)/shard_map/ppermute | solution.py:480
  194.7 4.4 collective-permute-start.6
  199.1 8.0 collective-permute-done.6
  208.2 11.4 %conditional.50 = (bf16[256,1024]{1,0:T(8,128)(2,1)}, bf16[256,5504]{0,1:T(8,128)(2,1)}, bf16[256,2752]{0,1:T(8,128)(2,1)}, f32[1024]{0:T(1024)S(1)}) conditional(s32[]{:T(128)} %clamp.2, () %tuple.322, () %tuple.323, () %tuple.324, (bf16[256,1024]{1,0:T(8,128)(2,1)}, bf16[256,1024]{1,0:T(8,128)(2,1)S(1)}, ...), branch_computations={%region_45.46_spmd, %region_46.47_spmd, %region_47.48_spmd, %regio... | conditional | flops 4351819776 | bytes 94690520 | solution.py:573
  221.0 27.3 %collective-permute-done.11 = bf16[256,1024]{1,0:T(8,128)(2,1)S(1)} collective-permute-done((bf16[256,1024]{1,0:T(8,128)(2,1)}, bf16[256,1024]{1,0:T(8,128)(2,1)S(1)}, u32[]{:S(2)}, u32[]{:S(2)}) %collective-permute-start.11) | collective-permute-done | bytes 524320 | tf_op jit(solution)/shard_map/ppermute | solution.py:586
  250.2 10.6 %conditional.51 = (bf16[256,1024]{1,0:T(8,128)(2,1)}, bf16[256,5504]{0,1:T(8,128)(2,1)}, bf16[256,2752]{0,1:T(8,128)(2,1)S(1)}, f32[1024]{0:T(1024)S(1)}, f32[128,1024]{1,0:T(8,128)}, /*index=5*/f32[128,1024]{1,0:T(8,128)}) conditional(s32[]{:T(128)} %clamp.2, () %tuple.320, () %tuple.321, ...), branch_computations={%region_52.53_spmd, %region_53.54_spmd, %region_54.58_spmd, %regio... | conditional | flops 4853071872 | bytes 88005840 | solution.py:573
  262.1 10.6 %collective-permute-done.12 = bf16[256,1024]{1,0:T(8,128)(2,1)S(1)} collective-permute-done((bf16[256,1024]{1,0:T(8,128)(2,1)}, bf16[256,1024]{1,0:T(8,128)(2,1)S(1)}, u32[]{:S(2)}, u32[]{:S(2)}) %collective-permute-start.12) | collective-permute-done | bytes 524320 | tf_op jit(solution)/shard_map/ppermute | solution.py:586
  274.6 12.0 %conditional.52 = (bf16[256,1024]{1,0:T(8,128)(2,1)}, bf16[256,5504]{0,1:T(8,128)(2,1)}, bf16[256,2752]{0,1:T(8,128)(2,1)}, f32[1024]{0:T(1024)S(1)}, f32[128,1024]{1,0:T(8,128)}, /*index=5*/f32[128,1024]{1,0:T(8,128)}) conditional(s32[]{:T(128)} %clamp.2, () %tuple.319, (bf16[256,1024]{1,0:T(8,128)(2,1)S(1)}, ...), branch_computations={%region_62.63_spmd, %region_63.67_spmd, %region_67.71_spmd, %regio... | conditional | flops 4853071872 | bytes 78175360 | solution.py:573
  288.0 75.3 %collective-permute-done.13 = bf16[256,1024]{1,0:T(8,128)(2,1)S(1)} collective-permute-done((bf16[256,1024]{1,0:T(8,128)(2,1)}, bf16[256,1024]{1,0:T(8,128)(2,1)S(1)}, u32[]{:S(2)}, u32[]{:S(2)}) %collective-permute-start.13) | collective-permute-done | bytes 524320 | tf_op jit(solution)/shard_map/ppermute | solution.py:586
  365.1 63.2 %conditional.59 = (bf16[256,5504]{0,1:T(8,128)(2,1)}, bf16[256,2752]{0,1:T(8,128)(2,1)}, f32[768,256]{1,0:T(8,128)}, f32[768,1024]{1,0:T(8,128)}, f32[128,1024]{...) conditional(s32[]{:T(128)} %clamp.2, ...), branch_computations={%region_75.78_spmd, %region_78.81_spmd, %region_81.84_spmd, %regio... | conditional | flops 12097487872 | bytes 95997168
  365.4 2.6 fusion.390.refs_11_
  368.1 18.6 %branch_0_fun.13 = (f32[256,256]{1,0:T(8,128)S(1)}, f32[1024,256]{1,0:T(8,128)S(1)}, f32[1024,1024]{1,0:T(8,128)S(1)}) custom-call(s32[1024,1]{1,0:T(8,128)S(1)} %copy.206.refs_0_, s32[1,1024]{1,0:T(1,128)S(1)} %get-tuple-element.856.refs_1_, bf16[256,5504]{1,0:T(8,128)(2,1)} %get-tuple-element.857.refs_2_.refs_6_.refs_10_.refs_12_, ...), custom_call_target="tpu_custom_call" | custom-call | flops 10737418240 | bytes 20971520 | tf_op jit(solution)/shard_map/cond/branch_0_fun/pallas_call | solution.py:196
  391.1 3.9 slice.278
  395.3 4.1 fusion.397
  403.9 6.1 maximum_maximum_fusion.10
  429.6 9.9 %collective-permute-done.14 = bf16[256,1024]{1,0:T(8,128)(2,1)} collective-permute-done((bf16[256,1024]{1,0:T(8,128)(2,1)S(1)}, bf16[256,1024]{1,0:T(8,128)(2,1)}, u32[]{:S(2)}, u32[]{:S(2)}) %collective-permute-start.14) | collective-permute-done | bytes 524320 | tf_op jit(solution)/shard_map/ppermute | solution.py:586
  439.5 38.2 %conditional.54 = (bf16[256,1024]{1,0:T(8,128)(2,1)}, bf16[256,5504]{1,0:T(8,128)(2,1)}, bf16[256,2752]{1,0:T(8,128)(2,1)}, f32[1024]{0:T(1024)S(1)}, f32[512,256]{1,0:T(8,128)S(1)}, /*index=5*/f32[512,1024]{1,0:T(8,128)S(1)}) conditional(s32[]{:T(128)} %clamp.2, (bf16[256,1024]{1,0:T(8,128)(2,1)}, ...), branch_computations={%region_87.91_spmd, %region_91.95_spmd, %region_95.99_spmd, %regio... | conditional | flops 9414180864 | bytes 78739584 | solution.py:573
  441.8 2.5 fusion.456.refs_9_
  444.3 15.8 %branch_0_fun.14 = (f32[256,256]{1,0:T(8,128)S(1)}, f32[768,256]{1,0:T(8,128)S(1)}, f32[768,1024]{1,0:T(8,128)S(1)}) custom-call(s32[1024,1]{1,0:T(8,128)S(1)} %copy.210.refs_0_, s32[1,1024]{1,0:T(1,128)S(1)} %get-tuple-element.901.refs_1_, bf16[256,5504]{1,0:T(8,128)(2,1)} %get-tuple-element.902.refs_2_.refs_5_.refs_8_.refs_10_, ...), custom_call_target="tpu_custom_call" | custom-call | flops 8053063680 | bytes 15728640 | tf_op jit(solution)/shard_map/cond/branch_0_fun/pallas_call | solution.py:196
  460.5 3.2 fusion.466
  479.0 10.1 %collective-permute-done.15 = bf16[256,1024]{1,0:T(8,128)(2,1)} collective-permute-done((bf16[256,1024]{1,0:T(8,128)(2,1)}, bf16[256,1024]{1,0:T(8,128)(2,1)}, u32[]{:S(2)}, u32[]{:S(2)}) %collective-permute-start.15) | collective-permute-done | bytes 524320 | tf_op jit(solution)/shard_map/ppermute | solution.py:586
  489.1 37.6 %conditional.55 = (bf16[256,1024]{1,0:T(8,128)(2,1)}, bf16[256,5504]{0,1:T(8,128)(2,1)}, bf16[256,2752]{0,1:T(8,128)(2,1)}, f32[1024]{0:T(1024)}, f32[256,256]{1,0:T(8,128)S(1)}, /*index=5*/f32[256,1024]{1,0:T(8,128)}) conditional(s32[]{:T(128)} %clamp.2, (bf16[256,1024]{1,0:T(8,128)(2,1)}, ...), branch_computations={%region_100.0_spmd, %region_104.108_spmd, %region_108.109_spmd, %r... | conditional | flops 6729826304 | bytes 78437504 | solution.py:573
  491.6 2.6 fusion.517.refs_7_
  494.2 11.2 %branch_0_fun.15 = (f32[256,256]{1,0:T(8,128)S(1)}, f32[512,256]{1,0:T(8,128)S(1)}, f32[512,1024]{1,0:T(8,128)S(1)}) custom-call(s32[1024,1]{1,0:T(8,128)S(1)} %copy.213.refs_0_, s32[1,1024]{1,0:T(1,128)S(1)} %get-tuple-element.936.refs_1_, bf16[256,5504]{1,0:T(8,128)(2,1)} %get-tuple-element.937.refs_2_.refs_4_.refs_6_.refs_8_, ...), custom_call_target="tpu_custom_call" | custom-call | flops 5368709120 | bytes 10485760 | tf_op jit(solution)/shard_map/cond/branch_0_fun/pallas_call | solution.py:196
  508.3 3.9 fusion.527
  514.6 6.1 maximum_maximum_fusion.14
  528.1 10.1 %collective-permute-done.16 = bf16[256,1024]{1,0:T(8,128)(2,1)} collective-permute-done((bf16[256,1024]{1,0:T(8,128)(2,1)}, bf16[256,1024]{1,0:T(8,128)(2,1)}, u32[]{:S(2)}, u32[]{:S(2)}) %collective-permute-start.16) | collective-permute-done | bytes 524320 | tf_op jit(solution)/shard_map/ppermute | solution.py:586
  538.1 18.1 %conditional.56 = (bf16[256,1024]{1,0:T(8,128)(2,1)S(1)}, bf16[256,5504]{1,0:T(8,128)(2,1)S(1)}, f32[1024]{0:T(1024)S(1)}) conditional(s32[]{:T(128)} %clamp.2, (bf16[256,1024]{1,0:T(8,128)(2,1)}, bf16[256,1024]{1,0:T(8,128)(2,1)}, bf16[2752,1024]{1,0:T(8,128)(2,1)}, s32[1024,1]{0,1:T(1,128)S(1)}, ...), branch_computations={%region_110.0_spmd, %region_114.115_spmd, %region_115.116_spmd, %r... | conditional | flops 4045799168 | bytes 37010600 | solution.py:573
  540.4 2.5 fusion.556.refs_5_
  543.0 8.1 branch_0_fun.16
  551.2 3.2 fusion.566
  557.1 58.2 %conditional.57 = (bf16[1024,5504]{1,0:T(8,128)(2,1)}, bf16[2752,1024]{1,0:T(8,128)(2,1)}) conditional(s32[]{:T(128)} %clamp.2, (bf16[256,1024]{1,0:T(8,128)(2,1)}, bf16[256,1024]{1,0:T(8,128)(2,1)}, bf16[256,1024]{1,0:T(8,128)(2,1)}, bf16[256,1024]{1,0:T(8,128)(2,1)}, f32[1,1024]{1,0:T(1,128)S(1)}, ...), branch_computations={%region_117.119_spmd, %region_119.121_spmd, %region_121.123_spmd, ... | conditional | flops 17420582912 | bytes 122966264 | solution.py:616
  563.6 5.1 fusion.601
  571.8 4.7 copy.217
  578.5 3.4 copy.216
  583.2 6.1 convolution_convert_fusion
  589.2 3.1 pad.12
  592.3 4.8 pad.11
  635.3 7.3 collective-permute-done.10
  645.8 17.2 %all-reduce.4 = f32[1024]{0:T(1024)S(1)} all-reduce(f32[1024]{0:T(1024)S(1)} %add_add_fusion), channel_id=4, replica_groups=mesh['section'=4,'dp'=4,'seq'=2] {'dp','seq'}, use_global_device_ids=true, to_apply=%region_128.129.clone | all-reduce | flops 1024 | bytes 8192
  664.6 14.2 %reduce-scatter.5.cloned.1.call-done = bf16[344,1024]{1,0:T(8,128)(2,1)} async-done(((bf16[2752,1024]{1,0:T(8,128)(2,1)}), bf16[344,1024]{1,0:T(8,128)(2,1)}) %reduce-scatter.5.cloned.1.call-update) | async-done | bytes 704528 | tf_op jit(solution)/shard_map/reduce_scatter | solution.py:619
  681.1 115.3 %reduce-scatter.3.cloned.1.call-done = bf16[128,5504]{1,0:T(8,128)(2,1)} async-done(((bf16[1024,5504]{1,0:T(8,128)(2,1)}), bf16[128,5504]{1,0:T(8,128)(2,1)}) %reduce-scatter.3.cloned.1.call-update) | async-done | bytes 1409040 | tf_op jit(solution)/shard_map/reduce_scatter | solution.py:618
  796.5 3.1 bitcast_convert_fusion
  (300 shorter events, 137.9 us)
Async XLA Ops:
  7.2 2.6 copy-start
  7.2 671.6 %reduce-scatter.5.cloned.1.call-start = ((), (), s32[]{:S(2)}) async-start(), calls=%async_computation.3 | async-start | bytes 6340608 | tf_op jit(solution)/shard_map/reduce_scatter | solution.py:619
  9.2 2.8 collective-permute-start
  27.1 91.1 %copy-start.4 = (bf16[256,5504]{1,0:T(8,128)(2,1)}, bf16[256,5504]{1,0:T(8,128)(2,1)S(1)}, u32[]{:S(2)}) copy-start(bf16[256,5504]{1,0:T(8,128)(2,1)S(1)} %get-tuple-element.1104) | copy-start | bytes 8454148
  27.1 13.3 %collective-permute-start.1 = (bf16[256,1024]{1,0:T(8,128)(2,1)S(1)}, bf16[256,1024]{1,0:T(8,128)(2,1)S(1)}, u32[]{:S(2)}, u32[]{:S(2)}) collective-permute-start(bf16[256,1024]{1,0:T(8,128)(2,1)S(1)} %get-tuple-element.1103), channel_id=1, source_target_pairs={{0,8},{8,16},{16,24},{1,9},{9,17},{17,25},{2,10},{10,18},{18,26},{... | collective-permute-start | bytes 1572872 | tf_op jit(solution)/shard_map/ppermute | solution.py:480
  57.4 28.3 %copy-start.91 = (f32[256,128]{1,0:T(8,128)}, f32[256,128]{1,0:T(8,128)S(1)}, u32[]{:S(2)}) copy-start(f32[256,128]{1,0:T(8,128)S(1)} %get-tuple-element.1132) | copy-start | bytes 393220
  57.4 26.3 %collective-permute-start.2 = (bf16[256,1024]{1,0:T(8,128)(2,1)S(1)}, bf16[256,1024]{1,0:T(8,128)(2,1)S(1)}, u32[]{:S(2)}, u32[]{:S(2)}) collective-permute-start(bf16[256,1024]{1,0:T(8,128)(2,1)S(1)} %get-tuple-element.1105), channel_id=1, source_target_pairs={{0,8},{8,16},{16,24},{1,9},{9,17},{17,25},{2,10},{10,18},{18,26},{... | collective-permute-start | bytes 1572872 | tf_op jit(solution)/shard_map/ppermute | solution.py:480
  104.5 13.8 %copy-start.107 = (f32[256,128]{1,0:T(8,128)}, f32[256,128]{1,0:T(8,128)S(1)}, u32[]{:S(2)}) copy-start(f32[256,128]{1,0:T(8,128)S(1)} %get-tuple-element.1126) | copy-start | bytes 393220
  104.5 11.8 %collective-permute-start.3 = (bf16[256,1024]{1,0:T(8,128)(2,1)S(1)}, bf16[256,1024]{1,0:T(8,128)(2,1)S(1)}, u32[]{:S(2)}, u32[]{:S(2)}) collective-permute-start(bf16[256,1024]{1,0:T(8,128)(2,1)S(1)} %get-tuple-element.1107), channel_id=1, source_target_pairs={{0,8},{8,16},{16,24},{1,9},{9,17},{17,25},{2,10},{10,18},{18,26},{... | collective-permute-start | bytes 1572872 | tf_op jit(solution)/shard_map/ppermute | solution.py:480
  136.9 12.4 %copy-start.87 = (bf16[256,1024]{1,0:T(8,128)(2,1)}, bf16[256,1024]{1,0:T(8,128)(2,1)S(1)}, u32[]{:S(2)}) copy-start(bf16[256,1024]{1,0:T(8,128)(2,1)S(1)} %get-tuple-element.2096) | copy-start | bytes 1572868
  136.9 12.4 %copy-start.9 = (bf16[256,5504]{1,0:T(8,128)(2,1)}, bf16[256,5504]{1,0:T(8,128)(2,1)S(1)}, u32[]{:S(2)}) copy-start(bf16[256,5504]{1,0:T(8,128)(2,1)S(1)} %get-tuple-element.1110) | copy-start | bytes 8454148
  136.9 12.4 %copy-start.109 = (f32[256,128]{1,0:T(8,128)}, f32[256,128]{1,0:T(8,128)S(1)}, u32[]{:S(2)}) copy-start(f32[256,128]{1,0:T(8,128)S(1)} %get-tuple-element.1122) | copy-start | bytes 393220
  137.0 12.3 %collective-permute-start.4 = (bf16[256,1024]{1,0:T(8,128)(2,1)S(1)}, bf16[256,1024]{1,0:T(8,128)(2,1)}, u32[]{:S(2)}, u32[]{:S(2)}) collective-permute-start(bf16[256,1024]{1,0:T(8,128)(2,1)S(1)} %get-tuple-element.2096), channel_id=1, source_target_pairs={{0,8},{8,16},{16,24},{1,9},{9,17},{17,25},{2,10},{10,18},{18,26},{... | collective-permute-start | bytes 1572872 | tf_op jit(solution)/shard_map/ppermute | solution.py:480
  159.8 33.0 %copy-start.71 = (bf16[256,1024]{1,0:T(8,128)(2,1)}, bf16[256,1024]{1,0:T(8,128)(2,1)S(1)}, u32[]{:S(2)}) copy-start(bf16[256,1024]{1,0:T(8,128)(2,1)S(1)} %get-tuple-element.1111) | copy-start | bytes 1572868
  159.8 33.0 %collective-permute-start.5 = (bf16[256,1024]{1,0:T(8,128)(2,1)S(1)}, bf16[256,1024]{1,0:T(8,128)(2,1)S(1)}, u32[]{:S(2)}, u32[]{:S(2)}) collective-permute-start(bf16[256,1024]{1,0:T(8,128)(2,1)S(1)} %get-tuple-element.1111), channel_id=1, source_target_pairs={{0,8},{8,16},{16,24},{1,9},{9,17},{17,25},{2,10},{10,18},{18,26},{... | collective-permute-start | bytes 1572872 | tf_op jit(solution)/shard_map/ppermute | solution.py:480
  194.7 12.5 %copy-start.12 = (bf16[256,5504]{1,0:T(8,128)(2,1)}, bf16[256,5504]{1,0:T(8,128)(2,1)S(1)}, u32[]{:S(2)}) copy-start(bf16[256,5504]{1,0:T(8,128)(2,1)S(1)} %get-tuple-element.1117) | copy-start | bytes 8454148
  194.7 12.5 %collective-permute-start.6 = (bf16[256,1024]{1,0:T(8,128)(2,1)}, bf16[256,1024]{1,0:T(8,128)(2,1)S(1)}, u32[]{:S(2)}, u32[]{:S(2)}) collective-permute-start(bf16[256,1024]{1,0:T(8,128)(2,1)} %get-tuple-element.1113), channel_id=1, source_target_pairs={{0,8},{8,16},{16,24},{1,9},{9,17},{17,25},{2,10},{10,18},{18,26},{... | collective-permute-start | bytes 1572872 | tf_op jit(solution)/shard_map/ppermute | solution.py:480
  207.4 42.0 %copy-start.21 = (bf16[256,1024]{1,0:T(8,128)(2,1)S(1)}, bf16[256,1024]{1,0:T(8,128)(2,1)}, u32[]{:S(2)}) copy-start(bf16[256,1024]{1,0:T(8,128)(2,1)} %copy-done.20) | copy-start | bytes 1572868
  219.7 29.7 %copy-start.100 = (f32[1024]{0:T(1024)}, f32[1024]{0:T(1024)S(1)}, u32[]{:S(2)}) copy-start(f32[1024]{0:T(1024)S(1)} %get-tuple-element.1155) | copy-start | bytes 12292
  219.7 28.6 %collective-permute-start.11 = (bf16[256,1024]{1,0:T(8,128)(2,1)}, bf16[256,1024]{1,0:T(8,128)(2,1)S(1)}, u32[]{:S(2)}, u32[]{:S(2)}) collective-permute-start(bf16[256,1024]{1,0:T(8,128)(2,1)} %get-tuple-element.1116), channel_id=1, source_target_pairs={{8,0},{16,8},{24,16},{9,1},{17,9},{25,17},{10,2},{18,10},{26,18},{... | collective-permute-start | bytes 1572872 | tf_op jit(solution)/shard_map/ppermute | solution.py:586
  260.7 13.1 %copy-start.54 = (bf16[256,2752]{0,1:T(8,128)(2,1)}, bf16[256,2752]{0,1:T(8,128)(2,1)S(1)}, u32[]{:S(2)}) copy-start(bf16[256,2752]{0,1:T(8,128)(2,1)S(1)} %get-tuple-element.1152) | copy-start | bytes 4227076
  260.8 13.1 %copy-start.96 = (f32[1024]{0:T(1024)}, f32[1024]{0:T(1024)S(1)}, u32[]{:S(2)}) copy-start(f32[1024]{0:T(1024)S(1)} %get-tuple-element.1156) | copy-start | bytes 12292
  260.8 11.9 %collective-permute-start.12 = (bf16[256,1024]{1,0:T(8,128)(2,1)}, bf16[256,1024]{1,0:T(8,128)(2,1)S(1)}, u32[]{:S(2)}, u32[]{:S(2)}) collective-permute-start(bf16[256,1024]{1,0:T(8,128)(2,1)} %get-tuple-element.1118), channel_id=1, source_target_pairs={{8,0},{16,8},{24,16},{9,1},{17,9},{25,17},{10,2},{18,10},{26,18},{... | collective-permute-start | bytes 1572872 | tf_op jit(solution)/shard_map/ppermute | solution.py:586
  286.6 78.5 %copy-start.98 = (f32[1024]{0:T(1024)}, f32[1024]{0:T(1024)S(1)}, u32[]{:S(2)}) copy-start(f32[1024]{0:T(1024)S(1)} %get-tuple-element.1157) | copy-start | bytes 12292
  286.7 76.6 %collective-permute-start.13 = (bf16[256,1024]{1,0:T(8,128)(2,1)}, bf16[256,1024]{1,0:T(8,128)(2,1)S(1)}, u32[]{:S(2)}, u32[]{:S(2)}) collective-permute-start(bf16[256,1024]{1,0:T(8,128)(2,1)} %get-tuple-element.1121), channel_id=1, source_target_pairs={{8,0},{16,8},{24,16},{9,1},{17,9},{25,17},{10,2},{18,10},{26,18},{... | collective-permute-start | bytes 1572872 | tf_op jit(solution)/shard_map/ppermute | solution.py:586
  365.1 2.9 copy-start.5
  365.4 2.7 copy-start.110
  395.3 4.1 copy-start.33
  428.3 11.2 %copy-start.73 = (bf16[256,1024]{1,0:T(8,128)(2,1)}, bf16[256,1024]{1,0:T(8,128)(2,1)S(1)}, u32[]{:S(2)}) copy-start(bf16[256,1024]{1,0:T(8,128)(2,1)S(1)} %get-tuple-element.2108) | copy-start | bytes 1572868
  428.3 11.2 %collective-permute-start.14 = (bf16[256,1024]{1,0:T(8,128)(2,1)S(1)}, bf16[256,1024]{1,0:T(8,128)(2,1)}, u32[]{:S(2)}, u32[]{:S(2)}) collective-permute-start(bf16[256,1024]{1,0:T(8,128)(2,1)S(1)} %get-tuple-element.2108), channel_id=1, source_target_pairs={{8,0},{16,8},{24,16},{9,1},{17,9},{25,17},{10,2},{18,10},{26,18},{... | collective-permute-start | bytes 1572872 | tf_op jit(solution)/shard_map/ppermute | solution.py:586
  439.5 49.6 %copy-start.92 = (f32[256,128]{1,0:T(8,128)S(1)}, f32[256,128]{1,0:T(8,128)}, u32[]{:S(2)}) copy-start(f32[256,128]{1,0:T(8,128)} %copy-done.91) | copy-start | bytes 393220
  439.5 4.8 copy-start.6
  441.8 2.6 copy-start.108
  460.5 5.6 copy-start.94
  477.7 11.4 %copy-start.103 = (f32[1024]{0:T(1024)}, f32[1024]{0:T(1024)S(1)}, u32[]{:S(2)}) copy-start(f32[1024]{0:T(1024)S(1)} %get-tuple-element.1162) | copy-start | bytes 12292
  477.7 11.4 %collective-permute-start.15 = (bf16[256,1024]{1,0:T(8,128)(2,1)}, bf16[256,1024]{1,0:T(8,128)(2,1)}, u32[]{:S(2)}, u32[]{:S(2)}) collective-permute-start(bf16[256,1024]{1,0:T(8,128)(2,1)} %get-tuple-element.1131), channel_id=1, source_target_pairs={{8,0},{16,8},{24,16},{9,1},{17,9},{25,17},{10,2},{18,10},{26,18},{... | collective-permute-start | bytes 1572872 | tf_op jit(solution)/shard_map/ppermute | solution.py:586
  491.6 2.7 copy-start.7
  508.2 6.3 copy-start.84
  508.3 6.3 copy-start.93
  526.8 11.4 %collective-permute-start.16 = (bf16[256,1024]{1,0:T(8,128)(2,1)}, bf16[256,1024]{1,0:T(8,128)(2,1)}, u32[]{:S(2)}, u32[]{:S(2)}) collective-permute-start(bf16[256,1024]{1,0:T(8,128)(2,1)} %get-tuple-element.1135), channel_id=1, source_target_pairs={{8,0},{16,8},{24,16},{9,1},{17,9},{25,17},{10,2},{18,10},{26,18},{... | collective-permute-start | bytes 1572872 | tf_op jit(solution)/shard_map/ppermute | solution.py:586
  538.1 4.8 copy-start.8
  538.2 4.8 copy-start.90
  540.4 2.6 copy-start.83
  551.2 4.8 copy-start.95
  557.2 6.4 copy-start.37
  571.8 6.8 copy-start.16
  583.2 6.1 copy-start.67
  615.3 181.2 %reduce-scatter.3.cloned.1.call-start = ((), (), s32[]{:S(2)}) async-start(), calls=%async_computation.2 | async-start | bytes 12681216 | tf_op jit(solution)/shard_map/reduce_scatter | solution.py:618
  618.2 4.8 collective-permute-start.7
  621.7 7.8 collective-permute-start.17
  622.9 4.9 copy-start.60
  625.1 17.5 %collective-permute-start.10 = (bf16[2,512,256]{2,1,0:T(8,128)(2,1)S(1)}, bf16[2,512,256]{2,1,0:T(8,128)(2,1)S(1)}, u32[]{:S(2)}, u32[]{:S(2)}) collective-permute-start(bf16[2,512,256]{2,1,0:T(8,128)(2,1)S(1)} %get-tuple-element.2240), channel_id=1, source_target_pairs={{24,0},{25,1},{26,2},{27,3},{28,4},{29,5},{30,6},{31,7}} | collective-permute-start | bytes 1572872 | tf_op jit(solution)/shard_map/ppermute | solution.py:629
  626.4 18.4 %collective-permute-start.9 = (bf16[2,512,256]{2,1,0:T(8,128)(2,1)S(1)}, bf16[2,512,256]{2,1,0:T(8,128)(2,1)S(1)}, u32[]{:S(2)}, u32[]{:S(2)}) collective-permute-start(bf16[2,512,256]{2,1,0:T(8,128)(2,1)S(1)} %get-tuple-element.2241), channel_id=1, source_target_pairs={{24,8},{25,9},{26,10},{27,11},{28,12},{29,13},{30,14},{31,15}} | collective-permute-start | bytes 1572872 | tf_op jit(solution)/shard_map/ppermute | solution.py:629
  627.1 17.8 %collective-permute-start.8 = (bf16[2,512,256]{2,1,0:T(8,128)(2,1)S(1)}, bf16[2,512,256]{2,1,0:T(8,128)(2,1)S(1)}, u32[]{:S(2)}, u32[]{:S(2)}) collective-permute-start(bf16[2,512,256]{2,1,0:T(8,128)(2,1)S(1)} %get-tuple-element.2242), channel_id=1, source_target_pairs={{24,16},{25,17},{26,18},{27,19},{28,20},{29,21},{30,22},{31,23}} | collective-permute-start | bytes 1572872 | tf_op jit(solution)/shard_map/ppermute | solution.py:629
  631.4 14.4 %copy-start.97 = (f32[1024]{0:T(1024)S(1)}, f32[1024]{0:T(1024)}, u32[]{:S(2)}) copy-start(f32[1024]{0:T(1024)} %copy-done.96) | copy-start | bytes 12292
  631.4 14.4 %copy-start.99 = (f32[1024]{0:T(1024)S(1)}, f32[1024]{0:T(1024)}, u32[]{:S(2)}) copy-start(f32[1024]{0:T(1024)} %copy-done.98) | copy-start | bytes 12292
  631.4 14.3 %copy-start.101 = (f32[1024]{0:T(1024)S(1)}, f32[1024]{0:T(1024)}, u32[]{:S(2)}) copy-start(f32[1024]{0:T(1024)} %copy-done.100) | copy-start | bytes 12292
  631.4 14.3 %copy-start.102 = (f32[1024]{0:T(1024)S(1)}, f32[1024]{0:T(1024)}, u32[]{:S(2)}) copy-start(f32[1024]{0:T(1024)} %get-tuple-element.1163) | copy-start | bytes 12292
  631.4 14.3 %copy-start.104 = (f32[1024]{0:T(1024)S(1)}, f32[1024]{0:T(1024)}, u32[]{:S(2)}) copy-start(f32[1024]{0:T(1024)} %copy-done.103) | copy-start | bytes 12292
  631.5 14.3 %copy-start.106 = (f32[1024]{0:T(1024)S(1)}, f32[1024]{0:T(1024)}, u32[]{:S(2)}) copy-start(f32[1024]{0:T(1024)} %copy-done.105) | copy-start | bytes 12292
  632.7 30.9 %collective-permute-start.20 = (bf16[2,512,256]{2,1,0:T(8,128)(2,1)}, bf16[2,512,256]{2,1,0:T(8,128)(2,1)S(1)}, u32[]{:S(2)}, u32[]{:S(2)}) collective-permute-start(bf16[2,512,256]{2,1,0:T(8,128)(2,1)} %get-tuple-element.2233), channel_id=1, source_target_pairs={{0,8},{1,9},{2,10},{3,11},{4,12},{5,13},{6,14},{7,15}} | collective-permute-start | bytes 1572872 | tf_op jit(solution)/shard_map/ppermute | solution.py:629
  634.0 29.6 %collective-permute-start.19 = (bf16[2,512,256]{2,1,0:T(8,128)(2,1)}, bf16[2,512,256]{2,1,0:T(8,128)(2,1)S(1)}, u32[]{:S(2)}, u32[]{:S(2)}) collective-permute-start(bf16[2,512,256]{2,1,0:T(8,128)(2,1)} %get-tuple-element.2234), channel_id=1, source_target_pairs={{0,16},{1,17},{2,18},{3,19},{4,20},{5,21},{6,22},{7,23}} | collective-permute-start | bytes 1572872 | tf_op jit(solution)/shard_map/ppermute | solution.py:629
  642.6 21.0 %collective-permute-start.18 = (bf16[2,512,256]{2,1,0:T(8,128)(2,1)}, bf16[2,512,256]{2,1,0:T(8,128)(2,1)}, u32[]{:S(2)}, u32[]{:S(2)}) collective-permute-start(bf16[2,512,256]{2,1,0:T(8,128)(2,1)} %get-tuple-element.2235), channel_id=1, source_target_pairs={{0,24},{1,25},{2,26},{3,27},{4,28},{5,29},{6,30},{7,31}} | collective-permute-start | bytes 1572872 | tf_op jit(solution)/shard_map/ppermute | solution.py:629
  663.6 135.9 %copy-start.1 = (s32[2,4]{1,0:T(2,128)S(1)}, s32[2,4]{1,0:T(2,128)}, u32[]{:S(2)}) copy-start(s32[2,4]{1,0:T(2,128)} %param.70) | copy-start | bytes 100
  (22 other events, 24.0 us)
Sparse Core Ops, SparseCore 0:
  615.4 63.3 reduce-scatter.4
  681.2 115.1 reduce-scatter.2

commit v2 on v1

v2 whole, which is shorter than its diff:
```python
import functools

import jax
import jax.numpy as jnp
from jax import lax
from jax.experimental import pallas as pl
from jax.experimental.pallas import tpu as pltpu
from jax.sharding import PartitionSpec as P

HEADS = 16
FEAT_DIM = 16
WINDOW = 64
CHUNKS = 4
LAG = 2
TILE = 256
PAIRS = HEADS // 2
epsilon = 1e-06

F32 = jnp.float32
BF16 = jnp.bfloat16


def nn(a, b):
    return jnp.dot(a, b, preferred_element_type=F32)


def nt(a, b):
    return lax.dot_general(a, b, (((1,), (1,)), ((), ())), preferred_element_type=F32)


def tn(a, b):
    return lax.dot_general(a, b, (((0,), (0,)), ((), ())), preferred_element_type=F32)


def lanes(rows, width):
    return lax.broadcasted_iota(jnp.int32, (rows, width), 1)


def call(kernel, grid, in_specs, out_specs, out_shape, scratch, flops):
    return pl.pallas_call(
        kernel,
        grid=grid,
        in_specs=in_specs,
        out_specs=out_specs,
        out_shape=out_shape,
        scratch_shapes=scratch,
        compiler_params=pltpu.CompilerParams(
            vmem_limit_bytes=40 * 1024 * 1024, dimension_semantics=("arbitrary",)
        ),
        cost_estimate=pl.CostEstimate(flops=flops, bytes_accessed=flops // 512, transcendentals=0),
    )


def whole(shape):
    return pl.BlockSpec(shape, lambda p: (0,) * len(shape))


def columns(rows, start=0, row=0):
    return pl.BlockSpec((rows, 128), lambda p: (row, start + p))


def taylor_mask(doc_t, doc_s, j, m, t_axis):
    same = doc_t == doc_s
    if j == m:
        t = lax.broadcasted_iota(jnp.int32, same.shape, t_axis)
        s = lax.broadcasted_iota(jnp.int32, same.shape, 1 - t_axis)
        same = same & (s <= t)
    return jnp.where(same, 1.0, 0.0).astype(F32)


def taylor_forward_kernel(m, size, *refs):
    docc, docr, q_ref = refs[:3]
    ks, vs = refs[3 : 4 + m], refs[4 + m : 5 + 2 * m]
    mix_ref, den_ref, mask = refs[5 + 2 * m :]
    pair = pl.program_id(0)

    @pl.when(pair == 0)
    def _():
        for j in range(m + 1):
            mask[j] = taylor_mask(
                docc[m * size : (m + 1) * size, :], docr[:, j * size : (j + 1) * size], j, m, 0
            )
        den_ref[...] = jnp.zeros_like(den_ref)

    q = q_ref[...]
    wide = lanes(size, 2 * 128) // FEAT_DIM
    lane = lanes(size, 128)
    ratios = []
    dens = den_ref[...]
    for i in range(2):
        head = 2 * pair + i
        q_head = jnp.where(wide == head, q * jnp.asarray(0.25, BF16), jnp.zeros_like(q))
        numer = jnp.zeros((size, 128), F32)
        denom = jnp.zeros((size, 1), F32)
        for j in range(m + 1):
            a = nt(q_head, ks[j][...])
            w = (1.0 + a * (1.0 + 0.5 * a)) * mask[j]
            denom += jnp.sum(w, axis=1, keepdims=True)
            numer += nn(w.astype(BF16), vs[j][...])
        ratios.append(numer / denom)
        dens = jnp.where(lane == head, denom, dens)
    den_ref[...] = dens
    mix_ref[...] = jnp.where(lane < 64, ratios[0], ratios[1]).astype(BF16)


def taylor_forward(m, docs, kept):
    size = kept[0].shape[0]
    docc, docr = docs
    return call(
        functools.partial(taylor_forward_kernel, m, size),
        (PAIRS,),
        [whole(docc.shape), whole(docr.shape), whole((size, 256))]
        + [pl.BlockSpec((size, 256), lambda p: (0, 1))] * (m + 1)
        + [columns(size, 4)] * (m + 1),
        [columns(size), whole((size, 128))],
        [
            jax.ShapeDtypeStruct((size, HEADS * 64), BF16),
            jax.ShapeDtypeStruct((size, 128), F32),
        ],
        [pltpu.VMEM((m + 1, size, size), F32)],
        2 * HEADS * (m + 1) * size * size * 512,
    )(docc, docr, kept[m], *kept, *kept)


def taylor_backward_kernel(m, size, later, *refs):
    docc, docr, q_ref = refs[:3]
    refs = refs[3:]
    ks, vs = refs[: m + 1], refs[m + 1 : 2 * m + 2]
    dmix_ref, mix_ref, den_ref = refs[2 * m + 2 : 2 * m + 5]
    refs = refs[2 * m + 5 :]
    if later:
        dk_in, dv_in = refs[:2]
        refs = refs[2:]
    dq_ref, dk_ref, dv_ref, mask, k_turned, dq_turned = refs
    pair = pl.program_id(0)

    @pl.when(pair == 0)
    def _():
        for j in range(m + 1):
            mask[j] = taylor_mask(
                docr[:, m * size : (m + 1) * size], docc[j * size : (j + 1) * size, :], j, m, 1
            )
            k_turned[j] = (ks[j][...].astype(F32) * 0.25).T.astype(BF16)
        dk_ref[...] = jnp.zeros_like(dk_ref)
        if later:
            dk_ref[: m * size, :] = dk_in[...]

    q = q_ref[...]
    wide = lanes(size, 2 * 128) // FEAT_DIM
    lane = lanes(size, 128)
    dm = dmix_ref[...].astype(F32)
    both = dm * mix_ref[...].astype(F32)
    den = den_ref[...]
    for i in range(2):
        head = 2 * pair + i
        inside = lane // 64 == i
        spare = 64 * (1 - i)
        turn = 1.0 / jnp.sum(jnp.where(lane == head, den, 0.0), axis=1, keepdims=True)
        dden = -jnp.sum(jnp.where(inside, both, 0.0), axis=1, keepdims=True) * turn
        dden_high = dden.astype(BF16).astype(F32)
        dnum = jnp.where(inside, dm * turn, 0.0)
        dnum_low = dnum.astype(BF16)
        dnum_more = jnp.where(
            lane == spare, dden_high, jnp.where(lane == spare + 1, dden - dden_high, dnum)
        ).astype(BF16)
        q_head = jnp.where(wide == head, q * jnp.asarray(0.25, BF16), jnp.zeros_like(q))
        own = pl.ds(pl.multiple_of(head * FEAT_DIM, FEAT_DIM), FEAT_DIM)
        dq_head = jnp.zeros((FEAT_DIM, size), F32)
        for j in range(m + 1):
            rows = pl.ds(j * size, size)
            v = vs[j][...]
            v_more = jnp.where(
                inside,
                v,
                jnp.where((lane == spare) | (lane == spare + 1), jnp.ones_like(v), jnp.zeros_like(v)),
            )
            a = nt(ks[j][...], q_head)
            w = (1.0 + a * (1.0 + 0.5 * a)) * mask[j]
            dw = nt(v_more, dnum_more)
            da = (dw * (1.0 + a) * mask[j]).astype(BF16)
            dv = nn(w.astype(BF16), dnum_low)
            if i == 0:
                dv_ref[rows, :] = dv_in[rows, :] + dv if later and j < m else dv
            else:
                dv_ref[rows, :] += dv
            dk_ref[rows, :] += nn(da, q_head)
            dq_head += nn(k_turned[j, own, :], da)
        dq_turned[own, :] = dq_head

    @pl.when(pair == PAIRS - 1)
    def _():
        dq_ref[...] = dq_turned[...].T


def taylor_backward(m, docs, kept, dmix, mix, den, later):
    size = kept[0].shape[0]
    docc, docr = docs
    rows = (m + 1) * size
    return call(
        functools.partial(taylor_backward_kernel, m, size, later is not None),
        (PAIRS,),
        [whole(docc.shape), whole(docr.shape), whole((size, 256))]
        + [pl.BlockSpec((size, 256), lambda p: (0, 1))] * (m + 1)
        + [columns(size, 4)] * (m + 1)
        + [columns(size), columns(size), whole((size, 128))]
        + ([whole((m * size, 256)), columns(m * size)] if later is not None else []),
        [whole((size, 256)), whole((rows, 256)), columns(rows)],
        [
            jax.ShapeDtypeStruct((size, 256), F32),
            jax.ShapeDtypeStruct((rows, 256), F32),
            jax.ShapeDtypeStruct((rows, HEADS * 64), F32),
        ],
        [
            pltpu.VMEM((m + 1, size, size), F32),
            pltpu.VMEM((m + 1, 256, size), BF16),
            pltpu.VMEM((256, size), F32),
        ],
        5 * HEADS * (m + 1) * size * size * 512,
    )(docc, docr, kept[m], *kept, *kept, dmix, mix, den, *(later or ()))


STEP = 128


def part(pair, start):
    return pl.ds(pl.multiple_of(start + pair * 128, 128), 128)


def window_spans(m, size):
    lead = STEP if m > 0 else 0
    for b in range(size // STEP):
        first = max(b * STEP + lead - STEP, 0)
        yield b * STEP, first, b * STEP + lead + STEP - first, lead


def window_mask(doc_t, doc_s, lead_rows, t_axis):
    t = lax.broadcasted_iota(jnp.int32, (doc_t == doc_s).shape, t_axis)
    s = lax.broadcasted_iota(jnp.int32, (doc_t == doc_s).shape, 1 - t_axis)
    distance = t + lead_rows - s
    return (distance >= 0) & (distance < WINDOW) & (doc_t == doc_s)


def joined(before, own):
    return jnp.concatenate([before[...], own[...]], axis=0) if before is not None else own[...]


def window_forward_kernel(m, size, *refs):
    docc, docr, q_ref, k_ref, v_ref = refs[:5]
    before_k, before_v = refs[5:7] if m > 0 else (None, None)
    mix_ref = refs[-1]
    k_all, v_all = joined(before_k, k_ref), joined(before_v, v_ref)
    lane = lanes(STEP, 128)
    for row, first, count, lead in window_spans(m, size):
        at = m * size - lead + first
        q = q_ref[row : row + STEP, :]
        k, v = k_all[first : first + count], v_all[first : first + count]
        mask = window_mask(
            docc[m * size + row : m * size + row + STEP, :],
            docr[:, at : at + count],
            row + lead - first,
            0,
        )
        mixes = []
        for i in range(2):
            q_head = jnp.where(lane // 64 == i, q * jnp.asarray(0.125, BF16), jnp.zeros_like(q))
            a = jnp.where(mask, nt(q_head, k), -1e30)
            p = jnp.exp(a - jnp.max(a, axis=1, keepdims=True))
            p = p * (1.0 / jnp.sum(p, axis=1, keepdims=True))
            mixes.append(nn(p.astype(BF16), v))
        mix_ref[row : row + STEP, :] = jnp.where(lane < 64, mixes[0], mixes[1]).astype(BF16)


def window_sources(m, size, kept, kept_before):
    last = size // STEP - 1
    specs = [columns(size), columns(size, 8), columns(size, 16)]
    arrays = [kept] * 3
    if m > 0:
        specs += [columns(STEP, 8, last), columns(STEP, 16, last)]
        arrays += [kept_before] * 2
    return specs, arrays


def window_forward(m, docs, kept, kept_before):
    size = kept.shape[0]
    docc, docr = docs
    specs, arrays = window_sources(m, size, kept, kept_before)
    return call(
        functools.partial(window_forward_kernel, m, size),
        (PAIRS,),
        [whole(docc.shape), whole(docr.shape)] + specs,
        columns(size),
        jax.ShapeDtypeStruct((size, HEADS * 64), BF16),
        [],
        2 * HEADS * size * 256 * 512,
    )(docc, docr, *arrays)


def window_backward_kernel(m, size, later, *refs):
    docc, docr, q_ref, k_ref, v_ref = refs[:5]
    refs = refs[5:]
    before_k, before_v = None, None
    if m > 0:
        before_k, before_v = refs[:2]
        refs = refs[2:]
    dmix_ref = refs[0]
    refs = refs[1:]
    if later:
        dk_in, dv_in = refs[:2]
        refs = refs[2:]
    grad_ref = refs[0]
    refs = refs[1:]
    pair = pl.program_id(0)
    width = HEADS * 64
    if m > 0:
        dk_out, dv_out = refs[:2]
        refs = refs[2:]
    dk_sum, dv_sum = refs
    lead = STEP if m > 0 else 0
    rows = size + lead
    dk_sum[...] = jnp.zeros_like(dk_sum)
    dv_sum[...] = jnp.zeros_like(dv_sum)
    if later:
        dk_sum[rows - STEP : rows, :] = dk_in[...]
        dv_sum[rows - STEP : rows, :] = dv_in[...]
    k_all, v_all = joined(before_k, k_ref), joined(before_v, v_ref)
    lane = lanes(STEP, 128)
    for row, first, count, _ in window_spans(m, size):
        at = m * size - lead + first
        q, dm = q_ref[row : row + STEP, :], dmix_ref[row : row + STEP, :]
        k, v = k_all[first : first + count], v_all[first : first + count]
        mask = window_mask(
            docr[:, m * size + row : m * size + row + STEP],
            docc[at : at + count, :],
            row + lead - first,
            1,
        )
        dq = jnp.zeros((STEP, 128), F32)
        dk = jnp.zeros((count, 128), F32)
        dv = jnp.zeros((count, 128), F32)
        for i in range(2):
            inside = lane // 64 == i
            q_head = jnp.where(inside, q * jnp.asarray(0.125, BF16), jnp.zeros_like(q))
            dm_head = jnp.where(inside, dm, jnp.zeros_like(dm))
            k_head = jnp.where(
                lanes(count, 128) // 64 == i, k * jnp.asarray(0.125, BF16), jnp.zeros_like(k)
            )
            a = jnp.where(mask, nt(k, q_head), -1e30)
            p = jnp.exp(a - jnp.max(a, axis=0, keepdims=True))
            p = p * (1.0 / jnp.sum(p, axis=0, keepdims=True))
            dp = nt(v, dm_head)
            da = (p * (dp - jnp.sum(p * dp, axis=0, keepdims=True))).astype(BF16)
            dk += nn(da, q_head)
            dv += nn(p.astype(BF16), dm_head)
            dq += tn(da, k_head)
        grad_ref[row : row + STEP, part(pair, 0)] = dq.astype(BF16)
        dk_sum[first : first + count, :] += dk
        dv_sum[first : first + count, :] += dv
    grad_ref[:, part(pair, width)] = dk_sum[lead:rows, :].astype(BF16)
    grad_ref[:, part(pair, 2 * width)] = dv_sum[lead:rows, :].astype(BF16)
    if m > 0:
        dk_out[...] = dk_sum[:STEP, :]
        dv_out[...] = dv_sum[:STEP, :]


def window_backward(m, docs, kept, kept_before, dmix, later):
    size = kept.shape[0]
    docc, docr = docs
    specs, arrays = window_sources(m, size, kept, kept_before)
    rows = size + (STEP if m > 0 else 0)
    low = jax.ShapeDtypeStruct((size, 3 * HEADS * 64), BF16)
    edge = jax.ShapeDtypeStruct((STEP, HEADS * 64), F32)
    return call(
        functools.partial(window_backward_kernel, m, size, later is not None),
        (PAIRS,),
        [whole(docc.shape), whole(docr.shape)]
        + specs
        + [columns(size)]
        + ([columns(STEP)] * 2 if later is not None else []),
        [whole((size, 3 * HEADS * 64))] + ([columns(STEP)] * 2 if m > 0 else []),
        [low] + ([edge] * 2 if m > 0 else []),
        [pltpu.VMEM((rows, 128), F32), pltpu.VMEM((rows, 128), F32)],
        5 * HEADS * size * 256 * 512,
    )(docc, docr, *arrays, dmix, *(later or ()))


def blank(shapes):
    return pl.pallas_call(
        lambda *refs: None,
        out_specs=[pl.BlockSpec(memory_space=pl.ANY)] * len(shapes),
        out_shape=[jax.ShapeDtypeStruct(*shape) for shape in shapes],
    )()


def rms_inverse(inputs):
    return lax.rsqrt(jnp.mean(inputs * inputs, axis=-1, keepdims=True) + epsilon)


def rms_forward(inputs, gain_row):
    return (inputs * rms_inverse(inputs) * gain_row).astype(BF16)


def rms_backward(inputs, gain_row, grad_normed):
    inverse = rms_inverse(inputs)
    scaled = grad_normed * gain_row
    grad_inputs = inverse * scaled - inputs * inverse**3 * jnp.mean(
        scaled * inputs, axis=-1, keepdims=True
    )
    grad_gain = jnp.sum(grad_normed * inputs * inverse, axis=0, keepdims=True)
    return grad_inputs, grad_gain


def spans(width):
    part = width // 2 if width % 256 == 0 else width
    return [(start, part) for start in range(0, width, part)]


def begin(sems, copies):
    made = [pltpu.make_async_copy(a, b, sems.at[i]) for i, (a, b) in enumerate(copies)]
    for copy in made:
        copy.start()
    return made


def finish(copies):
    for copy in copies:
        copy.wait()


def dense_forward_kernel(
    x_ref, gain_ref, wg_ref, wu_ref, wo_ref, out_ref, gate_ref, up_ref, wg, wu, wo, gates, ups, sems, done
):
    tiles = spans(gates.shape[1])
    reads = []
    for n, (at, w) in enumerate(tiles):
        cut = pl.ds(at, w)
        reads.append(
            begin(
                sems.at[n],
                [
                    (wg_ref.at[:, cut], wg.at[:, cut]),
                    (wu_ref.at[:, cut], wu.at[:, cut]),
                    (wo_ref.at[cut, :], wo.at[cut, :]),
                ],
            )
        )
    inputs = x_ref[...].astype(F32)
    normed = rms_forward(inputs, gain_ref[...])
    total = inputs
    writes = []
    for n, (at, w) in enumerate(tiles):
        cut = pl.ds(at, w)
        reads[n][0].wait()
        gate = nn(normed, wg[:, cut])
        reads[n][1].wait()
        up = nn(normed, wu[:, cut])
        gates[:, cut] = gate.astype(BF16)
        ups[:, cut] = up.astype(BF16)
        writes += begin(
            done.at[n], [(gates.at[:, cut], gate_ref.at[:, cut]), (ups.at[:, cut], up_ref.at[:, cut])]
        )
        hidden = (gate * jax.nn.sigmoid(gate) * up).astype(BF16)
        reads[n][2].wait()
        total = total + nn(hidden, wo[cut, :])
    out_ref[...] = total.astype(BF16)
    finish(writes)


IN_VMEM = pl.BlockSpec(memory_space=pltpu.VMEM)
IN_PLACE = pl.BlockSpec(memory_space=pl.ANY)


def plain_call(kernel, in_specs, out_specs, out_shape, scratch, flops):
    return pl.pallas_call(
        kernel,
        in_specs=in_specs,
        out_specs=out_specs,
        out_shape=out_shape,
        scratch_shapes=scratch,
        compiler_params=pltpu.CompilerParams(vmem_limit_bytes=48 * 1024 * 1024),
        cost_estimate=pl.CostEstimate(flops=flops, bytes_accessed=flops // 512, transcendentals=0),
    )


def weight_scratch(width, padded):
    return [pltpu.VMEM((width, padded), BF16)] * 2 + [pltpu.VMEM((padded, width), BF16)]


def dense_forward(x, gain, weights):
    size, width = x.shape
    padded = weights[0].shape[1]
    tiles = len(spans(padded))
    return plain_call(
        dense_forward_kernel,
        [IN_VMEM, IN_VMEM] + [IN_PLACE] * 3,
        [IN_VMEM, IN_PLACE, IN_PLACE],
        [jax.ShapeDtypeStruct((size, width), BF16)]
        + [jax.ShapeDtypeStruct((size, padded), BF16)] * 2,
        weight_scratch(width, padded)
        + [pltpu.VMEM((size, padded), BF16)] * 2
        + [pltpu.SemaphoreType.DMA((tiles, 3)), pltpu.SemaphoreType.DMA((tiles, 2))],
        6 * size * width * padded,
    )(x, gain, *weights)


def dense_backward_kernel(
    x_ref,
    gain_ref,
    g_ref,
    gate_ref,
    up_ref,
    wg_ref,
    wu_ref,
    wo_ref,
    out_ref,
    dgate_ref,
    dup_ref,
    hidden_ref,
    dgain_ref,
    wg,
    wu,
    wo,
    gates,
    ups,
    dgates,
    dups,
    hiddens,
    sems,
    done,
):
    tiles = spans(gates.shape[1])
    reads = []
    for n, (at, w) in enumerate(tiles):
        cut = pl.ds(at, w)
        reads.append(
            begin(
                sems.at[n],
                [
                    (wo_ref.at[cut, :], wo.at[cut, :]),
                    (gate_ref.at[:, cut], gates.at[:, cut]),
                    (up_ref.at[:, cut], ups.at[:, cut]),
                    (wg_ref.at[:, cut], wg.at[:, cut]),
                    (wu_ref.at[:, cut], wu.at[:, cut]),
                ],
            )
        )
    g = g_ref[...]
    total = jnp.zeros(g.shape, F32)
    writes = []
    for n, (at, w) in enumerate(tiles):
        cut = pl.ds(at, w)
        finish(reads[n][:3])
        dh = nt(g, wo[cut, :])
        gate = gates[:, cut].astype(F32)
        up = ups[:, cut].astype(F32)
        sg = jax.nn.sigmoid(gate)
        active = gate * sg
        hiddens[:, cut] = (active * up).astype(BF16)
        dgate = (dh * up * (sg + active * (1.0 - sg))).astype(BF16)
        dup = (dh * active).astype(BF16)
        dgates[:, cut] = dgate
        dups[:, cut] = dup
        writes += begin(
            done.at[n],
            [
                (hiddens.at[:, cut], hidden_ref.at[:, cut]),
                (dgates.at[:, cut], dgate_ref.at[:, cut]),
                (dups.at[:, cut], dup_ref.at[:, cut]),
            ],
        )
        finish(reads[n][3:])
        total = total + nt(dgate, wg[:, cut]) + nt(dup, wu[:, cut])
    grad, dgain = rms_backward(x_ref[...].astype(F32), gain_ref[...], total)
    out_ref[...] = (g.astype(F32) + grad).astype(BF16)
    dgain_ref[...] = dgain
    finish(writes)


def dense_backward(x, gain, g, gate, up, weights):
    size, width = x.shape
    padded = weights[0].shape[1]
    tiles = len(spans(padded))
    return plain_call(
        dense_backward_kernel,
        [IN_VMEM] * 3 + [IN_PLACE] * 5,
        [IN_VMEM] + [IN_PLACE] * 3 + [IN_VMEM],
        [jax.ShapeDtypeStruct((size, width), BF16)]
        + [jax.ShapeDtypeStruct((size, padded), BF16)] * 3
        + [jax.ShapeDtypeStruct((1, width), F32)],
        weight_scratch(width, padded)
        + [pltpu.VMEM((size, padded), BF16)] * 5
        + [pltpu.SemaphoreType.DMA((tiles, 5)), pltpu.SemaphoreType.DMA((tiles, 3))],
        6 * size * width * padded,
    )(x, gain, g, gate, up, *weights)


def dense_both_kernel(
    x_ref,
    gain_ref,
    g_ref,
    wg_ref,
    wu_ref,
    wo_ref,
    final_ref,
    out_ref,
    dgate_ref,
    dup_ref,
    hidden_ref,
    dgain_ref,
    wg,
    wu,
    wo,
    dgates,
    dups,
    hiddens,
    sems,
    done,
):
    tiles = spans(dgates.shape[1])
    reads = []
    for n, (at, w) in enumerate(tiles):
        cut = pl.ds(at, w)
        reads.append(
            begin(
                sems.at[n],
                [
                    (wg_ref.at[:, cut], wg.at[:, cut]),
                    (wu_ref.at[:, cut], wu.at[:, cut]),
                    (wo_ref.at[cut, :], wo.at[cut, :]),
                ],
            )
        )
    inputs = x_ref[...].astype(F32)
    normed = rms_forward(inputs, gain_ref[...])
    g = g_ref[...]
    final = inputs
    total = jnp.zeros(g.shape, F32)
    writes = []
    for n, (at, w) in enumerate(tiles):
        cut = pl.ds(at, w)
        reads[n][0].wait()
        gate = nn(normed, wg[:, cut])
        reads[n][1].wait()
        up = nn(normed, wu[:, cut])
        sg = jax.nn.sigmoid(gate)
        active = gate * sg
        hidden = (active * up).astype(BF16)
        hiddens[:, cut] = hidden
        reads[n][2].wait()
        final = final + nn(hidden, wo[cut, :])
        dh = nt(g, wo[cut, :])
        dgate = (dh * up * (sg + active * (1.0 - sg))).astype(BF16)
        dup = (dh * active).astype(BF16)
        dgates[:, cut] = dgate
        dups[:, cut] = dup
        writes += begin(
            done.at[n],
            [
                (hiddens.at[:, cut], hidden_ref.at[:, cut]),
                (dgates.at[:, cut], dgate_ref.at[:, cut]),
                (dups.at[:, cut], dup_ref.at[:, cut]),
            ],
        )
        total = total + nt(dgate, wg[:, cut]) + nt(dup, wu[:, cut])
    final_ref[...] = final.astype(BF16)
    grad, dgain = rms_backward(inputs, gain_ref[...], total)
    out_ref[...] = (g.astype(F32) + grad).astype(BF16)
    dgain_ref[...] = dgain
    finish(writes)


def dense_both(x, gain, g, weights):
    size, width = x.shape
    padded = weights[0].shape[1]
    tiles = len(spans(padded))
    return plain_call(
        dense_both_kernel,
        [IN_VMEM] * 3 + [IN_PLACE] * 3,
        [IN_VMEM] * 2 + [IN_PLACE] * 3 + [IN_VMEM],
        [jax.ShapeDtypeStruct((size, width), BF16)] * 2
        + [jax.ShapeDtypeStruct((size, padded), BF16)] * 3
        + [jax.ShapeDtypeStruct((1, width), F32)],
        weight_scratch(width, padded)
        + [pltpu.VMEM((size, padded), BF16)] * 3
        + [pltpu.SemaphoreType.DMA((tiles, 3)), pltpu.SemaphoreType.DMA((tiles, 3))],
        12 * size * width * padded,
    )(x, gain, g, *weights)


def grad_in_kernel(count, tiles, gain_ref, *refs):
    xs, refs = refs[:count], refs[count:]
    groups = [refs[count * n : count * (n + 1)] for n in range(len(tiles))]
    out_ref, turned = refs[count * len(tiles) :]
    step = pl.program_id(0)
    size = xs[0].shape[0]

    @pl.when(step == 0)
    def _():
        for c in range(count):
            normed = rms_forward(xs[c][...].astype(F32), gain_ref[...])
            turned[:, c * size : (c + 1) * size] = normed.astype(F32).T.astype(BF16)

    start = 0
    for parts, (_, used) in zip(groups, tiles):

        @pl.when((step >= start) & (step < start + used))
        def _(parts=parts):
            joined = jnp.concatenate([part[...] for part in parts], axis=0)
            out_ref[...] = nn(turned[...], joined).astype(BF16)

        start += used


def grad_in(gain, xs, groups, out_width):
    count = len(xs)
    size, width = xs[0].shape
    specs = [whole((1, width))] + [whole((size, width))] * count
    arrays, begun = [], 0
    for parts, first, used in groups:

        def at(j, first=first, used=used, begun=begun):
            return (0, first + jnp.clip(j - begun, 0, used - 1))

        specs += [pl.BlockSpec((size, TILE), at)] * count
        arrays += parts
        begun += used
    return call(
        functools.partial(grad_in_kernel, count, [group[1:] for group in groups]),
        (begun,),
        specs,
        pl.BlockSpec((width, TILE), lambda j: (0, j)),
        jax.ShapeDtypeStruct((width, out_width), BF16),
        [pltpu.VMEM((width, count * size), BF16)],
        2 * count * size * width * TILE * begun,
    )(gain, *xs, *arrays)


def grad_out_kernel(count, used, *refs):
    left, right = refs[:count], refs[count : 2 * count]
    out_ref = refs[2 * count]
    step = pl.program_id(0)

    @pl.when(step < used)
    def _():
        joined = jnp.concatenate([part[...] for part in left], axis=0)
        turned = joined.astype(F32).T.astype(BF16)
        out_ref[...] = nn(turned, jnp.concatenate([part[...] for part in right], axis=0)).astype(
            BF16
        )

    @pl.when(step >= used)
    def _():
        out_ref[...] = jnp.zeros_like(out_ref)


def grad_out(left, right, used, rows):
    count = len(left)
    size, width = right[0].shape
    tiles = -(-rows // TILE)
    return call(
        functools.partial(grad_out_kernel, count, used),
        (tiles,),
        [pl.BlockSpec((size, TILE), lambda j: (0, jnp.minimum(j, used - 1)))] * count
        + [whole((size, width))] * count,
        pl.BlockSpec((TILE, width), lambda j: (j, 0)),
        jax.ShapeDtypeStruct((rows, width), BF16),
        [],
        2 * count * size * width * TILE * used,
    )(*left, *right)


def local(tokens, section_in, section_out, gains, bounds, cotangent):
    section = lax.axis_index("section")
    seq = lax.axis_index("seq")
    sections = lax.axis_size("section")
    pack_in = section_in[0]
    pack_out = section_out[0]
    gain_row = gains
    _, block, width = tokens.shape
    hidden_dim = pack_out.shape[0]
    padded = -(-hidden_dim // TILE) * TILE
    length = 2 * block
    size = length // CHUNKS
    taylor_cols = 2 * HEADS * FEAT_DIM + width
    window_cols = 3 * width
    last = sections - 1

    def swapped(two):
        away = lax.dynamic_index_in_dim(two, 1 - seq, 0, keepdims=False)
        own = lax.dynamic_index_in_dim(two, seq, 0, keepdims=False)
        came = lax.ppermute(away, "seq", [(0, 1), (1, 0)])
        return jnp.where(seq == 0, jnp.stack([own, came]), jnp.stack([came, own]))

    def branches(shapes, makers):
        names = list(shapes)

        def branch(maker):
            def run():
                made = maker() if maker is not None else {}
                missing = [name for name in names if name not in made]
                empty = dict(zip(missing, blank([shapes[name] for name in missing]))) if missing else {}
                return tuple(made[name] if name in made else empty[name] for name in names)

            return run

        values = lax.switch(section, [branch(maker) for maker in makers])
        return dict(zip(names, values))

    starts = lax.dynamic_index_in_dim(bounds, seq, 0, keepdims=False)
    positions = jnp.arange(length, dtype=jnp.int32)
    docs = jnp.sum((starts[None, :] <= positions[:, None]).astype(jnp.int32), axis=1)
    docs = (docs[:, None], docs[None, :])

    feed = swapped(jnp.where(section == 0, tokens, cotangent)).reshape(length, width)

    def fed(m):
        return feed[m * size : (m + 1) * size]

    first_back = (last + 1) * LAG
    pair_turn = first_back + CHUNKS - 1
    turns = pair_turn + LAG + 1
    low = ((size, width), BF16)
    wide = ((size, padded), BF16)
    edge = ((STEP, width), F32)
    gain_shape = ((1, width), F32)
    made, sent = [], []
    back_one, back_two = {}, {}

    def prepare():
        more = padded - hidden_dim
        return {
            "wg": jnp.pad(pack_in[:, :hidden_dim], ((0, 0), (0, more))),
            "wu": jnp.pad(pack_in[:, hidden_dim:], ((0, 0), (0, more))),
            "wo": jnp.pad(pack_out, ((0, more), (0, 0))),
        }

    def entry(s, m):
        return fed(m) if s == 0 else sent[m + LAG * (s - 1)]["out"]

    def upstream(s, m):
        if s == last:
            return fed(m)
        if s == 2:
            return sent[m + LAG * last]["out"]
        turn = first_back + 1 + LAG * (1 - s) + m
        if m < CHUNKS - 1:
            return sent[turn]["out"]
        return sent[turn - 1]["out2"]

    def taylor_turn(m):
        def run():
            inputs = entry(0, m).astype(F32)
            projected = nn(rms_forward(inputs, gain_row), pack_in[:, :taylor_cols]).astype(BF16)
            mix, den = taylor_forward(m, docs, [made[i]["linear"] for i in range(m)] + [projected])
            output = (inputs + nn(mix, pack_out[:width])).astype(BF16)
            return {"out": output, "linear": projected, "mix": mix, "den": den}

        return run

    def dense_turn(m):
        def run():
            out, gate, up = dense_forward(entry(1, m), gain_row, weights)
            return {"out": out, "gate": gate, "up": up}

        return run

    def window_turn(m):
        def run():
            inputs = entry(2, m).astype(F32)
            projected = nn(rms_forward(inputs, gain_row), pack_in[:, :window_cols]).astype(BF16)
            before = made[2 * LAG + m - 1]["window"] if m > 0 else None
            mix = window_forward(m, docs, projected, before)
            output = (inputs + nn(mix, pack_out[:width])).astype(BF16)
            return {"out": output, "window": projected, "mix": mix}

        return run

    def dense_both_turn(m):
        def run():
            final, out, dgate, dup, hidden, gain = dense_both(
                entry(3, m), gain_row, upstream(3, m), weights
            )
            return {
                "final": final,
                "out": out,
                "dgate": dgate,
                "dup": dup,
                "hidden": hidden,
                "gain": gain,
            }

        return run

    def window_back(m):
        def settled(m, grad, edges):
            if edges is not None:
                more = jnp.concatenate(edges, axis=1)
                tail = grad[size - STEP :, width:].astype(F32) + more
                grad = lax.dynamic_update_slice(grad, tail.astype(BF16), (size - STEP, width))
            grad_inputs, gain = rms_backward(
                entry(2, m).astype(F32), gain_row, nt(grad, pack_in[:, :window_cols])
            )
            return (upstream(2, m).astype(F32) + grad_inputs).astype(BF16), grad, gain

        def run():
            kept = made[2 * LAG + m]["window"]
            before = made[2 * LAG + m - 1]["window"] if m > 0 else None
            dmix = nt(upstream(2, m), pack_out[:width]).astype(BF16)
            results = window_backward(m, docs, kept, before, dmix, None)
            if m == 0:
                return {"part": results[0]}
            out, done, gain = settled(m - 1, made[first_back + m - 1]["part"], results[1:])
            values = {"out": out, "done": done, "gain": gain}
            if m < CHUNKS - 1:
                values["part"] = results[0]
            else:
                out, done, more = settled(m, results[0], None)
                values.update(out2=out, done2=done, gain=gain + more)
            return values

        return run

    def dense_back(ms):
        def run():
            values, gains_sum = {}, 0.0
            for n, m in enumerate(ms):
                kept = made[LAG + m]
                out, dgate, dup, hidden, gain = dense_backward(
                    entry(1, m), gain_row, upstream(1, m), kept["gate"], kept["up"], weights
                )
                more = "2" if n else ""
                values.update(
                    {"out" + more: out, "dgate" + more: dgate, "dup" + more: dup,
                     "hidden" + more: hidden}
                )
                gains_sum = gains_sum + gain
            values["gain"] = gains_sum
            return values

        return run

    def taylor_back(ms, earlier):
        dqs = []
        for m in ms:
            dmix = nt(upstream(0, m), pack_out[:width]).astype(BF16)
            dq, dk, dv = taylor_backward(
                m,
                docs,
                [made[i]["linear"] for i in range(m + 1)],
                dmix,
                made[m]["mix"],
                made[m]["den"],
                earlier,
            )
            earlier = (dk, dv)
            dqs.append(dq)
        return dqs, earlier

    def taylor_turn_back(m):
        def run():
            earlier = (made[-1]["dk"], made[-1]["dv"]) if m > 0 else None
            dqs, (dk, dv) = taylor_back([m], earlier)
            return {"dq": dqs[0], "dk": dk, "dv": dv}

        return run

    def spread(two, source):
        share = width // sections
        mine = two[:, :, source * share : (source + 1) * share]
        for target in range(sections):
            if target != source:
                piece = two[:, :, target * share : (target + 1) * share]
                came = lax.ppermute(piece, "section", [(source, target)])
                mine = jnp.where(section == target, came, mine)
        return mine

    taylor_shapes = {}
    for t in range(turns + 1):
        shapes, makers, pairs, pairs_two = {}, [None] * sections, [], []
        for s in range(sections):
            m = t - LAG * s
            if 0 <= m < CHUNKS:
                shapes["out"] = low
                makers[s] = (taylor_turn, dense_turn, window_turn, dense_both_turn)[s](m)
                if s == 0:
                    shapes.update(linear=((size, taylor_cols), BF16), mix=low)
                    shapes["den"] = ((size, 128), F32)
                elif s == 1:
                    shapes.update(gate=wide, up=wide)
                elif s == 2:
                    shapes.update(window=((size, window_cols), BF16), mix=low)
                else:
                    shapes.update(final=low, dgate=wide, dup=wide, hidden=wide, gain=gain_shape)
                pairs.append((s, s + 1) if s < last else (s, s - 1))
        if t == 0:
            shapes.update(
                wg=((width, padded), BF16), wu=((width, padded), BF16), wo=((padded, width), BF16)
            )
            makers[1] = makers[3] = prepare
        m = t - first_back
        if 0 <= m < CHUNKS:
            makers[2] = window_back(m)
            if m < CHUNKS - 1:
                shapes["part"] = ((size, window_cols), BF16)
            if m > 0:
                shapes.update(out=low, done=((size, window_cols), BF16), gain=gain_shape)
                pairs.append((2, 1))
            if m == CHUNKS - 1:
                shapes.update(out2=low, done2=((size, window_cols), BF16))
                pairs_two.append((2, 1))
        m = t - first_back - 1 - LAG
        if 0 <= m < CHUNKS - 1:
            ms = [m] if m < CHUNKS - 2 else [m, m + 1]
            makers[1] = dense_back(ms)
            shapes.update(out=low, dgate=wide, dup=wide, hidden=wide, gain=gain_shape)
            pairs.append((1, 0))
            if len(ms) > 1:
                shapes.update(out2=low, dgate2=wide, dup2=wide, hidden2=wide)
                pairs_two.append((1, 0))
        m = t - first_back - 1 - 2 * LAG
        if 0 <= m < CHUNKS - 2:
            makers[0] = taylor_turn_back(m)
            rows = (m + 1) * size
            taylor_shapes = {
                "dq": ((size, 256), F32),
                "dk": ((rows, 256), F32),
                "dv": ((rows, width), F32),
            }
            shapes.update(taylor_shapes)
        if t == turns:
            break
        made.append(branches(shapes, makers))
        if t == 0:
            weights = (made[0]["wg"], made[0]["wu"], made[0]["wo"])
        sent.append(
            {
                name: lax.ppermute(made[t][name], "section", which)
                for name, which in (("out", pairs), ("out2", pairs_two))
                if which
            }
        )

    def turns_of(s):
        if s == last:
            return [made[LAG * last + m] for m in range(CHUNKS)]
        if s == 2:
            return [made[first_back + 1 + m] for m in range(CHUNKS - 1)]
        return [made[first_back + 1 + LAG + m] for m in range(CHUNKS - 1)]

    def every(s, name):
        values = turns_of(s)
        found = [value[name] for value in values]
        return found + [values[-1][name + "2"]] if s != last else found

    def gains_of(s):
        return sum(value["gain"] for value in turns_of(s))

    def entries(s):
        return [entry(s, m) for m in range(CHUNKS)]

    def upstreams(s):
        return [upstream(s, m) for m in range(CHUNKS)]

    b_cols = taylor_cols
    a_cols = 2 * padded - b_cols
    half_tiles = padded // TILE
    a_shape, b_shape = ((width, a_cols), BF16), ((width, b_cols), BF16)

    def dense_first(s):
        def run():
            groups = [
                (every(s, "dgate"), 0, half_tiles),
                (every(s, "dup"), 0, a_cols // TILE - half_tiles),
            ]
            return {"a": grad_in(gain_row, entries(s), groups, a_cols)}

        return run

    def window_first():
        groups = [(every(2, "done"), 0, window_cols // TILE)]
        return {"a": grad_in(gain_row, entries(2), groups, a_cols)}

    def dense_second(s):
        def run():
            groups = [(every(s, "dup"), a_cols // TILE - half_tiles, b_cols // TILE)]
            return {
                "b": grad_in(gain_row, entries(s), groups, b_cols),
                "c": grad_out(every(s, "hidden"), upstreams(s), half_tiles, hidden_dim),
                "gain": gains_of(s),
            }

        return run

    def window_second():
        mixes = [made[2 * LAG + m]["mix"] for m in range(CHUNKS)]
        return {
            "c": grad_out(mixes, upstreams(2), width // TILE, hidden_dim),
            "gain": gains_of(2),
        }

    def taylor_last():
        done = CHUNKS - 2
        dqs, (dk, dv) = taylor_back(
            range(done, CHUNKS), (made[turns]["dk"], made[turns]["dv"])
        )
        dqs = [made[turns - done + 1 + m]["dq"] for m in range(done)] + dqs
        grad = jnp.concatenate([jnp.concatenate(dqs, axis=0), dk, dv], axis=1).astype(BF16)
        came = jnp.concatenate(upstreams(0), axis=0)
        grad_inputs, gain = rms_backward(
            feed.astype(F32), gain_row, nt(grad, pack_in[:, :taylor_cols])
        )
        return {
            "returned": (came.astype(F32) + grad_inputs).astype(BF16),
            "b": grad_in(gain_row, [feed], [([grad], 0, taylor_cols // TILE)], b_cols),
            "c": grad_out(
                [made[m]["mix"] for m in range(CHUNKS)], upstreams(0), width // TILE, hidden_dim
            ),
            "gain": gain,
        }

    made.append(
        branches(
            {"a": a_shape, **taylor_shapes},
            [taylor_turn_back(CHUNKS - 3), dense_first(1), window_first, dense_first(3)],
        )
    )
    axes = ("dp", "seq")
    a = made[turns]["a"]
    sum_a = lax.psum_scatter(a, axes, scatter_dimension=0, tiled=True)
    rest = branches(
        {
            "b": b_shape,
            "c": ((hidden_dim, width), BF16),
            "gain": gain_shape,
            "returned": ((length, width), BF16),
        },
        [taylor_last, dense_second(1), window_second, dense_second(3)],
    )
    sum_b = lax.psum_scatter(rest["b"], axes, scatter_dimension=0, tiled=True)
    sum_c = lax.psum_scatter(rest["c"], axes, scatter_dimension=0, tiled=True)
    out_gain = lax.psum_scatter(rest["gain"][0], axes, scatter_dimension=0, tiled=True)

    finals = [made[LAG * last + m]["final"] for m in range(CHUNKS)]
    block_out = spread(swapped(jnp.concatenate(finals, axis=0).reshape(2, block, width)), last)
    grad_tokens = spread(swapped(rest["returned"].reshape(2, block, width)), 0)

    def narrow(value, used):
        return lambda: jnp.pad(value[:, :used].astype(F32), ((0, 0), (0, 2 * hidden_dim - used)))

    def dense_result():
        up_end = padded + hidden_dim - a_cols
        return jnp.concatenate(
            [sum_a[:, :hidden_dim], sum_a[:, padded:], sum_b[:, :up_end]], axis=1
        ).astype(F32)

    out_in = lax.switch(
        section,
        [narrow(sum_b, taylor_cols), dense_result, narrow(sum_a, window_cols), dense_result],
    )
    return (
        block_out,
        grad_tokens,
        out_in[None],
        sum_c.astype(F32)[None],
        out_gain[None],
    )


def solution(mesh):
    placed = (
        P("dp", "seq", None),
        P("section", None, None),
        P("section", None, None),
        P("section", None),
        P("dp", None),
        P("dp", "seq", None),
    )
    return jax.shard_map(
        local,
        mesh=mesh,
        in_specs=placed,
        out_specs=(
            P("dp", "seq", "section"),
            P("dp", "seq", "section"),
            P("section", ("dp", "seq"), None),
            P("section", ("dp", "seq"), None),
            P("section", ("dp", "seq")),
        ),
        check_vma=False,
    )
```

time: 811 us -> 629 us (0.78)
  local copies, waits for them, and re-layouts: 77.1 us -> 11.2 us
  waiting for transfers between devices: 342 us -> 287 us
  other arithmetic: 66 us -> 25.7 us
  starting transfers between devices: 66.1 us -> 49.4 us
  matrix products: 58 us -> 41.4 us
  Pallas kernels: 85.8 us -> 101 us
  loops' own time: 78.8 us -> 68.7 us
    ppermute x12 -> x16, waiting for transfers between devices: 202 us -> 137 us  [local(): lax.ppermute(made[t][name], 'section', which)]
    another operation x45 -> x7, local copies, waits for them, and re-layouts: 32 us -> 1.54 us
    ppermute x12 -> x16, starting transfers between devices: 57.9 us -> 33.5 us  [local(): lax.ppermute(made[t][name], 'section', which)]
    slice x24 -> x0, local copies, waits for them, and re-layouts: 18.8 us -> none  [the longest x4 6.28 us: branch(): grad = joined_turns([grads_low[t][:, :used] for t in picks])]
    unnamed x2 -> x0, loops' own time: 17.5 us -> none
    concatenate x10 -> x2, other arithmetic: 21.2 us -> 4.81 us  [the longest x1 3.44 us: taylor_last(): jnp.concatenate([jnp.concatenate(dqs, axis=0), dk, dv], axis=1).astype(BF16)]
    pallas_call x0 -> x16, Pallas kernels: none -> 15.6 us  [the longest x1 8.8 us: grad_out(): call(functools.partial(grad_out_kernel, count, used), (tiles,), [pl.Block...]
    reduce_scatter x2 -> x3, waiting for transfers between devices: 130 us -> 145 us  [the longest x1 91.1 us: local(): sum_a = lax.psum_scatter(a, axes, scatter_dimension=0, tiled=True)]
  transfers between devices with their start and end apart: 23 -> 28, of which waited for: 16 -> 9; matrix products, arithmetic and copies ran while one was open for 2% -> 6% of each run, Pallas kernels for 0% -> 7%
where the time goes in v2:
time: 629 us; the launch traced here: 617 us
  waiting for transfers between devices  287 us (46%)
  Pallas kernels  101 us (16%)
  loops' own time  68.7 us (11%)
  starting transfers between devices  49.4 us (8%)
  matrix products  41.4 us (7%)
  other arithmetic  25.7 us (4%)
  blocking collectives  17.4 us (3%)
  between operations  15.3 us (2%)
  local copies, waits for them, and re-layouts  11.2 us (2%)
    ppermute x16, waiting for transfers between devices, local(): lax.ppermute(made[t][name], 'section', which)  137 us
    reduce_scatter x1, waiting for transfers between devices, local(): sum_a = lax.psum_scatter(a, axes, scatter_dimension=0, tiled=True)  91.1 us
    another operation x16, loops' own time, branches(): values = lax.switch(section, [branch(maker) for maker in makers])  68.7 us
    pallas_call x4, Pallas kernels, taylor_backward(): call(functools.partial(taylor_backward_kernel, m, size, later is not None...  52.4 us
    reduce_scatter x1, waiting for transfers between devices, local(): sum_b = lax.psum_scatter(rest['b'], axes, scatter_dimension=0, tiled=True)  38.8 us
    ppermute x16, starting transfers between devices, local(): lax.ppermute(made[t][name], 'section', which)  33.5 us
    pallas_call x4, Pallas kernels, taylor_forward(): call(functools.partial(taylor_forward_kernel, m, size), (PAIRS,), [whole(...  33.1 us
    dot_general x8, matrix products, nn(): return jnp.dot(a, b, preferred_element_type=F32)  25.3 us
  transfers between devices with their start and end apart: 28, of which 9 were waited for; matrix products, arithmetic and copies ran while one was open for 6% of the time, Pallas kernels for 7%

profile of v2, /device:TPU:0, one launch (start us, length us, event | category | flops | bytes accessed | tf_op | source)
XLA Modules:
  0.0 616.8 jit_solution(16966836284868699198)
XLA Ops:
  7.2 1.8 broadcast_select_fusion
  9.9 2.3 collective-permute-done
  12.2 1.9 maximum_select_fusion
  14.1 12.4 %conditional.17 = ((bf16[256,1024]{1,0:T(8,128)(2,1)}, bf16[256,1536]{1,0:T(8,128)(2,1)}, bf16[256,1024]{1,0:T(8,128)(2,1)}, f32[256,128]{1,0:T(8,128)}, bf16[10...) conditional(s32[]{:T(128)} %clamp.2, ...), branch_computations={%region_1.3_spmd, %region_3.4_spmd, %region_4.5_spmd, %region_5.6_... | conditional | flops 2418934016 | bytes 90704736 | solution.py:805
  14.5 2.9 fusion.2.refs_2_.refs_3_.refs_4_
  17.5 5.7 branch_0_fun.24
  23.2 3.3 fusion.9
  26.5 11.9 %collective-permute-start.1 = (bf16[256,1024]{1,0:T(8,128)(2,1)}, bf16[256,1024]{1,0:T(8,128)(2,1)S(1)}, u32[]{:S(2)}, u32[]{:S(2)}) collective-permute-start(bf16[256,1024]{1,0:T(8,128)(2,1)} %get-tuple-element.1184), channel_id=1, source_target_pairs={{0,8},{1,9},{2,10},{3,11},{4,12},{5,13},{6,14},{7,15}} | collective-permute-start | bytes 1572872 | tf_op jit(solution)/shard_map/ppermute | solution.py:1036
  38.4 13.8 %conditional.18 = ((bf16[256,1024]{1,0:T(8,128)(2,1)}, bf16[256,1536]{1,0:T(8,128)(2,1)}, bf16[256,1024]{1,0:T(8,128)(2,1)}, f32[256,128]{1,0:T(8,128)})) conditional(s32[]{:T(128)} %clamp.2, (bf16[1024,1024]{1,0:T(8,128)(2,1)S(1)}, f32[1,1024]{1,0:T(1,128)S(1)}, bf16[1024,5504]{1,0:T(8,128)(2,1)}, ...), branch_computations={%region_6.8_spmd, %region_8.9_spmd, %region_9.10_spmd, %region_10.... | conditional | flops 3492675840 | bytes 21250172 | solution.py:805
  38.8 3.0 fusion.21.refs_2_.refs_4_.refs_6_
  41.9 6.8 %branch_0_fun.26 = (bf16[256,1024]{1,0:T(8,128)(2,1)S(1)}, f32[256,128]{1,0:T(8,128)}) custom-call(s32[1024,1]{1,0:T(8,128)S(1)} %copy.42.refs_0_, s32[1,1024]{1,0:T(1,128)S(1)} %get-tuple-element.636.refs_1_, bf16[256,1536]{1,0:T(8,128)(2,1)S(1)} %fusion.21.refs_2_.refs_4_.refs_6_, bf16[256,1536]{1,0:T(8,128)(2,1)S(1)} %copy-done.59, ...), custom_call_target="tpu_custom_call" | custom-call | flops 2147483648 | bytes 4194304 | tf_op jit(solution)/shard_map/cond/branch_0_fun/pallas_call | solution.py:109
  48.7 3.3 fusion.28
  52.2 2.1 collective-permute-start.4
  55.0 16.5 %conditional.19 = ((bf16[256,1024]{1,0:T(8,128)(2,1)}, bf16[256,1536]{1,0:T(8,128)(2,1)}, bf16[256,1024]{1,0:T(8,128)(2,1)}, f32[256,128]{1,0:T(8,128)}, bf16[25...) conditional(s32[]{:T(128)} %clamp.2, (bf16[1024,1024]{1,0:T(8,128)(2,1)S(1)}, ...), branch_computations={%region_11.13_spmd, %region_13.14_spmd, %region_14.15_spmd, %regio... | conditional | flops 4566417408 | bytes 26493096 | solution.py:805
  55.5 3.1 fusion.40.refs_2_.refs_5_.refs_8_
  58.6 9.6 %branch_0_fun.27 = (bf16[256,1024]{1,0:T(8,128)(2,1)S(1)}, f32[256,128]{1,0:T(8,128)}) custom-call(s32[1024,1]{1,0:T(8,128)S(1)} %copy.43.refs_0_, s32[1,1024]{1,0:T(1,128)S(1)} %get-tuple-element.645.refs_1_, bf16[256,1536]{1,0:T(8,128)(2,1)S(1)} %fusion.40.refs_2_.refs_5_.refs_8_, bf16[256,1536]{1,0:T(8,128)(2,1)S(1)} %copy-done.60, ...), custom_call_target="tpu_custom_call" | custom-call | flops 3221225472 | bytes 6291456 | tf_op jit(solution)/shard_map/cond/branch_0_fun/pallas_call | solution.py:109
  68.2 3.3 fusion.47
  72.8 24.2 %conditional.21 = ((bf16[256,1024]{1,0:T(8,128)(2,1)}, bf16[256,1536]{1,0:T(8,128)(2,1)}, bf16[256,1024]{1,0:T(8,128)(2,1)}, f32[256,128]{1,0:T(8,128)}, bf16[25...) conditional(s32[]{:T(128)} %clamp.2, (bf16[1024,1024]{1,0:T(8,128)(2,1)S(1)}, ...), branch_computations={%region_21.23_spmd, %region_23.24_spmd, %region_24.25_spmd, %regio... | conditional | flops 5640159232 | bytes 31736004 | solution.py:805
  73.3 3.1 fusion.77.refs_2_.refs_6_.refs_10_
  76.4 11.0 %branch_0_fun.30 = (bf16[256,1024]{1,0:T(8,128)(2,1)S(1)}, f32[256,128]{1,0:T(8,128)}) custom-call(s32[1024,1]{1,0:T(8,128)S(1)} %copy.45.refs_0_, s32[1,1024]{1,0:T(1,128)S(1)} %get-tuple-element.686.refs_1_, bf16[256,1536]{1,0:T(8,128)(2,1)S(1)} %fusion.77.refs_2_.refs_6_.refs_10_, bf16[256,1536]{1,0:T(8,128)(2,1)S(1)} %copy-done.61, ...), custom_call_target="tpu_custom_call" | custom-call | flops 4294967296 | bytes 8388608 | tf_op jit(solution)/shard_map/cond/branch_0_fun/pallas_call | solution.py:109
  87.4 3.3 fusion.84
  97.0 2.1 collective-permute-start.5
  100.6 9.5 %collective-permute-done.5 = bf16[256,1024]{1,0:T(8,128)(2,1)} collective-permute-done((bf16[256,1024]{1,0:T(8,128)(2,1)}, bf16[256,1024]{1,0:T(8,128)(2,1)}, u32[]{:S(2)}, u32[]{:S(2)}) %collective-permute-start.5) | collective-permute-done | bytes 524320 | tf_op jit(solution)/shard_map/ppermute | solution.py:1036
  110.1 5.3 conditional.22
  115.4 1.5 collective-permute-start.6
  116.9 8.6 %conditional.23 = ((bf16[256,1024]{1,0:T(8,128)(2,1)}, bf16[256,3072]{1,0:T(8,128)(2,1)}, bf16[256,1024]{1,0:T(8,128)(2,1)}, bf16[256,1024]{1,0:T(8,128)(2,1)}, ...) conditional(s32[]{:T(128)} %clamp.2, () %tuple.253, () %tuple.254, ...), branch_computations={%region_31.32_spmd, %region_32.33_spmd, %region_33.35_spmd, %regio... | conditional | flops 8858370048 | bytes 27279488 | solution.py:805
  127.0 13.4 %conditional.24 = ((bf16[256,1024]{1,0:T(8,128)(2,1)}, bf16[256,3072]{1,0:T(8,128)(2,1)}, bf16[256,1024]{1,0:T(8,128)(2,1)}, bf16[256,1024]{1,0:T(8,128)(2,1)}, ...) conditional(s32[]{:T(128)} %clamp.2, () %tuple.280, () %tuple.281, ...), branch_computations={%region_36.37_spmd, %region_37.38_spmd, %region_38.40_spmd, %regio... | conditional | flops 8858370048 | bytes 27279488 | solution.py:805
  140.3 1.5 collective-permute-start.8
  141.8 1.5 collective-permute-start.14
  143.3 13.4 %conditional.26 = ((bf16[256,1024]{1,0:T(8,128)(2,1)}, bf16[256,1024]{1,0:T(8,128)(2,1)}, bf16[256,2816]{1,0:T(8,128)(2,1)}, bf16[256,2816]{1,0:T(8,128)(2,1)}, ...) conditional(s32[]{:T(128)} %clamp.2, () %tuple.288, () %tuple.289, ...), branch_computations={%region_45.46_spmd, %region_46.47_spmd, %region_47.51_spmd, %regio... | conditional | flops 8858370048 | bytes 93355216 | solution.py:805
  158.1 1.5 collective-permute-start.17
  159.6 7.2 %conditional.28 = ((bf16[256,1024]{1,0:T(8,128)(2,1)}, bf16[256,3072]{1,0:T(8,128)(2,1)}, f32[1,1024]{1,0:T(1,128)S(1)}, bf16[256,1024]{1,0:T(8,128)(2,1)}, bf16...) conditional(s32[]{:T(128)} %clamp.2, () %tuple.292, ...), branch_computations={%region_59.60_spmd, %region_60.61_spmd, %region_61.68_spmd, %regio... | conditional | flops 6453723136 | bytes 100722880 | solution.py:805
  170.2 85.2 %collective-permute-done.15 = bf16[256,1024]{1,0:T(8,128)(2,1)} collective-permute-done((bf16[256,1024]{1,0:T(8,128)(2,1)}, bf16[256,1024]{1,0:T(8,128)(2,1)}, u32[]{:S(2)}, u32[]{:S(2)}) %collective-permute-start.15) | collective-permute-done | bytes 524320 | tf_op jit(solution)/shard_map/ppermute | solution.py:1036
  256.2 17.4 %conditional.29 = ((bf16[256,1024]{1,0:T(8,128)(2,1)}, bf16[256,2816]{1,0:T(8,128)(2,1)}, bf16[256,2816]{1,0:T(8,128)(2,1)}, bf16[256,2816]{1,0:T(8,128)(2,1)}, ...) conditional(s32[]{:T(128)} %clamp.2, ...), branch_computations={%region_69.70_spmd, %region_70.71_spmd, %region_71.72_spmd, %regio... | conditional | flops 8858371072 | bytes 57684196 | solution.py:805
  256.5 2.6 fusion.216.refs_5_
  259.1 7.5 %branch_0_fun.40 = (f32[256,256]{1,0:T(8,128)S(1)}, f32[256,256]{1,0:T(8,128)}, f32[256,1024]{1,0:T(8,128)}) custom-call(s32[1024,1]{1,0:T(8,128)S(1)} %copy.53.refs_0_, s32[1,1024]{1,0:T(1,128)S(1)} %get-tuple-element.892.refs_1_, bf16[256,1536]{1,0:T(8,128)(2,1)S(1)} %copy-done.62, bf16[256,1536]{1,0:T(8,128)(2,1)S(1)} %copy-done.62, ...), custom_call_target="tpu_custom_call" | custom-call | flops 2684354560 | bytes 5242880 | tf_op jit(solution)/shard_map/cond/branch_0_fun/pallas_call | solution.py:199
  276.3 14.1 %conditional.31 = (bf16[1024,4096]{1,0:T(8,128)(2,1)}, f32[256,256]{1,0:T(8,128)}, f32[512,256]{1,0:T(8,128)}, f32[512,1024]{1,0:T(8,128)}) conditional(s32[]{:T(128)} %clamp.2, (bf16[2752,1024]{1,0:T(8,128)(2,1)}, bf16[256,1024]{1,0:T(8,128)(2,1)}, s32[1024,1]{0,1:T(1,128)S(1)}, s32[1,1024]{1,0:T(1,128)S(1)}, ...), branch_computations={%region_77.78_spmd, %region_78.79_spmd, %region_79.80_spmd, %regio... | conditional | flops 8589934592 | bytes 27795656 | solution.py:805
  276.6 2.6 fusion.221.refs_7_
  279.3 11.1 %branch_0_fun.43 = (f32[256,256]{1,0:T(8,128)}, f32[512,256]{1,0:T(8,128)}, f32[512,1024]{1,0:T(8,128)}) custom-call(s32[1024,1]{1,0:T(8,128)S(1)} %copy.54.refs_0_, s32[1,1024]{1,0:T(1,128)S(1)} %get-tuple-element.935.refs_1_, bf16[256,1536]{1,0:T(8,128)(2,1)S(1)} %copy-done.73, bf16[256,1536]{1,0:T(8,128)(2,1)S(1)} %copy-done.63, ...), custom_call_target="tpu_custom_call" | custom-call | flops 5368709120 | bytes 10485760 | tf_op jit(solution)/shard_map/cond/branch_0_fun/pallas_call | solution.py:199
  290.3 34.2 %collective-permute-done.19 = bf16[256,1024]{1,0:T(8,128)(2,1)} collective-permute-done((bf16[256,1024]{1,0:T(8,128)(2,1)}, bf16[256,1024]{1,0:T(8,128)(2,1)}, u32[]{:S(2)}, u32[]{:S(2)}) %collective-permute-start.19) | collective-permute-done | bytes 524320 | tf_op jit(solution)/shard_map/ppermute | solution.py:1036
  324.5 8.5 %collective-permute-done.20 = bf16[256,1024]{1,0:T(8,128)(2,1)} collective-permute-done((bf16[256,1024]{1,0:T(8,128)(2,1)}, bf16[256,1024]{1,0:T(8,128)(2,1)}, u32[]{:S(2)}, u32[]{:S(2)}) %collective-permute-start.20) | collective-permute-done | bytes 524320 | tf_op jit(solution)/shard_map/ppermute | solution.py:1036
  333.0 77.5 %conditional.32 = (bf16[1024,1536]{1,0:T(8,128)(2,1)}, bf16[2752,1024]{1,0:T(8,128)(2,1)}, f32[1,1024]{1,0:T(1,128)S(1)}, bf16[2,512,1024]{2,1,0:T(8,128)(2,1)}) conditional(s32[]{:T(128)} %clamp.2, (f32[256,256]{1,0:T(8,128)S(1)}, f32[256,256]{1,0:T(8,128)}, bf16[2752,1024]{1,0:T(8,128)(2,1)}, ...), branch_computations={%region_81.85_spmd, %region_85.86_spmd, %region_86.87_spmd, %regio... | conditional | flops 28521271296 | bytes 116457784 | solution.py:805
  333.5 2.5 fusion.241.refs_11_
  336.1 2.6 fusion.238.refs_9_
  338.8 15.6 %branch_0_fun.44 = (f32[256,256]{1,0:T(8,128)S(1)}, f32[768,256]{1,0:T(8,128)S(1)}, f32[768,1024]{1,0:T(8,128)S(1)}) custom-call(s32[1024,1]{1,0:T(8,128)S(1)} %copy.55.refs_0_, s32[1,1024]{1,0:T(1,128)S(1)} %get-tuple-element.996.refs_1_, bf16[256,1536]{1,0:T(8,128)(2,1)S(1)} %copy-done.67, bf16[256,1536]{1,0:T(8,128)(2,1)S(1)} %copy-done.64, ...), custom_call_target="tpu_custom_call" | custom-call | flops 8053063680 | bytes 15728640 | tf_op jit(solution)/shard_map/cond/branch_0_fun/pallas_call | solution.py:199
  354.5 18.2 %branch_0_fun.45 = (f32[256,256]{1,0:T(8,128)S(1)}, f32[1024,256]{1,0:T(8,128)S(1)}, f32[1024,1024]{1,0:T(8,128)S(1)}) custom-call(s32[1024,1]{1,0:T(8,128)S(1)} %copy.55.refs_0_, s32[1,1024]{1,0:T(1,128)S(1)} %get-tuple-element.996.refs_1_, bf16[256,1536]{1,0:T(8,128)(2,1)S(1)} %copy-done.69, bf16[256,1536]{1,0:T(8,128)(2,1)S(1)} %copy-done.64, ...), custom_call_target="tpu_custom_call" | custom-call | flops 10737418240 | bytes 20971520 | tf_op jit(solution)/shard_map/cond/branch_0_fun/pallas_call | solution.py:199
  374.1 3.4 pad_maximum_fusion.refs_1_
  377.6 6.8 %branch_0_fun.46 = bf16[1024,1536]{1,0:T(8,128)(2,1)} custom-call(f32[1,1024]{1,0:T(1,128)S(1)} %get-tuple-element.991.gain_ref, bf16[1024,1024]{1,0:T(8,128)(2,1)S(1)} %get-tuple-element.992.refs_0_, bf16[1024,1536]{1,0:T(8,128)(2,1)S(1)} %pad_maximum_fusion.refs_1_), custom_call_target="tpu_custom_call" | custom-call | flops 3221225472 | bytes 6291456 | tf_op jit(solution)/shard_map/cond/branch_0_fun/pallas_call | solution.py:726
  384.4 8.8 %branch_0_fun.47 = bf16[2752,1024]{1,0:T(8,128)(2,1)} custom-call(bf16[256,1024]{1,0:T(8,128)(2,1)S(1)} %copy-done.29, bf16[256,1024]{1,0:T(8,128)(2,1)S(1)} %copy-done.36, bf16[256,1024]{1,0:T(8,128)(2,1)S(1)} %copy-done.31, bf16[256,1024]{1,0:T(8,128)(2,1)S(1)} %copy-done.33, bf16[256,1024]{1,0:T(8,128)(2,1)} %get-tuple-element.1018.refs_4_, ...), custom_call_target="tpu_custom_call" | custom-call | flops 2147483648 | bytes 4194304 | tf_op jit(solution)/shard_map/cond/branch_0_fun/pallas_call | solution.py:759
  393.7 5.8 fusion.231
  399.5 4.8 fusion.230
  414.2 1.7 constant_dynamic-slice_fusion
  424.5 7.0 %collective-permute-start.22 = (bf16[2,512,256]{2,1,0:T(8,128)(2,1)}, bf16[2,512,256]{2,1,0:T(8,128)(2,1)}, u32[]{:S(2)}, u32[]{:S(2)}) collective-permute-start(bf16[2,512,256]{2,1,0:T(8,128)(2,1)} %get-tuple-element.1730), channel_id=1, source_target_pairs={{0,24},{1,25},{2,26},{3,27},{4,28},{5,29},{6,30},{7,31}} | collective-permute-start | bytes 1572872 | tf_op jit(solution)/shard_map/ppermute | solution.py:972
  431.5 2.1 collective-permute-start.23
  433.6 2.1 collective-permute-start.24
  436.9 17.4 %all-reduce.6 = f32[1024]{0:T(1024)S(1)} all-reduce(f32[1024]{0:T(1024)S(1)} %bitcast.194), channel_id=5, replica_groups=mesh['section'=4,'dp'=4,'seq'=2] {'dp','seq'}, use_global_device_ids=true, to_apply=%region_95.96.clone | all-reduce | flops 1024 | bytes 8192
  455.0 2.0 fusion.247
  456.9 2.0 fusion.245
  458.9 15.2 %reduce-scatter.8.cloned.1.call-done = bf16[344,1024]{1,0:T(8,128)(2,1)} async-done(((bf16[2752,1024]{1,0:T(8,128)(2,1)}), bf16[344,1024]{1,0:T(8,128)(2,1)}) %reduce-scatter.8.cloned.1.call-update) | async-done | bytes 704528 | tf_op jit(solution)/shard_map/reduce_scatter | solution.py:1139
  474.1 2.4 bitcast_convert_fusion.2
  476.4 38.8 %reduce-scatter.4.cloned.1.call-done = bf16[128,1536]{1,0:T(8,128)(2,1)} async-done(((bf16[1024,1536]{1,0:T(8,128)(2,1)}), bf16[128,1536]{1,0:T(8,128)(2,1)}) %reduce-scatter.4.cloned.1.call-update) | async-done | bytes 393232 | tf_op jit(solution)/shard_map/reduce_scatter | solution.py:1138
  515.2 91.1 %reduce-scatter.6.cloned.1.call-done = bf16[128,4096]{1,0:T(8,128)(2,1)} async-done(((bf16[1024,4096]{1,0:T(8,128)(2,1)}), bf16[128,4096]{1,0:T(8,128)(2,1)}) %reduce-scatter.6.cloned.1.call-update) | async-done | bytes 1048592 | tf_op jit(solution)/shard_map/reduce_scatter | solution.py:1128
  606.3 2.7 conditional.33
  606.3 2.7 bitcast_convert_fusion
  (184 shorter events, 32.3 us)
Async XLA Ops:
  7.2 466.9 %reduce-scatter.8.cloned.1.call-start = ((), (), s32[]{:S(2)}) async-start(), calls=%async_computation.5 | async-start | bytes 6340608 | tf_op jit(solution)/shard_map/reduce_scatter | solution.py:1139
  9.2 2.9 collective-permute-start
  17.5 9.0 %copy-start.58 = (bf16[256,1536]{1,0:T(8,128)(2,1)}, bf16[256,1536]{1,0:T(8,128)(2,1)S(1)}, u32[]{:S(2)}) copy-start(bf16[256,1536]{1,0:T(8,128)(2,1)S(1)} %fusion.2.refs_2_.refs_3_.refs_4_) | copy-start | bytes 2359300 | tf_op jit(solution)/shard_map/cond
  23.2 3.3 copy-start.27
  26.5 27.8 %collective-permute-start.1 = (bf16[256,1024]{1,0:T(8,128)(2,1)}, bf16[256,1024]{1,0:T(8,128)(2,1)S(1)}, u32[]{:S(2)}, u32[]{:S(2)}) collective-permute-start(bf16[256,1024]{1,0:T(8,128)(2,1)} %get-tuple-element.1184), channel_id=1, source_target_pairs={{0,8},{1,9},{2,10},{3,11},{4,12},{5,13},{6,14},{7,15}} | collective-permute-start | bytes 1572872 | tf_op jit(solution)/shard_map/ppermute | solution.py:1036
  38.8 3.0 copy-start.59
  41.8 6.8 %copy-start.70 = (bf16[256,1536]{1,0:T(8,128)(2,1)}, bf16[256,1536]{1,0:T(8,128)(2,1)S(1)}, u32[]{:S(2)}) copy-start(bf16[256,1536]{1,0:T(8,128)(2,1)S(1)} %fusion.21.refs_2_.refs_4_.refs_6_) | copy-start | bytes 2359300 | tf_op jit(solution)/shard_map/cond
  48.7 3.3 copy-start.34
  52.2 20.7 %collective-permute-start.4 = (bf16[256,1024]{1,0:T(8,128)(2,1)}, bf16[256,1024]{1,0:T(8,128)(2,1)}, u32[]{:S(2)}, u32[]{:S(2)}) collective-permute-start(bf16[256,1024]{1,0:T(8,128)(2,1)} %get-tuple-element.1191), channel_id=1, source_target_pairs={{0,8},{1,9},{2,10},{3,11},{4,12},{5,13},{6,14},{7,15}} | collective-permute-start | bytes 1572872 | tf_op jit(solution)/shard_map/ppermute | solution.py:1036
  55.5 3.1 copy-start.60
  55.5 3.1 copy-start.71
  58.6 9.7 %copy-start.65 = (bf16[256,1536]{1,0:T(8,128)(2,1)}, bf16[256,1536]{1,0:T(8,128)(2,1)S(1)}, u32[]{:S(2)}) copy-start(bf16[256,1536]{1,0:T(8,128)(2,1)S(1)} %fusion.40.refs_2_.refs_5_.refs_8_) | copy-start | bytes 2359300 | tf_op jit(solution)/shard_map/cond
  68.2 3.3 copy-start.30
  71.5 27.6 %collective-permute-start.2 = (bf16[256,1024]{1,0:T(8,128)(2,1)}, bf16[256,1024]{1,0:T(8,128)(2,1)S(1)}, u32[]{:S(2)}, u32[]{:S(2)}) collective-permute-start(bf16[256,1024]{1,0:T(8,128)(2,1)} %get-tuple-element.1188), channel_id=1, source_target_pairs={{0,8},{8,16},{1,9},{9,17},{2,10},{10,18},{3,11},{11,19},{4,12},{12... | collective-permute-start | bytes 1572872 | tf_op jit(solution)/shard_map/ppermute | solution.py:1036
  73.3 3.1 copy-start.61
  73.3 3.1 copy-start.66
  73.3 3.1 copy-start.72
  76.4 11.0 %copy-start.68 = (bf16[256,1536]{1,0:T(8,128)(2,1)}, bf16[256,1536]{1,0:T(8,128)(2,1)S(1)}, u32[]{:S(2)}) copy-start(bf16[256,1536]{1,0:T(8,128)(2,1)S(1)} %fusion.77.refs_2_.refs_6_.refs_10_) | copy-start | bytes 2359300 | tf_op jit(solution)/shard_map/cond
  87.4 3.3 copy-start.32
  97.0 13.1 %collective-permute-start.5 = (bf16[256,1024]{1,0:T(8,128)(2,1)}, bf16[256,1024]{1,0:T(8,128)(2,1)}, u32[]{:S(2)}, u32[]{:S(2)}) collective-permute-start(bf16[256,1024]{1,0:T(8,128)(2,1)} %get-tuple-element.1192), channel_id=1, source_target_pairs={{0,8},{8,16},{1,9},{9,17},{2,10},{10,18},{3,11},{11,19},{4,12},{12... | collective-permute-start | bytes 1572872 | tf_op jit(solution)/shard_map/ppermute | solution.py:1036
  99.2 17.7 %collective-permute-start.3 = (bf16[256,1024]{1,0:T(8,128)(2,1)}, bf16[256,1024]{1,0:T(8,128)(2,1)}, u32[]{:S(2)}, u32[]{:S(2)}) collective-permute-start(bf16[256,1024]{1,0:T(8,128)(2,1)} %get-tuple-element.1189), channel_id=1, source_target_pairs={{8,16},{16,24},{9,17},{17,25},{10,18},{18,26},{11,19},{19,27},{12,... | collective-permute-start | bytes 1572872 | tf_op jit(solution)/shard_map/ppermute | solution.py:1036
  115.4 11.6 %collective-permute-start.6 = (bf16[256,1024]{1,0:T(8,128)(2,1)}, bf16[256,1024]{1,0:T(8,128)(2,1)}, u32[]{:S(2)}, u32[]{:S(2)}) collective-permute-start(bf16[256,1024]{1,0:T(8,128)(2,1)} %get-tuple-element.1196), channel_id=1, source_target_pairs={{8,16},{16,24},{9,17},{17,25},{10,18},{18,26},{11,19},{19,27},{12,... | collective-permute-start | bytes 1572872 | tf_op jit(solution)/shard_map/ppermute | solution.py:1036
  125.5 16.3 %collective-permute-start.7 = (bf16[256,1024]{1,0:T(8,128)(2,1)}, bf16[256,1024]{1,0:T(8,128)(2,1)}, u32[]{:S(2)}, u32[]{:S(2)}) collective-permute-start(bf16[256,1024]{1,0:T(8,128)(2,1)} %get-tuple-element.1199), channel_id=1, source_target_pairs={{16,24},{24,16},{17,25},{25,17},{18,26},{26,18},{19,27},{27,19},{2... | collective-permute-start | bytes 1572872 | tf_op jit(solution)/shard_map/ppermute | solution.py:1036
  140.3 2.9 collective-permute-start.8
  141.8 16.3 %collective-permute-start.14 = (bf16[256,1024]{1,0:T(8,128)(2,1)}, bf16[256,1024]{1,0:T(8,128)(2,1)}, u32[]{:S(2)}, u32[]{:S(2)}) collective-permute-start(bf16[256,1024]{1,0:T(8,128)(2,1)} %get-tuple-element.1207), channel_id=1, source_target_pairs={{24,16},{25,17},{26,18},{27,19},{28,20},{29,21},{30,22},{31,23}} | collective-permute-start | bytes 1572872 | tf_op jit(solution)/shard_map/ppermute | solution.py:1036
  156.7 3.0 collective-permute-start.13
  158.1 10.7 %collective-permute-start.17 = (bf16[256,1024]{1,0:T(8,128)(2,1)}, bf16[256,1024]{1,0:T(8,128)(2,1)}, u32[]{:S(2)}, u32[]{:S(2)}) collective-permute-start(bf16[256,1024]{1,0:T(8,128)(2,1)} %get-tuple-element.1220), channel_id=1, source_target_pairs={{16,8},{17,9},{18,10},{19,11},{20,12},{21,13},{22,14},{23,15}} | collective-permute-start | bytes 1572872 | tf_op jit(solution)/shard_map/ppermute | solution.py:1036
  166.8 88.6 %collective-permute-start.15 = (bf16[256,1024]{1,0:T(8,128)(2,1)}, bf16[256,1024]{1,0:T(8,128)(2,1)}, u32[]{:S(2)}, u32[]{:S(2)}) collective-permute-start(bf16[256,1024]{1,0:T(8,128)(2,1)} %get-tuple-element.1211), channel_id=1, source_target_pairs={{16,8},{8,0},{17,9},{9,1},{18,10},{10,2},{19,11},{11,3},{20,12},{1... | collective-permute-start | bytes 1572872 | tf_op jit(solution)/shard_map/ppermute | solution.py:1036
  168.1 87.3 %collective-permute-start.16 = (bf16[256,1024]{1,0:T(8,128)(2,1)}, bf16[256,1024]{1,0:T(8,128)(2,1)S(1)}, u32[]{:S(2)}, u32[]{:S(2)}) collective-permute-start(bf16[256,1024]{1,0:T(8,128)(2,1)} %get-tuple-element.1216), channel_id=1, source_target_pairs={{16,8},{17,9},{18,10},{19,11},{20,12},{21,13},{22,14},{23,15}} | collective-permute-start | bytes 1572872 | tf_op jit(solution)/shard_map/ppermute | solution.py:1036
  168.9 107.3 %collective-permute-start.18 = (bf16[256,1024]{1,0:T(8,128)(2,1)}, bf16[256,1024]{1,0:T(8,128)(2,1)}, u32[]{:S(2)}, u32[]{:S(2)}) collective-permute-start(bf16[256,1024]{1,0:T(8,128)(2,1)} %get-tuple-element.1223), channel_id=1, source_target_pairs={{8,0},{9,1},{10,2},{11,3},{12,4},{13,5},{14,6},{15,7}} | collective-permute-start | bytes 1572872 | tf_op jit(solution)/shard_map/ppermute | solution.py:1036
  256.4 2.6 copy-start.28
  256.4 2.6 copy-start.62
  273.6 50.9 %collective-permute-start.19 = (bf16[256,1024]{1,0:T(8,128)(2,1)}, bf16[256,1024]{1,0:T(8,128)(2,1)}, u32[]{:S(2)}, u32[]{:S(2)}) collective-permute-start(bf16[256,1024]{1,0:T(8,128)(2,1)} %get-tuple-element.1249), channel_id=1, source_target_pairs={{8,0},{9,1},{10,2},{11,3},{12,4},{13,5},{14,6},{15,7}} | collective-permute-start | bytes 1572872 | tf_op jit(solution)/shard_map/ppermute | solution.py:1036
  274.9 58.1 %collective-permute-start.20 = (bf16[256,1024]{1,0:T(8,128)(2,1)}, bf16[256,1024]{1,0:T(8,128)(2,1)}, u32[]{:S(2)}, u32[]{:S(2)}) collective-permute-start(bf16[256,1024]{1,0:T(8,128)(2,1)} %get-tuple-element.1254), channel_id=1, source_target_pairs={{8,0},{9,1},{10,2},{11,3},{12,4},{13,5},{14,6},{15,7}} | collective-permute-start | bytes 1572872 | tf_op jit(solution)/shard_map/ppermute | solution.py:1036
  276.2 56.8 %copy-start.45 = (f32[1,1024]{1,0:T(1,128)S(1)}, f32[1,1024]{1,0:T(1,128)}, u32[]{:S(2)}) copy-start(f32[1,1024]{1,0:T(1,128)} %get-tuple-element.1275) | copy-start | bytes 12292
  276.2 56.8 %copy-start.46 = (f32[1,1024]{1,0:T(1,128)S(1)}, f32[1,1024]{1,0:T(1,128)}, u32[]{:S(2)}) copy-start(f32[1,1024]{1,0:T(1,128)} %get-tuple-element.1276) | copy-start | bytes 12292
  276.2 56.8 %copy-start.47 = (f32[1,1024]{1,0:T(1,128)S(1)}, f32[1,1024]{1,0:T(1,128)}, u32[]{:S(2)}) copy-start(f32[1,1024]{1,0:T(1,128)} %get-tuple-element.1277) | copy-start | bytes 12292
  276.5 2.7 copy-start.35
  276.5 2.7 copy-start.57
  276.5 2.7 copy-start.63
  276.5 2.7 copy-start.73
  276.6 2.7 copy-start.75
  276.6 2.7 copy-start.79
  336.0 2.7 copy-start.31
  336.0 2.7 copy-start.64
  336.0 2.7 copy-start.67
  336.1 2.7 copy-start.74
  336.1 2.7 copy-start.77
  338.8 15.7 %copy-start.33 = (bf16[256,1024]{1,0:T(8,128)(2,1)S(1)}, bf16[256,1024]{1,0:T(8,128)(2,1)}, u32[]{:S(2)}) copy-start(bf16[256,1024]{1,0:T(8,128)(2,1)} %get-tuple-element.1009.refs_12_.refs_3_) | copy-start | bytes 1572868 | tf_op jit(solution)/shard_map/cond
  338.8 15.7 %copy-start.69 = (bf16[256,1536]{1,0:T(8,128)(2,1)S(1)}, bf16[256,1536]{1,0:T(8,128)(2,1)}, u32[]{:S(2)}) copy-start(bf16[256,1536]{1,0:T(8,128)(2,1)} %get-tuple-element.1007.refs_2_.refs_6_.refs_10_) | copy-start | bytes 2359300 | tf_op jit(solution)/shard_map/cond
  338.8 15.7 %copy-start.78 = (f32[256,128]{1,0:T(8,128)S(1)}, f32[256,128]{1,0:T(8,128)}, u32[]{:S(2)}) copy-start(f32[256,128]{1,0:T(8,128)} %get-tuple-element.1010.refs_13_) | copy-start | bytes 393220 | tf_op jit(solution)/shard_map/cond
  377.6 6.8 %copy-start.29 = (bf16[256,1024]{1,0:T(8,128)(2,1)S(1)}, bf16[256,1024]{1,0:T(8,128)(2,1)}, u32[]{:S(2)}) copy-start(bf16[256,1024]{1,0:T(8,128)(2,1)} %get-tuple-element.1016.refs_0_) | copy-start | bytes 1572868 | tf_op jit(solution)/shard_map/cond
  377.6 6.8 %copy-start.36 = (bf16[256,1024]{1,0:T(8,128)(2,1)S(1)}, bf16[256,1024]{1,0:T(8,128)(2,1)}, u32[]{:S(2)}) copy-start(bf16[256,1024]{1,0:T(8,128)(2,1)} %get-tuple-element.1017.refs_1_) | copy-start | bytes 1572868 | tf_op jit(solution)/shard_map/cond
  410.6 104.6 %reduce-scatter.4.cloned.1.call-start = ((), (), s32[]{:S(2)}) async-start(), calls=%async_computation.3 | async-start | bytes 3538944 | tf_op jit(solution)/shard_map/reduce_scatter | solution.py:1138
  411.3 195.0 %reduce-scatter.6.cloned.1.call-start = ((), (), s32[]{:S(2)}) async-start(), calls=%async_computation.4 | async-start | bytes 9437184 | tf_op jit(solution)/shard_map/reduce_scatter | solution.py:1128
  414.2 2.7 collective-permute-start.9
  416.0 5.6 collective-permute-start.21
  418.1 15.4 %collective-permute-start.10 = (bf16[2,512,256]{2,1,0:T(8,128)(2,1)S(1)}, bf16[2,512,256]{2,1,0:T(8,128)(2,1)S(1)}, u32[]{:S(2)}, u32[]{:S(2)}) collective-permute-start(bf16[2,512,256]{2,1,0:T(8,128)(2,1)S(1)} %get-tuple-element.1735), channel_id=1, source_target_pairs={{24,16},{25,17},{26,18},{27,19},{28,20},{29,21},{30,22},{31,23}} | collective-permute-start | bytes 1572872 | tf_op jit(solution)/shard_map/ppermute | solution.py:972
  418.8 36.1 %collective-permute-start.11 = (bf16[2,512,256]{2,1,0:T(8,128)(2,1)}, bf16[2,512,256]{2,1,0:T(8,128)(2,1)}, u32[]{:S(2)}, u32[]{:S(2)}) collective-permute-start(bf16[2,512,256]{2,1,0:T(8,128)(2,1)} %get-tuple-element.1734), channel_id=1, source_target_pairs={{24,8},{25,9},{26,10},{27,11},{28,12},{29,13},{30,14},{31,15}} | collective-permute-start | bytes 1572872 | tf_op jit(solution)/shard_map/ppermute | solution.py:972
  420.3 34.7 %collective-permute-start.12 = (bf16[2,512,256]{2,1,0:T(8,128)(2,1)S(1)}, bf16[2,512,256]{2,1,0:T(8,128)(2,1)}, u32[]{:S(2)}, u32[]{:S(2)}) collective-permute-start(bf16[2,512,256]{2,1,0:T(8,128)(2,1)S(1)} %get-tuple-element.1733), channel_id=1, source_target_pairs={{24,0},{25,1},{26,2},{27,3},{28,4},{29,5},{30,6},{31,7}} | collective-permute-start | bytes 1572872 | tf_op jit(solution)/shard_map/ppermute | solution.py:972
  423.3 12.5 %copy-start.80 = (u32[32]{0:T(128)S(1)}, u32[32]{0:T(128)}, u32[]{:S(2)}) copy-start(u32[32]{0:T(128)} %constant.176) | copy-start | bytes 388
  424.5 32.5 %collective-permute-start.22 = (bf16[2,512,256]{2,1,0:T(8,128)(2,1)}, bf16[2,512,256]{2,1,0:T(8,128)(2,1)}, u32[]{:S(2)}, u32[]{:S(2)}) collective-permute-start(bf16[2,512,256]{2,1,0:T(8,128)(2,1)} %get-tuple-element.1730), channel_id=1, source_target_pairs={{0,24},{1,25},{2,26},{3,27},{4,28},{5,29},{6,30},{7,31}} | collective-permute-start | bytes 1572872 | tf_op jit(solution)/shard_map/ppermute | solution.py:972
  431.5 25.4 %collective-permute-start.23 = (bf16[2,512,256]{2,1,0:T(8,128)(2,1)}, bf16[2,512,256]{2,1,0:T(8,128)(2,1)}, u32[]{:S(2)}, u32[]{:S(2)}) collective-permute-start(bf16[2,512,256]{2,1,0:T(8,128)(2,1)} %get-tuple-element.1729), channel_id=1, source_target_pairs={{0,16},{1,17},{2,18},{3,19},{4,20},{5,21},{6,22},{7,23}} | collective-permute-start | bytes 1572872 | tf_op jit(solution)/shard_map/ppermute | solution.py:972
  433.6 23.4 %collective-permute-start.24 = (bf16[2,512,256]{2,1,0:T(8,128)(2,1)}, bf16[2,512,256]{2,1,0:T(8,128)(2,1)}, u32[]{:S(2)}, u32[]{:S(2)}) collective-permute-start(bf16[2,512,256]{2,1,0:T(8,128)(2,1)} %get-tuple-element.1728), channel_id=1, source_target_pairs={{0,8},{1,9},{2,10},{3,11},{4,12},{5,13},{6,14},{7,15}} | collective-permute-start | bytes 1572872 | tf_op jit(solution)/shard_map/ppermute | solution.py:972
  (9 other events, 12.9 us)
Sparse Core Ops, SparseCore 0:
  410.7 63.3 reduce-scatter.7
  476.5 38.6 reduce-scatter.3
  517.6 88.6 reduce-scatter.5

commit v3 on v2

v3 whole, which is shorter than its diff:
```python
import functools

import jax
import jax.numpy as jnp
from jax import lax
from jax.experimental import pallas as pl
from jax.experimental.pallas import tpu as pltpu
from jax.sharding import PartitionSpec as P

HEADS = 16
FEAT_DIM = 16
WINDOW = 64
CHUNKS = 4
LAG = 2
TILE = 256
PAIRS = HEADS // 2
epsilon = 1e-06

F32 = jnp.float32
BF16 = jnp.bfloat16


def nn(a, b):
    return jnp.dot(a, b, preferred_element_type=F32)


def nt(a, b):
    return lax.dot_general(a, b, (((1,), (1,)), ((), ())), preferred_element_type=F32)


def tn(a, b):
    return lax.dot_general(a, b, (((0,), (0,)), ((), ())), preferred_element_type=F32)


def lanes(rows, width):
    return lax.broadcasted_iota(jnp.int32, (rows, width), 1)


def call(kernel, grid, in_specs, out_specs, out_shape, scratch, flops):
    return pl.pallas_call(
        kernel,
        grid=grid,
        in_specs=in_specs,
        out_specs=out_specs,
        out_shape=out_shape,
        scratch_shapes=scratch,
        compiler_params=pltpu.CompilerParams(
            vmem_limit_bytes=40 * 1024 * 1024, dimension_semantics=("arbitrary",)
        ),
        cost_estimate=pl.CostEstimate(flops=flops, bytes_accessed=flops // 512, transcendentals=0),
    )


def whole(shape):
    return pl.BlockSpec(shape, lambda p: (0,) * len(shape))


def columns(rows, start=0, row=0):
    return pl.BlockSpec((rows, 128), lambda p: (row, start + p))


def finish(copies):
    for copy in copies:
        copy.wait()


IN_VMEM = pl.BlockSpec(memory_space=pltpu.VMEM)
IN_PLACE = pl.BlockSpec(memory_space=pl.ANY)


def plain_call(kernel, in_specs, out_specs, out_shape, scratch, flops):
    return pl.pallas_call(
        kernel,
        grid=(1,),
        in_specs=in_specs,
        out_specs=out_specs,
        out_shape=out_shape,
        scratch_shapes=scratch,
        compiler_params=pltpu.CompilerParams(vmem_limit_bytes=48 * 1024 * 1024),
        cost_estimate=pl.CostEstimate(flops=flops, bytes_accessed=flops // 512, transcendentals=0),
    )


def rms_inverse(inputs):
    return lax.rsqrt(jnp.mean(inputs * inputs, axis=-1, keepdims=True) + epsilon)


def rms_forward(inputs, gain_row):
    return (inputs * rms_inverse(inputs) * gain_row).astype(BF16)


def rms_backward(inputs, gain_row, grad_normed):
    inverse = rms_inverse(inputs)
    scaled = grad_normed * gain_row
    grad_inputs = inverse * scaled - inputs * inverse**3 * jnp.mean(
        scaled * inputs, axis=-1, keepdims=True
    )
    grad_gain = jnp.sum(grad_normed * inputs * inverse, axis=0, keepdims=True)
    return grad_inputs, grad_gain


def pair_lanes(pair, start=0):
    return pl.ds(pl.multiple_of(start + pair * 128, 128), 128)


def stacked(value):
    lane = lanes(*value.shape)
    zero = jnp.zeros_like(value)
    return jnp.concatenate(
        [jnp.where(lane < 64, value, zero), jnp.where(lane < 64, zero, value)], axis=0
    )


def unstacked(value):
    rows = value.shape[0] // 2
    return jnp.where(lanes(rows, 128) < 64, value[:rows], value[rows:])


def twice(value, axis):
    return jnp.concatenate([value, value], axis=axis)


def taylor_mask(doc_t, doc_s, t_start, t_axis):
    t = t_start + lax.broadcasted_iota(jnp.int32, (doc_t == doc_s).shape, t_axis)
    s = lax.broadcasted_iota(jnp.int32, (doc_t == doc_s).shape, 1 - t_axis)
    return jnp.where((doc_t == doc_s) & (s <= t), 1.0, 0.0).astype(F32)


def taylor_queries(q, pair):
    wide = lanes(*q.shape) // FEAT_DIM
    zero = jnp.zeros_like(q)
    scaled = q * jnp.asarray(0.25, BF16)
    return jnp.concatenate(
        [jnp.where(wide == 2 * pair + i, scaled, zero) for i in range(2)], axis=0
    )


def taylor_forward_kernel(m, size, x_ref, gain_ref, docc, docr, in_ref, out_w_ref, *refs):
    earlier, refs = refs[:m], refs[m:]
    out_ref, kept_ref, mix_ref, den_ref, w_in, w_out, kv, mask, sems = refs
    rows = (m + 1) * size
    narrow, width = 2 * 128, x_ref.shape[1]
    cols = kept_ref.shape[1]
    reads = [
        pltpu.make_async_copy(
            in_ref.at[:, pl.ds(0, 2 * narrow)], w_in.at[:, pl.ds(0, 2 * narrow)], sems.at[0]
        ),
        pltpu.make_async_copy(
            in_ref.at[:, pl.ds(2 * narrow, width)], w_in.at[:, pl.ds(2 * narrow, width)], sems.at[1]
        ),
        pltpu.make_async_copy(out_w_ref.at[pl.ds(0, width), :], w_out, sems.at[2]),
    ] + [
        pltpu.make_async_copy(
            earlier[j].at[:, pl.ds(narrow, cols - narrow)],
            kv.at[pl.ds(j * size, size), :],
            sems.at[3 + j],
        )
        for j in range(m)
    ]
    for copy in reads:
        copy.start()
    inputs = x_ref[...].astype(F32)
    normed = rms_forward(inputs, gain_ref[...])
    mask[...] = taylor_mask(docc[m * size : rows, :], docr[:, :rows], m * size, 0)
    den_ref[...] = jnp.zeros_like(den_ref)
    reads[0].wait()
    kept_ref[:, : 2 * narrow] = nn(normed, w_in[:, : 2 * narrow]).astype(BF16)
    reads[1].wait()
    kept_ref[:, 2 * narrow :] = nn(normed, w_in[:, 2 * narrow :]).astype(BF16)
    kv[m * size : rows, :] = kept_ref[:, narrow:]
    finish(reads[3:])
    lane = lanes(size, 128)

    def one(pair, carry):
        a = nt(taylor_queries(kept_ref[:, :narrow], pair), kv[:, :narrow])
        w = (1.0 + a * (1.0 + 0.5 * a)) * twice(mask[...], 0)
        denom = jnp.sum(w, axis=1, keepdims=True)
        ratio = nn(w.astype(BF16), kv[:, pair_lanes(pair, narrow)]) / denom
        mix_ref[:, pair_lanes(pair)] = unstacked(ratio).astype(BF16)
        den_ref[...] = jnp.where(
            lane == 2 * pair,
            denom[:size],
            jnp.where(lane == 2 * pair + 1, denom[size:], den_ref[...]),
        )
        return carry

    lax.fori_loop(0, PAIRS, one, 0)
    reads[2].wait()
    out_ref[...] = (inputs + nn(mix_ref[...], w_out[...])).astype(BF16)


def taylor_forward(m, x, x_row, gain, docs, pack_in, pack_out, earlier):
    width = pack_in.shape[0]
    size = docs[0].shape[0] // CHUNKS
    cols = 2 * HEADS * FEAT_DIM + width
    low = jax.ShapeDtypeStruct((size, width), BF16)
    return plain_call(
        functools.partial(taylor_forward_kernel, m, size),
        [pl.BlockSpec((size, width), lambda p: (x_row, 0))] + [IN_VMEM] * 3 + [IN_PLACE] * (2 + m),
        [IN_VMEM] * 4,
        [
            low,
            jax.ShapeDtypeStruct((size, cols), BF16),
            low,
            jax.ShapeDtypeStruct((size, 128), F32),
        ],
        [
            pltpu.VMEM((width, cols), BF16),
            pltpu.VMEM((width, width), BF16),
            pltpu.VMEM(((m + 1) * size, cols - 256), BF16),
            pltpu.VMEM((size, (m + 1) * size), F32),
            pltpu.SemaphoreType.DMA((3 + m,)),
        ],
        2 * size * width * (cols + width),
    )(x, gain, *docs[:2], pack_in, pack_out, *earlier)


def taylor_backward_kernel(m, size, later, *refs):
    docc, docr, q_ref = refs[:3]
    refs = refs[3:]
    ks, vs = refs[: m + 1], refs[m + 1 : 2 * m + 2]
    dmix_ref, mix_ref, den_ref = refs[2 * m + 2 : 2 * m + 5]
    refs = refs[2 * m + 5 :]
    if later:
        dk_in, dv_in = refs[:2]
        refs = refs[2:]
    dq_ref, dk_ref, dv_ref, mask, k_all, k_turned, dq_turned = refs
    pair = pl.program_id(0)
    rows = (m + 1) * size

    @pl.when(pair == 0)
    def _():
        mask[...] = taylor_mask(docr[:, m * size : rows], docc[:rows, :], m * size, 1)
        for j in range(m + 1):
            k = ks[j][...]
            k_all[j * size : (j + 1) * size, :] = k
            k_turned[:, j * size : (j + 1) * size] = (k.astype(F32) * 0.25).T.astype(BF16)
        dk_ref[...] = jnp.zeros_like(dk_ref)
        if later:
            dk_ref[: m * size, :] = dk_in[...]

    lane = lanes(size, 128)
    dm = dmix_ref[...].astype(F32)
    both = dm * mix_ref[...].astype(F32)
    dnums, extras = [], []
    for i in range(2):
        inside = lane // 64 == i
        turn = 1.0 / jnp.sum(
            jnp.where(lane == 2 * pair + i, den_ref[...], 0.0), axis=1, keepdims=True
        )
        dden = -jnp.sum(jnp.where(inside, both, 0.0), axis=1, keepdims=True) * turn
        high = dden.astype(BF16).astype(F32)
        dnums.append(jnp.where(inside, dm * turn, 0.0).astype(BF16))
        extras.append(
            jnp.where(lane == 0, high, jnp.where(lane == 1, dden - high, 0.0)).astype(BF16)
        )
    dnum = jnp.concatenate(dnums, axis=0)
    dnum_more = jnp.concatenate([dnum, jnp.concatenate(extras, axis=0)], axis=1)
    q = taylor_queries(q_ref[...], pair)
    v = jnp.concatenate([part[...] for part in vs], axis=0)
    a = nt(k_all[...], q)
    masks = twice(mask[...], 1)
    w = (1.0 + a * (1.0 + 0.5 * a)) * masks
    dw = nt(jnp.concatenate([v, jnp.ones_like(v)], axis=1), dnum_more)
    da = (dw * (1.0 + a) * masks).astype(BF16)
    dv = nn(w.astype(BF16), dnum)
    if later:
        dv_ref[: m * size, :] = dv_in[...] + dv[: m * size]
        dv_ref[m * size :, :] = dv[m * size :]
    else:
        dv_ref[...] = dv
    dk_ref[...] += nn(da, q)
    own = pl.ds(pl.multiple_of(pair * 2 * FEAT_DIM, 2 * FEAT_DIM), 2 * FEAT_DIM)
    dq = nn(k_turned[own, :], da)
    dq_turned[own, :] = jnp.concatenate([dq[:FEAT_DIM, :size], dq[FEAT_DIM:, size:]], axis=0)

    @pl.when(pair == PAIRS - 1)
    def _():
        dq_ref[...] = dq_turned[...].T


def taylor_backward(m, docs, kept, dmix, mix, den, later):
    size = kept[0].shape[0]
    docc, docr = docs[:2]
    rows = (m + 1) * size
    return call(
        functools.partial(taylor_backward_kernel, m, size, later is not None),
        (PAIRS,),
        [whole(docc.shape), whole(docr.shape), whole((size, 256))]
        + [pl.BlockSpec((size, 256), lambda p: (0, 1))] * (m + 1)
        + [columns(size, 4)] * (m + 1)
        + [columns(size), columns(size), whole((size, 128))]
        + ([whole((m * size, 256)), columns(m * size)] if later is not None else []),
        [whole((size, 256)), whole((rows, 256)), columns(rows)],
        [
            jax.ShapeDtypeStruct((size, 256), F32),
            jax.ShapeDtypeStruct((rows, 256), F32),
            jax.ShapeDtypeStruct((rows, HEADS * 64), F32),
        ],
        [
            pltpu.VMEM((rows, size), F32),
            pltpu.VMEM((rows, 256), BF16),
            pltpu.VMEM((256, rows), BF16),
            pltpu.VMEM((256, size), F32),
        ],
        5 * HEADS * (m + 1) * size * size * 512,
    )(docc, docr, kept[m], *kept, *kept, dmix, mix, den, *(later or ()))


STEP = 128
UNROLL = 4


def window_docs(docs):
    return jnp.concatenate([jnp.full((STEP,), -1, jnp.int32), docs])[:, None]


def window_biases(m, size, docc, docr, bias):
    s = lax.broadcasted_iota(jnp.int32, (2 * STEP, STEP), 0)
    t = STEP + lax.broadcasted_iota(jnp.int32, (2 * STEP, STEP), 1)
    near = (t >= s) & (t - s < WINDOW)
    for b in range(size // STEP):
        at = m * size + b * STEP
        same = docr[:, at : at + STEP] == docc[at : at + 2 * STEP, :]
        bias[b] = jnp.where(near & same, 0.0, -1e30).astype(F32)


def window_weights(k, q, bias):
    a = nt(k, q) + twice(bias, 1)
    p = jnp.exp(a - jnp.max(a, axis=0, keepdims=True))
    return p * (1.0 / jnp.sum(p, axis=0, keepdims=True))


def joined(before, own, cut):
    value = own[:, cut]
    first = before[:, cut] if before is not None else jnp.zeros((STEP, 128), BF16)
    return jnp.concatenate([first, value], axis=0)


def window_forward_kernel(m, size, x_ref, gain_ref, docc, docr, in_ref, out_w_ref, *refs):
    before, refs = (refs[0], refs[1:]) if m > 0 else (None, refs)
    out_ref, kept_ref, mix_ref, w_in, w_out, bias, sems = refs
    width = x_ref.shape[1]
    reads = [
        pltpu.make_async_copy(
            in_ref.at[:, pl.ds(i * width, width)], w_in.at[:, pl.ds(i * width, width)], sems.at[i]
        )
        for i in range(3)
    ] + [pltpu.make_async_copy(out_w_ref.at[pl.ds(0, width), :], w_out, sems.at[3])]
    for copy in reads:
        copy.start()
    inputs = x_ref[...].astype(F32)
    normed = rms_forward(inputs, gain_ref[...])
    for i in range(3):
        cut = slice(i * width, (i + 1) * width)
        reads[i].wait()
        kept_ref[:, cut] = nn(normed, w_in[:, cut]).astype(BF16)

    window_biases(m, size, docc, docr, bias)

    def one(pair, carry):
        cuts = [pair_lanes(pair, i * width) for i in range(3)]
        k_all = joined(before, kept_ref, cuts[1])
        v_all = joined(before, kept_ref, cuts[2])
        for b in range(size // STEP):
            own = slice(b * STEP, (b + 1) * STEP)
            keys = slice(b * STEP, (b + 2) * STEP)
            q = stacked(kept_ref[own, cuts[0]] * jnp.asarray(0.125, BF16))
            p = window_weights(k_all[keys], q, bias[b])
            mix_ref[own, cuts[0]] = unstacked(tn(p.astype(BF16), v_all[keys])).astype(BF16)
        return carry

    lax.fori_loop(0, PAIRS, one, 0, unroll=UNROLL)
    reads[3].wait()
    out_ref[...] = (inputs + nn(mix_ref[...], w_out[...])).astype(BF16)


def before_spec(size, cols):
    return pl.BlockSpec((STEP, cols), lambda p: (size // STEP - 1, 0))


def window_forward(m, x, gain, docs, pack_in, pack_out, before):
    size, width = x.shape
    low = jax.ShapeDtypeStruct((size, width), BF16)
    more = [before_spec(size, 3 * width)] if m > 0 else []
    return plain_call(
        functools.partial(window_forward_kernel, m, size),
        [IN_VMEM] * 4 + [IN_PLACE] * 2 + more,
        [IN_VMEM] * 3,
        [low, jax.ShapeDtypeStruct((size, 3 * width), BF16), low],
        [
            pltpu.VMEM((width, 3 * width), BF16),
            pltpu.VMEM((width, width), BF16),
            pltpu.VMEM((size // STEP, 2 * STEP, STEP), F32),
            pltpu.SemaphoreType.DMA((4,)),
        ],
        8 * size * width * width,
    )(x, gain, docs[2], docs[1], pack_in, pack_out, *([before] if m > 0 else []))


def window_backward_kernel(m, size, docc, docr, kept_ref, g_ref, out_w_ref, *refs):
    w_out, dmix, bias, sems = refs[-4:]
    refs = refs[:-4]
    before = None
    if m > 0:
        before, part_ref, x_ref, gain_ref, g_before_ref, in_ref = refs[:6]
        grad_ref, out_ref, done_ref, dgain_ref, w_in = refs[6:]
    else:
        (grad_ref,) = refs
    width = g_ref.shape[1]
    first = pltpu.make_async_copy(out_w_ref.at[pl.ds(0, width), :], w_out, sems.at[3])
    first.start()
    reads = []
    if m > 0:
        reads = [
            pltpu.make_async_copy(
                in_ref.at[:, pl.ds(i * width, width)],
                w_in.at[:, pl.ds(i * width, width)],
                sems.at[i],
            )
            for i in range(3)
        ]
        for copy in reads:
            copy.start()
        done_ref[...] = part_ref[...]
    first.wait()
    dmix[...] = nt(g_ref[...], w_out[...]).astype(BF16)

    window_biases(m, size, docc, docr, bias)

    def one(pair, carry):
        cuts = [pair_lanes(pair, i * width) for i in range(3)]
        k_all = joined(before, kept_ref, cuts[1])
        v_all = joined(before, kept_ref, cuts[2])
        blocks = size // STEP
        halves = [[0.0] * (blocks + 1) for _ in range(2)]
        for b in range(blocks):
            own = slice(b * STEP, (b + 1) * STEP)
            keys = slice(b * STEP, (b + 2) * STEP)
            q = stacked(kept_ref[own, cuts[0]] * jnp.asarray(0.125, BF16))
            dm = stacked(dmix[own, cuts[0]])
            k, v = k_all[keys], v_all[keys]
            p = window_weights(k, q, bias[b])
            dp = nt(v, dm)
            da = (p * (dp - jnp.sum(p * dp, axis=0, keepdims=True))).astype(BF16)
            for half, more in zip(halves, (nn(da, q), nn(p.astype(BF16), dm))):
                half[b] = half[b] + more[:STEP]
                half[b + 1] = more[STEP:]
            dq = unstacked(tn(da, k * jnp.asarray(0.125, BF16)))
            grad_ref[own, cuts[0]] = dq.astype(BF16)
        for half, cut in zip(halves, cuts[1:]):
            grad_ref[:, cut] = jnp.concatenate(half[1:], axis=0).astype(BF16)
            if m > 0:
                tail = slice(size - STEP, size)
                done_ref[tail, cut] = (part_ref[tail, cut].astype(F32) + half[0]).astype(BF16)
        return carry

    lax.fori_loop(0, PAIRS, one, 0, unroll=UNROLL)
    if m > 0:
        total = 0.0
        for i in range(3):
            cut = slice(i * width, (i + 1) * width)
            reads[i].wait()
            total = total + nt(done_ref[:, cut], w_in[:, cut])
        grad, dgain = rms_backward(x_ref[...].astype(F32), gain_ref[...], total)
        out_ref[...] = (g_before_ref[...].astype(F32) + grad).astype(BF16)
        dgain_ref[...] = dgain


def window_backward(m, docs, kept, g, pack_out, before, settle):
    size, width = g.shape
    low = jax.ShapeDtypeStruct((size, width), BF16)
    wide = jax.ShapeDtypeStruct((size, 3 * width), BF16)
    more, arrays = [], []
    if m > 0:
        more = [before_spec(size, 3 * width)] + [IN_VMEM] * 4 + [IN_PLACE]
        arrays = [before, *settle]
    return plain_call(
        functools.partial(window_backward_kernel, m, size),
        [IN_VMEM] * 4 + [IN_PLACE] + more,
        [IN_VMEM] * (4 if m > 0 else 1),
        [wide] + ([low, wide, jax.ShapeDtypeStruct((1, width), F32)] if m > 0 else []),
        ([pltpu.VMEM((width, 3 * width), BF16)] if m > 0 else [])
        + [
            pltpu.VMEM((width, width), BF16),
            pltpu.VMEM((size, width), BF16),
            pltpu.VMEM((size // STEP, 2 * STEP, STEP), F32),
            pltpu.SemaphoreType.DMA((4,)),
        ],
        16 * size * width * width,
    )(docs[2], docs[1], kept, g, pack_out, *arrays)


def blank(shapes):
    return pl.pallas_call(
        lambda *refs: None,
        out_specs=[pl.BlockSpec(memory_space=pl.ANY)] * len(shapes),
        out_shape=[jax.ShapeDtypeStruct(*shape) for shape in shapes],
    )()


def spans(width):
    return (2, width // 2) if width % 256 == 0 else (1, width)


def tile_copies(refs, sems, n, w):
    at = pl.ds(pl.multiple_of(n * w, 128), w)
    made = []
    for i, (a, b, axis) in enumerate(refs):
        cut = (at, slice(None)) if axis == 0 else (slice(None), at)
        made.append(pltpu.make_async_copy(a.at[cut], b.at[cut], sems.at[n, i]))
    return made


def start_all(refs, sems, count, w):
    for n in range(count):
        for copy in tile_copies(refs, sems, n, w):
            copy.start()


def out_copies(wo_ref, wo, sems, count, w):
    rows = wo_ref.shape[0]
    if wo.shape[0] > rows:
        wo[rows:, :] = jnp.zeros((wo.shape[0] - rows, wo.shape[1]), BF16)
    made = []
    for n in range(count):
        cut = pl.ds(n * w, min(w, rows - n * w))
        made.append(pltpu.make_async_copy(wo_ref.at[cut, :], wo.at[cut, :], sems.at[n]))
    return made


def wait_for(copies, n):
    for i, copy in enumerate(copies):
        pl.when(n == i)(copy.wait)


def dense_forward_kernel(
    x_ref,
    gain_ref,
    wg_ref,
    wu_ref,
    wo_ref,
    out_ref,
    gate_ref,
    up_ref,
    wg,
    wu,
    wo,
    gates,
    ups,
    normed,
    total,
    sems,
    out_sems,
    done,
):
    count, w = spans(gates.shape[1])
    reads = [(wg_ref, wg, 1), (wu_ref, wu, 1)]
    writes = [(gates, gate_ref, 1), (ups, up_ref, 1)]
    start_all(reads, sems, count, w)
    outs = out_copies(wo_ref, wo, out_sems, count, w)
    for copy in outs:
        copy.start()
    inputs = x_ref[...].astype(F32)
    normed[...] = rms_forward(inputs, gain_ref[...])
    total[...] = inputs

    def tile(n, carry):
        cut = pl.ds(pl.multiple_of(n * w, 128), w)
        came = tile_copies(reads, sems, n, w)
        came[0].wait()
        gate = nn(normed[...], wg[:, cut])
        came[1].wait()
        up = nn(normed[...], wu[:, cut])
        gates[:, cut] = gate.astype(BF16)
        ups[:, cut] = up.astype(BF16)
        for copy in tile_copies(writes, done, n, w):
            copy.start()
        hidden = (gate * jax.nn.sigmoid(gate) * up).astype(BF16)
        wait_for(outs, n)
        total[...] += nn(hidden, wo[cut, :])
        return carry

    lax.fori_loop(0, count, tile, 0)
    out_ref[...] = total[...].astype(BF16)
    for n in range(count):
        finish(tile_copies(writes, done, n, w))


def weight_scratch(width, padded):
    return [pltpu.VMEM((width, padded), BF16)] * 2 + [pltpu.VMEM((padded, width), BF16)]


def dense_forward(x, gain, weights):
    size, width = x.shape
    padded = weights[1].shape[1]
    tiles = spans(padded)[0]
    return plain_call(
        dense_forward_kernel,
        [IN_VMEM, IN_VMEM] + [IN_PLACE] * 3,
        [IN_VMEM, IN_PLACE, IN_PLACE],
        [jax.ShapeDtypeStruct((size, width), BF16)]
        + [jax.ShapeDtypeStruct((size, padded), BF16)] * 2,
        weight_scratch(width, padded)
        + [pltpu.VMEM((size, padded), BF16)] * 2
        + [pltpu.VMEM((size, width), BF16), pltpu.VMEM((size, width), F32)]
        + [pltpu.SemaphoreType.DMA(shape) for shape in ((tiles, 2), (tiles,), (tiles, 2))],
        6 * size * width * padded,
    )(x, gain, *weights)


def dense_backward_kernel(
    x_ref,
    gain_ref,
    g_ref,
    gate_ref,
    up_ref,
    wg_ref,
    wu_ref,
    wo_ref,
    out_ref,
    dgate_ref,
    dup_ref,
    hidden_ref,
    dgain_ref,
    wg,
    wu,
    wo,
    gates,
    ups,
    dgates,
    dups,
    hiddens,
    total,
    sems,
    out_sems,
    done,
):
    count, w = spans(gates.shape[1])
    reads = [(gate_ref, gates, 1), (up_ref, ups, 1), (wg_ref, wg, 1), (wu_ref, wu, 1)]
    writes = [(hiddens, hidden_ref, 1), (dgates, dgate_ref, 1), (dups, dup_ref, 1)]
    outs = out_copies(wo_ref, wo, out_sems, count, w)
    for copy in outs:
        copy.start()
    start_all(reads, sems, count, w)
    total[...] = jnp.zeros_like(total)

    def tile(n, carry):
        cut = pl.ds(pl.multiple_of(n * w, 128), w)
        came = tile_copies(reads, sems, n, w)
        wait_for(outs, n)
        finish(came[:2])
        dh = nt(g_ref[...], wo[cut, :])
        gate = gates[:, cut].astype(F32)
        up = ups[:, cut].astype(F32)
        sg = jax.nn.sigmoid(gate)
        active = gate * sg
        hiddens[:, cut] = (active * up).astype(BF16)
        dgate = (dh * up * (sg + active * (1.0 - sg))).astype(BF16)
        dup = (dh * active).astype(BF16)
        dgates[:, cut] = dgate
        dups[:, cut] = dup
        for copy in tile_copies(writes, done, n, w):
            copy.start()
        finish(came[2:])
        total[...] += nt(dgate, wg[:, cut]) + nt(dup, wu[:, cut])
        return carry

    lax.fori_loop(0, count, tile, 0)
    grad, dgain = rms_backward(x_ref[...].astype(F32), gain_ref[...], total[...])
    out_ref[...] = (g_ref[...].astype(F32) + grad).astype(BF16)
    dgain_ref[...] = dgain
    for n in range(count):
        finish(tile_copies(writes, done, n, w))


def dense_backward(x, gain, g, gate, up, weights):
    size, width = x.shape
    padded = weights[1].shape[1]
    tiles = spans(padded)[0]
    return plain_call(
        dense_backward_kernel,
        [IN_VMEM] * 3 + [IN_PLACE] * 5,
        [IN_VMEM] + [IN_PLACE] * 3 + [IN_VMEM],
        [jax.ShapeDtypeStruct((size, width), BF16)]
        + [jax.ShapeDtypeStruct((size, padded), BF16)] * 3
        + [jax.ShapeDtypeStruct((1, width), F32)],
        weight_scratch(width, padded)
        + [pltpu.VMEM((size, padded), BF16)] * 5
        + [pltpu.VMEM((size, width), F32)]
        + [pltpu.SemaphoreType.DMA(shape) for shape in ((tiles, 4), (tiles,), (tiles, 3))],
        6 * size * width * padded,
    )(x, gain, g, gate, up, *weights)


def dense_both_kernel(
    x_ref,
    gain_ref,
    g_ref,
    wg_ref,
    wu_ref,
    wo_ref,
    final_ref,
    out_ref,
    dgate_ref,
    dup_ref,
    hidden_ref,
    dgain_ref,
    wg,
    wu,
    wo,
    dgates,
    dups,
    hiddens,
    normed,
    final,
    total,
    sems,
    out_sems,
    done,
):
    count, w = spans(dgates.shape[1])
    reads = [(wg_ref, wg, 1), (wu_ref, wu, 1)]
    writes = [(hiddens, hidden_ref, 1), (dgates, dgate_ref, 1), (dups, dup_ref, 1)]
    start_all(reads, sems, count, w)
    outs = out_copies(wo_ref, wo, out_sems, count, w)
    for copy in outs:
        copy.start()
    inputs = x_ref[...].astype(F32)
    normed[...] = rms_forward(inputs, gain_ref[...])
    final[...] = inputs
    total[...] = jnp.zeros_like(total)

    def tile(n, carry):
        cut = pl.ds(pl.multiple_of(n * w, 128), w)
        came = tile_copies(reads, sems, n, w)
        came[0].wait()
        gate = nn(normed[...], wg[:, cut])
        came[1].wait()
        up = nn(normed[...], wu[:, cut])
        sg = jax.nn.sigmoid(gate)
        active = gate * sg
        hidden = (active * up).astype(BF16)
        hiddens[:, cut] = hidden
        wait_for(outs, n)
        final[...] += nn(hidden, wo[cut, :])
        dh = nt(g_ref[...], wo[cut, :])
        dgate = (dh * up * (sg + active * (1.0 - sg))).astype(BF16)
        dup = (dh * active).astype(BF16)
        dgates[:, cut] = dgate
        dups[:, cut] = dup
        for copy in tile_copies(writes, done, n, w):
            copy.start()
        total[...] += nt(dgate, wg[:, cut]) + nt(dup, wu[:, cut])
        return carry

    lax.fori_loop(0, count, tile, 0)
    final_ref[...] = final[...].astype(BF16)
    grad, dgain = rms_backward(inputs, gain_ref[...], total[...])
    out_ref[...] = (g_ref[...].astype(F32) + grad).astype(BF16)
    dgain_ref[...] = dgain
    for n in range(count):
        finish(tile_copies(writes, done, n, w))


def dense_both(x, gain, g, weights):
    size, width = x.shape
    padded = weights[1].shape[1]
    tiles = spans(padded)[0]
    return plain_call(
        dense_both_kernel,
        [IN_VMEM] * 3 + [IN_PLACE] * 3,
        [IN_VMEM] * 2 + [IN_PLACE] * 3 + [IN_VMEM],
        [jax.ShapeDtypeStruct((size, width), BF16)] * 2
        + [jax.ShapeDtypeStruct((size, padded), BF16)] * 3
        + [jax.ShapeDtypeStruct((1, width), F32)],
        weight_scratch(width, padded)
        + [pltpu.VMEM((size, padded), BF16)] * 3
        + [pltpu.VMEM((size, width), BF16)]
        + [pltpu.VMEM((size, width), F32)] * 2
        + [pltpu.SemaphoreType.DMA(shape) for shape in ((tiles, 2), (tiles,), (tiles, 3))],
        12 * size * width * padded,
    )(x, gain, g, *weights)


def grad_in_kernel(count, tiles, gain_ref, *refs):
    xs, refs = refs[:count], refs[count:]
    groups = [refs[count * n : count * (n + 1)] for n in range(len(tiles))]
    out_ref, turned = refs[count * len(tiles) :]
    step = pl.program_id(0)
    size = xs[0].shape[0]

    @pl.when(step == 0)
    def _():
        for c in range(count):
            normed = rms_forward(xs[c][...].astype(F32), gain_ref[...])
            turned[:, c * size : (c + 1) * size] = normed.astype(F32).T.astype(BF16)

    start = 0
    for parts, (_, used) in zip(groups, tiles):

        @pl.when((step >= start) & (step < start + used))
        def _(parts=parts):
            joined = jnp.concatenate([part[...] for part in parts], axis=0)
            out_ref[...] = nn(turned[...], joined).astype(BF16)

        start += used


def grad_in(gain, xs, groups, out_width, tile):
    count = len(xs)
    size, width = xs[0].shape
    specs = [whole((1, width))] + [whole((size, width))] * count
    arrays, begun = [], 0
    for parts, first, used in groups:

        def at(j, first=first, used=used, begun=begun):
            return (0, first + jnp.clip(j - begun, 0, used - 1))

        specs += [pl.BlockSpec((size, tile), at)] * count
        arrays += parts
        begun += used
    return call(
        functools.partial(grad_in_kernel, count, [group[1:] for group in groups]),
        (begun,),
        specs,
        pl.BlockSpec((width, tile), lambda j: (0, j)),
        jax.ShapeDtypeStruct((width, out_width), BF16),
        [pltpu.VMEM((width, count * size), BF16)],
        2 * count * size * width * tile * begun,
    )(gain, *xs, *arrays)


def grad_out_kernel(count, used, *refs):
    left, right = refs[:count], refs[count : 2 * count]
    out_ref = refs[2 * count]
    step = pl.program_id(0)

    @pl.when(step < used)
    def _():
        joined = jnp.concatenate([part[...] for part in left], axis=0)
        turned = joined.astype(F32).T.astype(BF16)
        out_ref[...] = nn(turned, jnp.concatenate([part[...] for part in right], axis=0)).astype(
            BF16
        )

    @pl.when(step >= used)
    def _():
        out_ref[...] = jnp.zeros_like(out_ref)


def grad_out(left, right, used, rows):
    count = len(left)
    size, width = right[0].shape
    tiles = -(-rows // TILE)
    return call(
        functools.partial(grad_out_kernel, count, used),
        (tiles,),
        [pl.BlockSpec((size, TILE), lambda j: (0, jnp.minimum(j, used - 1)))] * count
        + [whole((size, width))] * count,
        pl.BlockSpec((TILE, width), lambda j: (j, 0)),
        jax.ShapeDtypeStruct((rows, width), BF16),
        [],
        2 * count * size * width * TILE * used,
    )(*left, *right)


def local(tokens, section_in, section_out, gains, bounds, cotangent):
    section = lax.axis_index("section")
    seq = lax.axis_index("seq")
    sections = lax.axis_size("section")
    pack_in = section_in[0]
    pack_out = section_out[0]
    gain_row = gains
    _, block, width = tokens.shape
    hidden_dim = pack_out.shape[0]
    padded = -(-hidden_dim // TILE) * TILE
    length = 2 * block
    size = length // CHUNKS
    taylor_cols = 2 * HEADS * FEAT_DIM + width
    window_cols = 3 * width
    last = sections - 1

    def swapped(two):
        away = lax.dynamic_index_in_dim(two, 1 - seq, 0, keepdims=False)
        own = lax.dynamic_index_in_dim(two, seq, 0, keepdims=False)
        came = lax.ppermute(away, "seq", [(0, 1), (1, 0)])
        return jnp.where(seq == 0, jnp.stack([own, came]), jnp.stack([came, own]))

    def branches(shapes, makers):
        names = list(shapes)

        def branch(maker):
            def run():
                made = maker() if maker is not None else {}
                missing = [name for name in names if name not in made]
                empty = dict(zip(missing, blank([shapes[name] for name in missing]))) if missing else {}
                return tuple(made[name] if name in made else empty[name] for name in names)

            return run

        values = lax.switch(section, [branch(maker) for maker in makers])
        return dict(zip(names, values))

    starts = lax.dynamic_index_in_dim(bounds, seq, 0, keepdims=False)
    positions = jnp.arange(length, dtype=jnp.int32)
    docs = jnp.sum((starts[None, :] <= positions[:, None]).astype(jnp.int32), axis=1)
    docs = (docs[:, None], docs[None, :], window_docs(docs))

    feed = swapped(jnp.where(section == 0, tokens, cotangent)).reshape(length, width)

    def fed(m):
        return feed[m * size : (m + 1) * size]

    first_back = (last + 1) * LAG
    turns = first_back + LAG + CHUNKS + 1
    low = ((size, width), BF16)
    wide = ((size, padded), BF16)
    gain_shape = ((1, width), F32)
    made, sent = [], []

    def prepare():
        up = pack_in[:, hidden_dim:]
        return {"wu": jnp.pad(up, ((0, 0), (0, padded - hidden_dim)))}

    def entry(s, m):
        return fed(m) if s == 0 else sent[m + LAG * (s - 1)]["out"]

    def upstream(s, m):
        if s == last:
            return fed(m)
        if s == 2:
            return sent[m + LAG * last]["out"]
        return sent[first_back + 1 + LAG * (1 - s) + m]["out"]

    def taylor_turn(m):
        def run():
            earlier = [made[i]["linear"] for i in range(m)]
            out, projected, mix, den = taylor_forward(
                m, feed, m, gain_row, docs, pack_in, pack_out, earlier
            )
            return {"out": out, "linear": projected, "mix": mix, "den": den}

        return run

    def dense_turn(m):
        def run():
            out, gate, up = dense_forward(entry(1, m), gain_row, weights)
            return {"out": out, "gate": gate, "up": up}

        return run

    def window_turn(m):
        def run():
            before = made[2 * LAG + m - 1]["window"] if m > 0 else None
            out, projected, mix = window_forward(
                m, entry(2, m), gain_row, docs, pack_in, pack_out, before
            )
            return {"out": out, "window": projected, "mix": mix}

        return run

    def dense_both_turn(m):
        def run():
            final, out, dgate, dup, hidden, gain = dense_both(
                entry(3, m), gain_row, upstream(3, m), weights
            )
            return {
                "final": final,
                "out": out,
                "dgate": dgate,
                "dup": dup,
                "hidden": hidden,
                "gain": gain,
            }

        return run

    def window_back(m):
        def run():
            if m == CHUNKS:
                done = made[first_back + m - 1]["part"]
                grad, gain = rms_backward(
                    entry(2, m - 1).astype(F32), gain_row, nt(done, pack_in[:, :window_cols])
                )
                out = (upstream(2, m - 1).astype(F32) + grad).astype(BF16)
                return {"out": out, "done": done, "gain": gain}
            before = made[2 * LAG + m - 1]["window"] if m > 0 else None
            settle = ()
            if m > 0:
                settle = (
                    made[first_back + m - 1]["part"],
                    entry(2, m - 1),
                    gain_row,
                    upstream(2, m - 1),
                    pack_in,
                )
            results = window_backward(
                m, docs, made[2 * LAG + m]["window"], upstream(2, m), pack_out, before, settle
            )
            values = {"part": results[0]}
            if m > 0:
                values.update(out=results[1], done=results[2], gain=results[3])
            return values

        return run

    def dense_back(m):
        def run():
            kept = made[LAG + m]
            out, dgate, dup, hidden, gain = dense_backward(
                entry(1, m), gain_row, upstream(1, m), kept["gate"], kept["up"], weights
            )
            return {"out": out, "dgate": dgate, "dup": dup, "hidden": hidden, "gain": gain}

        return run

    def taylor_back(ms, earlier):
        dqs = []
        for m in ms:
            dmix = nt(upstream(0, m), pack_out[:width]).astype(BF16)
            dq, dk, dv = taylor_backward(
                m,
                docs,
                [made[i]["linear"] for i in range(m + 1)],
                dmix,
                made[m]["mix"],
                made[m]["den"],
                earlier,
            )
            earlier = (dk, dv)
            dqs.append(dq)
        return dqs, earlier

    def taylor_turn_back(m):
        def run():
            earlier = (made[-1]["dk"], made[-1]["dv"]) if m > 0 else None
            dqs, (dk, dv) = taylor_back([m], earlier)
            return {"dq": dqs[0], "dk": dk, "dv": dv}

        return run

    def spread(two, source):
        share = width // sections
        mine = two[:, :, source * share : (source + 1) * share]
        for target in range(sections):
            if target != source:
                piece = two[:, :, target * share : (target + 1) * share]
                came = lax.ppermute(piece, "section", [(source, target)])
                mine = jnp.where(section == target, came, mine)
        return mine

    taylor_shapes = {}
    for t in range(turns + 1):
        shapes, makers, pairs = {}, [None] * sections, []
        for s in range(sections):
            m = t - LAG * s
            if 0 <= m < CHUNKS:
                shapes["out"] = low
                makers[s] = (taylor_turn, dense_turn, window_turn, dense_both_turn)[s](m)
                if s == 0:
                    shapes.update(linear=((size, taylor_cols), BF16), mix=low)
                    shapes["den"] = ((size, 128), F32)
                elif s == 1:
                    shapes.update(gate=wide, up=wide)
                elif s == 2:
                    shapes.update(window=((size, window_cols), BF16), mix=low)
                else:
                    shapes.update(final=low, dgate=wide, dup=wide, hidden=wide, gain=gain_shape)
                pairs.append((s, s + 1) if s < last else (s, s - 1))
        if t == 0:
            shapes["wu"] = ((width, padded), BF16)
            makers[1] = makers[3] = prepare
        m = t - first_back
        if 0 <= m <= CHUNKS:
            makers[2] = window_back(m)
            if m < CHUNKS:
                shapes["part"] = ((size, window_cols), BF16)
            if m > 0:
                shapes.update(out=low, done=((size, window_cols), BF16), gain=gain_shape)
                pairs.append((2, 1))
        m = t - first_back - 1 - LAG
        if 0 <= m < CHUNKS:
            makers[1] = dense_back(m)
            shapes.update(out=low, dgate=wide, dup=wide, hidden=wide, gain=gain_shape)
            pairs.append((1, 0))
        m = t - first_back - 1 - 2 * LAG
        if 0 <= m < CHUNKS - 1:
            makers[0] = taylor_turn_back(m)
            rows = (m + 1) * size
            taylor_shapes = {
                "dq": ((size, 256), F32),
                "dk": ((rows, 256), F32),
                "dv": ((rows, width), F32),
            }
            shapes.update(taylor_shapes)
        if t == turns:
            break
        made.append(branches(shapes, makers))
        if t == 0:
            weights = (pack_in, made[0]["wu"], pack_out)
        sent.append({"out": lax.ppermute(made[t]["out"], "section", pairs)} if pairs else {})

    def turns_of(s):
        start = (0, first_back + 1 + LAG, first_back + 1, LAG * last)[s]
        return made[start : start + CHUNKS]

    def every(s, name):
        return [value[name] for value in turns_of(s)]

    def gains_of(s):
        return sum(value["gain"] for value in turns_of(s))

    def entries(s):
        return [entry(s, m) for m in range(CHUNKS)]

    def upstreams(s):
        return [upstream(s, m) for m in range(CHUNKS)]

    half = padded // 2
    b_cols = max(taylor_cols, half)
    owners = lax.axis_size("dp") * lax.axis_size("seq")
    a_cols = 3 * half
    a_shape = ((width, a_cols), BF16)
    fold = width // owners
    rest_rows = fold * b_cols // width + hidden_dim // owners
    rest_shape = ((owners, rest_rows, width), BF16)

    def folded(b, c):
        b = b.reshape(owners, fold, b_cols)
        parts = [b[:, :, :width]]
        extra = b_cols - width
        count = width // extra
        step = fold // count
        parts.append(
            jnp.concatenate(
                [b[:, i * step : (i + 1) * step, width:] for i in range(count)], axis=2
            )
        )
        return {"rest": jnp.concatenate(parts + [c.reshape(owners, -1, width)], axis=1)}

    def unfolded(rows):
        extra = b_cols - width
        step = fold * extra // width
        more = rows[fold : fold + step]
        right = jnp.concatenate(
            [more[:, i * extra : (i + 1) * extra] for i in range(width // extra)], axis=0
        )
        return jnp.concatenate([rows[:fold], right], axis=1), rows[fold + step :]

    def dense_first(s):
        def run():
            groups = [(every(s, "dgate"), 0, 2), (every(s, "dup"), 0, 1)]
            return {"a": grad_in(gain_row, entries(s), groups, a_cols, half)}

        return run

    def window_first():
        groups = [(every(2, "done"), 0, 3)]
        return {"a": grad_in(gain_row, entries(2), groups, a_cols, window_cols // 3)}

    def dense_second(s):
        def run():
            groups = [(every(s, "dup"), 1, 1)]
            return folded(
                grad_in(gain_row, entries(s), groups, b_cols, half),
                grad_out(every(s, "hidden"), upstreams(s), padded // TILE, hidden_dim),
            )

        return run

    def window_second():
        mixes = [made[2 * LAG + m]["mix"] for m in range(CHUNKS)]
        (unused,) = blank([((width, b_cols), BF16)])
        return folded(unused, grad_out(mixes, upstreams(2), width // TILE, hidden_dim))

    def taylor_last():
        done = CHUNKS - 1
        dqs, (dk, dv) = taylor_back([done], (made[turns]["dk"], made[turns]["dv"]))
        dqs = [made[turns - done + 1 + m]["dq"] for m in range(done)] + dqs
        grad = jnp.concatenate([jnp.concatenate(dqs, axis=0), dk, dv], axis=1).astype(BF16)
        parts = folded(
            grad_in(gain_row, [feed], [([grad], 0, 2)], b_cols, taylor_cols // 2),
            grad_out(
                [made[m]["mix"] for m in range(CHUNKS)], upstreams(0), width // TILE, hidden_dim
            ),
        )
        return {"linear": grad, **parts}

    def taylor_final():
        came = jnp.concatenate(upstreams(0), axis=0)
        grad_inputs, gain = rms_backward(
            feed.astype(F32), gain_row, nt(rest["linear"], pack_in[:, :taylor_cols])
        )
        return {"returned": (came.astype(F32) + grad_inputs).astype(BF16), "gain": gain}

    made.append(
        branches(
            {"a": a_shape, **taylor_shapes},
            [taylor_turn_back(CHUNKS - 2), dense_first(1), window_first, dense_first(3)],
        )
    )
    axes = ("dp", "seq")
    a, sent[-1]["out"] = lax.optimization_barrier((made[turns]["a"], sent[-1]["out"]))
    sum_a = lax.psum_scatter(a, axes, scatter_dimension=0, tiled=True)
    rest = branches(
        {"rest": rest_shape, "linear": ((length, taylor_cols), BF16)},
        [taylor_last, dense_second(1), window_second, dense_second(3)],
    )
    final = branches(
        {"gain": gain_shape, "returned": ((length, width), BF16)},
        [taylor_final] + [lambda s=s: {"gain": gains_of(s)} for s in (1, 2, 3)],
    )
    sum_a, rest["rest"] = lax.optimization_barrier((sum_a, rest["rest"]))
    sum_b, sum_c = unfolded(
        lax.psum_scatter(rest["rest"], axes, scatter_dimension=0, tiled=True)[0]
    )
    out_gain = lax.psum_scatter(final["gain"][0], axes, scatter_dimension=0, tiled=True)

    finals = [made[LAG * last + m]["final"] for m in range(CHUNKS)]
    block_out = spread(swapped(jnp.concatenate(finals, axis=0).reshape(2, block, width)), last)
    grad_tokens = spread(swapped(final["returned"].reshape(2, block, width)), 0)

    def narrow(value, used):
        return lambda: jnp.pad(value[:, :used].astype(F32), ((0, 0), (0, 2 * hidden_dim - used)))

    def dense_result():
        up_end = padded + hidden_dim - a_cols
        return jnp.concatenate(
            [sum_a[:, :hidden_dim], sum_a[:, padded:], sum_b[:, :up_end]], axis=1
        ).astype(F32)

    out_in = lax.switch(
        section,
        [narrow(sum_b, taylor_cols), dense_result, narrow(sum_a, window_cols), dense_result],
    )
    return (
        block_out,
        grad_tokens,
        out_in[None],
        sum_c.astype(F32)[None],
        out_gain[None],
    )


def solution(mesh):
    placed = (
        P("dp", "seq", None),
        P("section", None, None),
        P("section", None, None),
        P("section", None),
        P("dp", None),
        P("dp", "seq", None),
    )
    return jax.shard_map(
        local,
        mesh=mesh,
        in_specs=placed,
        out_specs=(
            P("dp", "seq", "section"),
            P("dp", "seq", "section"),
            P("section", ("dp", "seq"), None),
            P("section", ("dp", "seq"), None),
            P("section", ("dp", "seq")),
        ),
        check_vma=False,
    )
```

time: 629 us -> 488 us (0.78)
  waiting for transfers between devices: 287 us -> 168 us
  matrix products: 41.4 us -> 17.9 us
    reduce_scatter x1, waiting for transfers between devices: 91.1 us -> 41.2 us  [local(): sum_a = lax.psum_scatter(a, axes, scatter_dimension=0, tiled=True)]
    ppermute x16 -> x15, waiting for transfers between devices: 137 us -> 89.3 us  [local(): lax.ppermute(made[t]['out'], 'section', pairs)]
    dot_general x8 -> x0, matrix products: 25.3 us -> none  [nn(): return jnp.dot(a, b, preferred_element_type=F32)]
    reduce_scatter x2 -> x1, waiting for transfers between devices: 53.9 us -> 34.7 us  [local(): lax.psum_scatter(rest['rest'], axes, scatter_dimension=0, tiled=True)[0]]
    pallas_call x4, Pallas kernels: 52.4 us -> 45.3 us  [taylor_backward(): call(functools.partial(taylor_backward_kernel, m, size, later is not None...]
    another operation x16 -> x18, loops' own time: 68.7 us -> 70.3 us  [branches(): values = lax.switch(section, [branch(maker) for maker in makers])]
    ppermute x16 -> x15, starting transfers between devices: 33.5 us -> 32 us  [local(): lax.ppermute(made[t]['out'], 'section', pairs)]
  transfers between devices with their start and end apart: 28 -> 26, of which waited for: 9 -> 7; matrix products, arithmetic and copies ran while one was open for 6% -> 10% of each run, Pallas kernels for 7% -> 19%
where the time goes in v3:
time: 488 us; the launch traced here: 478 us
  waiting for transfers between devices  168 us (34%)
  Pallas kernels  96.4 us (20%)
  loops' own time  70.3 us (14%)
  starting transfers between devices  48 us (10%)
  other arithmetic  30.7 us (6%)
  matrix products  17.9 us (4%)
  local copies, waits for them, and re-layouts  17.3 us (4%)
  between operations  15.6 us (3%)
  blocking collectives  14.4 us (3%)
    ppermute x15, waiting for transfers between devices, local(): lax.ppermute(made[t]['out'], 'section', pairs)  89.3 us
    another operation x18, loops' own time, branches(): values = lax.switch(section, [branch(maker) for maker in makers])  70.3 us
    pallas_call x4, Pallas kernels, taylor_backward(): call(functools.partial(taylor_backward_kernel, m, size, later is not None...  45.3 us
    reduce_scatter x1, waiting for transfers between devices, local(): sum_a = lax.psum_scatter(a, axes, scatter_dimension=0, tiled=True)  41.2 us
    pallas_call x4, Pallas kernels, taylor_forward(): plain_call(functools.partial(taylor_forward_kernel, m, size), [pl.BlockSp...  38.3 us
    reduce_scatter x1, waiting for transfers between devices, local(): lax.psum_scatter(rest['rest'], axes, scatter_dimension=0, tiled=True)[0]  34.7 us
    ppermute x15, starting transfers between devices, local(): lax.ppermute(made[t]['out'], 'section', pairs)  32 us
    dot_general x5, matrix products, nt(): lax.dot_general(a, b, (((1,), (1,)), ((), ())), preferred_element_type=F32)  17.9 us
  transfers between devices with their start and end apart: 26, of which 7 were waited for; matrix products, arithmetic and copies ran while one was open for 10% of the time, Pallas kernels for 19%

profile of v3, /device:TPU:0, one launch (start us, length us, event | category | flops | bytes accessed | tf_op | source)
XLA Modules:
  0.0 478.3 jit_solution(4139923552263071717)
XLA Ops:
  7.2 1.8 broadcast_select_fusion
  9.9 2.3 collective-permute-done
  12.2 1.9 maximum_select_fusion
  14.1 8.2 %conditional.19 = ((bf16[256,1024]{1,0:T(8,128)(2,1)}, bf16[256,1536]{1,0:T(8,128)(2,1)S(1)}, bf16[256,1024]{1,0:T(8,128)(2,1)}, f32[256,128]{1,0:T(8,128)}, bf16[1024,2816]{1,0:T(8,128)(2,1)})) conditional(s32[]{:T(128)} %clamp.2, (bf16[1024,1024]{1,0:T(8,128)(2,1)S(1)}, f32[1,1024]{1,0:T(1,128)S(1)}, ...), branch_computations={%region_1.2_spmd, %region_2.3_spmd, %region_3.4_spmd, %region_4.5_... | conditional | flops 1342177280 | bytes 22675506 | solution.py:902
  14.3 7.9 %branch_0_fun.25 = (bf16[256,1024]{1,0:T(8,128)(2,1)}, bf16[256,1536]{1,0:T(8,128)(2,1)S(1)}, bf16[256,1024]{1,0:T(8,128)(2,1)}, f32[256,128]{1,0:T(8,128)}) custom-call(bf16[1024,1024]{1,0:T(8,128)(2,1)S(1)} %get-tuple-element.661.x_ref, f32[1,1024]{1,0:T(1,128)S(1)} %get-tuple-element.662.gain_ref, s32[1024,1]{1,0:T(8,128)S(1)} %copy.43.docc, ...), custom_call_target="tpu_custom_call" | custom-call | flops 1342177280 | bytes 2621440 | tf_op jit(solution)/shard_map/cond/branch_0_fun/pallas_call | solution.py:197
  22.3 5.8 %collective-permute-start.1 = (bf16[256,1024]{1,0:T(8,128)(2,1)}, bf16[256,1024]{1,0:T(8,128)(2,1)}, u32[]{:S(2)}, u32[]{:S(2)}) collective-permute-start(bf16[256,1024]{1,0:T(8,128)(2,1)} %get-tuple-element.1285), channel_id=1, source_target_pairs={{0,8},{1,9},{2,10},{3,11},{4,12},{5,13},{6,14},{7,15}} | collective-permute-start | bytes 1572872 | tf_op jit(solution)/shard_map/ppermute | solution.py:1102
  28.1 9.1 %conditional.20 = ((bf16[256,1024]{1,0:T(8,128)(2,1)}, bf16[256,1536]{1,0:T(8,128)(2,1)}, bf16[256,1024]{1,0:T(8,128)(2,1)}, f32[256,128]{1,0:T(8,128)})) conditional(s32[]{:T(128)} %clamp.2, (bf16[1024,1024]{1,0:T(8,128)(2,1)S(1)}, f32[1,1024]{1,0:T(1,128)S(1)}, s32[1024,1]{0,1:T(1,128)S(1)}, ...), branch_computations={%region_5.6_spmd, %region_6.7_spmd, %region_7.8_spmd, %region_8.9_... | conditional | flops 1342177280 | bytes 2629640 | solution.py:902
  28.3 8.8 %branch_0_fun.27 = (bf16[256,1024]{1,0:T(8,128)(2,1)}, bf16[256,1536]{1,0:T(8,128)(2,1)}, bf16[256,1024]{1,0:T(8,128)(2,1)}, f32[256,128]{1,0:T(8,128)}) custom-call(bf16[1024,1024]{1,0:T(8,128)(2,1)S(1)} %get-tuple-element.679.x_ref, f32[1,1024]{1,0:T(1,128)S(1)} %get-tuple-element.680.gain_ref, s32[1024,1]{1,0:T(8,128)S(1)} %copy.44.docc, ...), custom_call_target="tpu_custom_call" | custom-call | flops 1342177280 | bytes 2621440 | tf_op jit(solution)/shard_map/cond/branch_0_fun/pallas_call | solution.py:197
  37.2 2.1 collective-permute-start.4
  39.3 10.7 %conditional.21 = ((bf16[256,1024]{1,0:T(8,128)(2,1)}, bf16[256,1536]{1,0:T(8,128)(2,1)}, bf16[256,1024]{1,0:T(8,128)(2,1)}, f32[256,128]{1,0:T(8,128)}, bf16[25...) conditional(s32[]{:T(128)} %clamp.2, (bf16[1024,1024]{1,0:T(8,128)(2,1)S(1)}, ...), branch_computations={%region_9.10_spmd, %region_10.11_spmd, %region_11.12_spmd, %region... | conditional | flops 4429185024 | bytes 8650808 | solution.py:902
  39.8 10.0 %branch_0_fun.28 = (bf16[256,1024]{1,0:T(8,128)(2,1)}, bf16[256,1536]{1,0:T(8,128)(2,1)}, bf16[256,1024]{1,0:T(8,128)(2,1)}, f32[256,128]{1,0:T(8,128)}) custom-call(bf16[1024,1024]{1,0:T(8,128)(2,1)S(1)} %get-tuple-element.686.x_ref, f32[1,1024]{1,0:T(1,128)S(1)} %get-tuple-element.687.gain_ref, s32[1024,1]{1,0:T(8,128)S(1)} %copy.45.docc, ...), custom_call_target="tpu_custom_call" | custom-call | flops 1342177280 | bytes 2621440 | tf_op jit(solution)/shard_map/cond/branch_0_fun/pallas_call | solution.py:197
  50.0 5.8 %collective-permute-start.2 = (bf16[256,1024]{1,0:T(8,128)(2,1)}, bf16[256,1024]{1,0:T(8,128)(2,1)S(1)}, u32[]{:S(2)}, u32[]{:S(2)}) collective-permute-start(bf16[256,1024]{1,0:T(8,128)(2,1)} %get-tuple-element.1287), channel_id=1, source_target_pairs={{0,8},{8,16},{1,9},{9,17},{2,10},{10,18},{3,11},{11,19},{4,12},{12... | collective-permute-start | bytes 1572872 | tf_op jit(solution)/shard_map/ppermute | solution.py:1102
  55.9 11.8 %conditional.23 = ((bf16[256,1024]{1,0:T(8,128)(2,1)}, bf16[256,1536]{1,0:T(8,128)(2,1)}, bf16[256,1024]{1,0:T(8,128)(2,1)}, f32[256,128]{1,0:T(8,128)}, bf16[25...) conditional(s32[]{:T(128)} %clamp.2, (bf16[1024,1024]{1,0:T(8,128)(2,1)S(1)}, ...), branch_computations={%region_17.18_spmd, %region_18.19_spmd, %region_19.20_spmd, %regio... | conditional | flops 4429185024 | bytes 8650808 | solution.py:902
  56.1 11.5 %branch_0_fun.31 = (bf16[256,1024]{1,0:T(8,128)(2,1)}, bf16[256,1536]{1,0:T(8,128)(2,1)}, bf16[256,1024]{1,0:T(8,128)(2,1)}, f32[256,128]{1,0:T(8,128)}) custom-call(bf16[1024,1024]{1,0:T(8,128)(2,1)S(1)} %get-tuple-element.732.x_ref, f32[1,1024]{1,0:T(1,128)S(1)} %get-tuple-element.733.gain_ref, s32[1024,1]{1,0:T(8,128)S(1)} %copy.47.docc, ...), custom_call_target="tpu_custom_call" | custom-call | flops 1342177280 | bytes 2621440 | tf_op jit(solution)/shard_map/cond/branch_0_fun/pallas_call | solution.py:197
  67.7 2.8 collective-permute-start.5
  70.6 1.5 collective-permute-start.3
  72.1 8.6 %collective-permute-done.5 = bf16[256,1024]{1,0:T(8,128)(2,1)} collective-permute-done((bf16[256,1024]{1,0:T(8,128)(2,1)}, bf16[256,1024]{1,0:T(8,128)(2,1)}, u32[]{:S(2)}, u32[]{:S(2)}) %collective-permute-start.5) | collective-permute-done | bytes 524320 | tf_op jit(solution)/shard_map/ppermute | solution.py:1102
  80.7 5.8 %conditional.24 = ((bf16[256,1024]{1,0:T(8,128)(2,1)}, bf16[256,2816]{1,0:T(8,128)(2,1)}, bf16[256,2816]{1,0:T(8,128)(2,1)}, bf16[256,3072]{1,0:T(8,128)(2,1)}, bf16[256,1024]{1,0:T(8,128)(2,1)})) conditional(s32[]{:T(128)} %clamp.2, () %tuple.301, (bf16[256,1024]{1,0:T(8,128)(2,1)}, f32[1,1024]{1,0:T(1,128)S(1)}, ...), branch_computations={%region_21.22_spmd, %region_22.23_spmd, %region_23.24_spmd, %regio... | conditional | flops 4429185024 | bytes 8650800 | solution.py:902
  86.5 1.5 collective-permute-start.6
  88.0 10.0 %conditional.25 = ((bf16[256,1024]{1,0:T(8,128)(2,1)}, bf16[256,3072]{1,0:T(8,128)(2,1)}, bf16[256,1024]{1,0:T(8,128)(2,1)}, bf16[256,1024]{1,0:T(8,128)(2,1)}, ...) conditional(s32[]{:T(128)} %clamp.2, () %tuple.285, () %tuple.286, ...), branch_computations={%region_25.26_spmd, %region_26.27_spmd, %region_27.28_spmd, %regio... | conditional | flops 8858370048 | bytes 18350152 | solution.py:902
  98.0 1.5 collective-permute-start.7
  99.5 1.5 collective-permute-start.8
  101.0 12.5 %conditional.27 = ((bf16[256,1024]{1,0:T(8,128)(2,1)}, bf16[256,1024]{1,0:T(8,128)(2,1)}, bf16[256,2816]{1,0:T(8,128)(2,1)}, bf16[256,2816]{1,0:T(8,128)(2,1)}, ...) conditional(s32[]{:T(128)} %clamp.2, () %tuple.315, () %tuple.316, ...), branch_computations={%region_33.34_spmd, %region_34.35_spmd, %region_35.36_spmd, %regio... | conditional | flops 8858370048 | bytes 18350144 | solution.py:902
  113.5 1.5 collective-permute-start.14
  115.0 1.5 collective-permute-start.13
  116.4 8.4 %conditional.29 = ((bf16[256,3072]{1,0:T(8,128)(2,1)}, bf16[256,1024]{1,0:T(8,128)(2,1)}, bf16[256,3072]{1,0:T(8,128)(2,1)}, f32[1,1024]{1,0:T(1,128)})) conditional(s32[]{:T(128)} %clamp.2, () %tuple.325, () %tuple.326, (s32[1152,1]{0,1:T(1,128)S(1)}, s32[1,1024]{1,0:T(1,128)S(1)}, bf16[256,3072]{1,0:T(8,128)(2,1)}, ...), branch_computations={%region_41.42_spmd, %region_42.43_spmd, %region_43.44_spmd, %regio... | conditional | flops 4294967296 | bytes 8397832 | solution.py:902
  124.8 1.5 collective-permute-start.16
  127.6 7.5 %conditional.32 = ((bf16[256,1024]{1,0:T(8,128)(2,1)}, bf16[256,3072]{1,0:T(8,128)(2,1)}, f32[1,1024]{1,0:T(1,128)}, bf16[256,2816]{1,0:T(8,128)(2,1)}, bf16[256...) conditional(s32[]{:T(128)} %clamp.2, () %tuple.335, (bf16[256,1024]{1,0:T(8,128)(2,1)}, ...), branch_computations={%region_49.50_spmd, %region_50.51_spmd, %region_51.55_spmd, %regio... | conditional | flops 4429185024 | bytes 12606520 | solution.py:902
  136.5 73.4 %collective-permute-done.15 = bf16[256,1024]{1,0:T(8,128)(2,1)} collective-permute-done((bf16[256,1024]{1,0:T(8,128)(2,1)}, bf16[256,1024]{1,0:T(8,128)(2,1)}, u32[]{:S(2)}, u32[]{:S(2)}) %collective-permute-start.15) | collective-permute-done | bytes 524320 | tf_op jit(solution)/shard_map/ppermute | solution.py:1102
  209.9 9.8 %conditional.31 = ((bf16[256,1024]{1,0:T(8,128)(2,1)}, bf16[256,2816]{1,0:T(8,128)(2,1)}, bf16[256,2816]{1,0:T(8,128)(2,1)}, bf16[256,2816]{1,0:T(8,128)(2,1)}, ...) conditional(s32[]{:T(128)} %clamp.2, ...), branch_computations={%region_56.57_spmd, %region_57.58_spmd, %region_58.59_spmd, %regio... | conditional | flops 4429185024 | bytes 13639808 | solution.py:902
  210.1 2.6 fusion.12.refs_5_
  212.7 6.9 %branch_0_fun.42 = (f32[256,256]{1,0:T(8,128)}, f32[256,256]{1,0:T(8,128)}, f32[256,1024]{1,0:T(8,128)}) custom-call(s32[1024,1]{1,0:T(8,128)S(1)} %copy.55.refs_0_, s32[1,1024]{1,0:T(1,128)S(1)} %get-tuple-element.965.refs_1_, bf16[256,1536]{1,0:T(8,128)(2,1)S(1)} %copy-done.8, bf16[256,1536]{1,0:T(8,128)(2,1)S(1)} %copy-done.8, ...), custom_call_target="tpu_custom_call" | custom-call | flops 2684354560 | bytes 5242880 | tf_op jit(solution)/shard_map/cond/branch_0_fun/pallas_call | solution.py:286
  220.9 7.3 %collective-permute-done.17 = bf16[256,1024]{1,0:T(8,128)(2,1)} collective-permute-done((bf16[256,1024]{1,0:T(8,128)(2,1)}, bf16[256,1024]{1,0:T(8,128)(2,1)}, u32[]{:S(2)}, u32[]{:S(2)}) %collective-permute-start.17) | collective-permute-done | bytes 524320 | tf_op jit(solution)/shard_map/ppermute | solution.py:1102
  228.2 20.1 %conditional.33 = ((bf16[256,1024]{1,0:T(8,128)(2,1)}, bf16[256,2816]{1,0:T(8,128)(2,1)}, bf16[256,2816]{1,0:T(8,128)(2,1)}, bf16[256,2816]{1,0:T(8,128)(2,1)}, ...) conditional(s32[]{:T(128)} %clamp.2, ...), branch_computations={%region_60.61_spmd, %region_61.62_spmd, %region_62.63_spmd, %regio... | conditional | flops 5905842176 | bytes 27271380 | solution.py:902
  228.5 2.6 fusion.17.refs_7_
  231.2 9.4 %branch_0_fun.44 = (f32[256,256]{1,0:T(8,128)}, f32[512,256]{1,0:T(8,128)}, f32[512,1024]{1,0:T(8,128)}) custom-call(s32[1024,1]{1,0:T(8,128)S(1)} %copy.56.refs_0_, s32[1,1024]{1,0:T(1,128)S(1)} %get-tuple-element.996.refs_1_, bf16[256,1536]{1,0:T(8,128)(2,1)S(1)} %copy-done.12, bf16[256,1536]{1,0:T(8,128)(2,1)S(1)} %copy-done.9, ...), custom_call_target="tpu_custom_call" | custom-call | flops 5368709120 | bytes 10485760 | tf_op jit(solution)/shard_map/cond/branch_0_fun/pallas_call | solution.py:286
  249.6 22.9 %conditional.34 = (bf16[1024,4224]{1,0:T(8,128)(2,1)}, f32[256,256]{1,0:T(8,128)}, f32[768,256]{1,0:T(8,128)}, f32[768,1024]{1,0:T(8,128)}) conditional(s32[]{:T(128)} %clamp.2, (bf16[2752,1024]{1,0:T(8,128)(2,1)}, bf16[256,1024]{1,0:T(8,128)(2,1)}, s32[1024,1]{0,1:T(1,128)S(1)}, s32[1,1024]{1,0:T(1,128)S(1)}, ...), branch_computations={%region_64.65_spmd, %region_65.66_spmd, %region_66.67_spmd, %regio... | conditional | flops 8858370048 | bytes 32514220 | solution.py:902
  249.9 2.6 fusion.22.refs_9_
  252.6 13.0 %branch_0_fun.46 = (f32[256,256]{1,0:T(8,128)}, f32[768,256]{1,0:T(8,128)}, f32[768,1024]{1,0:T(8,128)}) custom-call(s32[1024,1]{1,0:T(8,128)S(1)} %copy.57.refs_0_, s32[1,1024]{1,0:T(1,128)S(1)} %get-tuple-element.1025.refs_1_, bf16[256,1536]{1,0:T(8,128)(2,1)S(1)} %copy-done.24, bf16[256,1536]{1,0:T(8,128)(2,1)S(1)} %copy-done.10, ...), custom_call_target="tpu_custom_call" | custom-call | flops 8053063680 | bytes 15728640 | tf_op jit(solution)/shard_map/cond/branch_0_fun/pallas_call | solution.py:286
  273.6 55.9 %conditional.35 = (bf16[8,536,1024]{2,1,0:T(8,128)(2,1)}, bf16[1024,1536]{1,0:T(8,128)(2,1)}) conditional(s32[]{:T(128)} %clamp.2, (f32[256,256]{1,0:T(8,128)}, f32[256,256]{1,0:T(8,128)}, f32[256,256]{1,0:T(8,128)}, bf16[2752,1024]{1,0:T(8,128)(2,1)}, bf16[256,1024]{1,0:T(8,128)(2,1)}, ...), branch_computations={%region_68.69_spmd, %region_69.70_spmd, %region_70.71_spmd, %regio... | conditional | flops 16698834944 | bytes 130425128 | solution.py:902
  273.6 6.3 %branch_0_fun.49 = bf16[2752,1024]{1,0:T(8,128)(2,1)S(1)} custom-call(bf16[256,1024]{1,0:T(8,128)(2,1)} %get-tuple-element.1102.refs_0_, bf16[256,1024]{1,0:T(8,128)(2,1)} %get-tuple-element.1103.refs_1_, bf16[256,1024]{1,0:T(8,128)(2,1)S(1)} %get-tuple-element.1104.refs_2_, bf16[256,1024]{1,0:T(8,128)(2,1)} %get-tuple-element.1095.refs_12_.refs_3_, ...), custom_call_target="tpu_custom_call" | custom-call | flops 2147483648 | bytes 4194304 | tf_op jit(solution)/shard_map/cond/branch_0_fun/pallas_call | solution.py:856
  279.8 2.4 copy-done.2
  282.6 2.7 fusion.27.refs_11_
  286.1 16.0 %branch_0_fun.47 = (f32[256,256]{1,0:T(8,128)S(1)}, f32[1024,256]{1,0:T(8,128)S(1)}, f32[1024,1024]{1,0:T(8,128)S(1)}) custom-call(s32[1024,1]{1,0:T(8,128)S(1)} %copy.58.refs_0_, s32[1,1024]{1,0:T(1,128)S(1)} %get-tuple-element.1088.refs_1_, bf16[256,1536]{1,0:T(8,128)(2,1)S(1)} %copy-done.42, bf16[256,1536]{1,0:T(8,128)(2,1)S(1)} %copy-done.11, ...), custom_call_target="tpu_custom_call" | custom-call | flops 10737418240 | bytes 20971520 | tf_op jit(solution)/shard_map/cond/branch_0_fun/pallas_call | solution.py:286
  303.7 4.6 pad_maximum_fusion.1.refs_1_
  308.3 6.5 %branch_0_fun.48 = bf16[1024,1536]{1,0:T(8,128)(2,1)S(1)} custom-call(f32[1,1024]{1,0:T(1,128)S(1)} %get-tuple-element.1082.gain_ref, bf16[1024,1024]{1,0:T(8,128)(2,1)S(1)} %get-tuple-element.1083.refs_0_, bf16[1024,1536]{1,0:T(8,128)(2,1)} %pad_maximum_fusion.1.refs_1_), custom_call_target="tpu_custom_call" | custom-call | flops 3221225472 | bytes 6291456 | tf_op jit(solution)/shard_map/cond/branch_0_fun/pallas_call | solution.py:823
  315.2 3.9 pad_maximum_fusion
  329.4 41.2 %reduce-scatter.3.cloned.1.call-done = bf16[128,4224]{1,0:T(8,128)(2,1)} async-done(((bf16[1024,4224]{1,0:T(8,128)(2,1)}), bf16[128,4224]{1,0:T(8,128)(2,1)}) %reduce-scatter.3.cloned.1.call-update) | async-done | bytes 1081360 | tf_op jit(solution)/shard_map/reduce_scatter | solution.py:1205
  374.4 12.5 %conditional.36 = (f32[1,1024]{1,0:T(1,128)S(1)}, bf16[2,512,1024]{2,1,0:T(8,128)(2,1)}) conditional(s32[]{:T(128)} %clamp.2, (bf16[1024,5504]{1,0:T(8,128)(2,1)}, bf16[1024,1536]{1,0:T(8,128)(2,1)}, bf16[1024,1024]{1,0:T(8,128)(2,1)S(1)}, bf16[256,1024]{1,0:T(8,128)(2,1)}, bf16[256,1024]{1,0:T(8,128)(2,1)}, ...), branch_computations={%region_72.76_spmd, %region_76.77_spmd, %region_77.78_spmd, %regio... | conditional | flops 3248490496 | bytes 25223184 | solution.py:902
  375.0 7.3 %fusion.37 = (f32[1024]{0:T(1024)S(1)}, f32[1024]{0:T(1024)S(1)}, f32[1024,1024]{1,0:T(8,128)S(1)}) fusion(bf16[1024,1024]{1,0:T(8,128)(2,1)S(1)} %get-tuple-element.1149, f32[1024]{0:T(1024)S(1)} %bitcast.148, f32[1024]{0:T(1024)S(1)} %get-tuple-element.1848, bf16[1024,1536]{1,0:T(8,128)(2,1)} %get-tuple-element.1147, ...), kind=kOutput, calls=%fused_computation.45 | convolution fusion | flops 3228563456 | bytes 12599296 | tf_op jit(solution)/shard_map/cond/branch_0_fun/dot_general | solution.py:28
  382.3 4.7 fusion.36
  387.0 1.8 constant_dynamic-slice_fusion
  389.5 1.9 maximum_select_fusion.1
  393.0 1.5 collective-permute-start.11
  398.7 7.0 %collective-permute-start.21 = (bf16[2,512,256]{2,1,0:T(8,128)(2,1)}, bf16[2,512,256]{2,1,0:T(8,128)(2,1)}, u32[]{:S(2)}, u32[]{:S(2)}) collective-permute-start(bf16[2,512,256]{2,1,0:T(8,128)(2,1)} %get-tuple-element.1852), channel_id=1, source_target_pairs={{0,24},{1,25},{2,26},{3,27},{4,28},{5,29},{6,30},{7,31}} | collective-permute-start | bytes 1572872 | tf_op jit(solution)/shard_map/ppermute | solution.py:1049
  405.7 2.1 collective-permute-start.22
  407.8 2.1 collective-permute-start.23
  411.2 2.0 fusion.43
  413.2 14.4 %all-reduce.5 = f32[1024]{0:T(1024)S(1)} all-reduce(f32[1024]{0:T(1024)S(1)} %bitcast.185), channel_id=4, replica_groups=mesh['section'=4,'dp'=4,'seq'=2] {'dp','seq'}, use_global_device_ids=true, to_apply=%region_85.86.clone | all-reduce | flops 1024 | bytes 8192
  428.2 2.0 fusion.41
  430.3 34.7 %reduce-scatter.5.cloned.1.call-done = bf16[1,536,1024]{2,1,0:T(8,128)(2,1)} async-done(((bf16[8,536,1024]{2,1,0:T(8,128)(2,1)}), bf16[1,536,1024]{2,1,0:T(8,128)(2,1)}) %reduce-scatter.5.cloned.1.call-update) | async-done | bytes 1097744 | tf_op jit(solution)/shard_map/reduce_scatter | solution.py:1216
  466.9 1.8 conditional.37
  466.9 1.7 bitcast_convert_fusion
  468.6 2.4 slice_convert_fusion
  (173 shorter events, 25.5 us)
Async XLA Ops:
  7.2 2.6 copy-start
  7.2 363.4 %reduce-scatter.3.cloned.1.call-start = ((), (), s32[]{:S(2)}) async-start(), calls=%async_computation.2 | async-start | bytes 9732096 | tf_op jit(solution)/shard_map/reduce_scatter | solution.py:1205
  9.2 2.9 collective-permute-start
  12.2 1.9 copy-start.15
  22.3 17.1 %copy-start.7 = (bf16[256,1536]{1,0:T(8,128)(2,1)}, bf16[256,1536]{1,0:T(8,128)(2,1)S(1)}, u32[]{:S(2)}) copy-start(bf16[256,1536]{1,0:T(8,128)(2,1)S(1)} %get-tuple-element.1283) | copy-start | bytes 2359300
  22.3 17.1 %collective-permute-start.1 = (bf16[256,1024]{1,0:T(8,128)(2,1)}, bf16[256,1024]{1,0:T(8,128)(2,1)}, u32[]{:S(2)}, u32[]{:S(2)}) collective-permute-start(bf16[256,1024]{1,0:T(8,128)(2,1)} %get-tuple-element.1285), channel_id=1, source_target_pairs={{0,8},{1,9},{2,10},{3,11},{4,12},{5,13},{6,14},{7,15}} | collective-permute-start | bytes 1572872 | tf_op jit(solution)/shard_map/ppermute | solution.py:1102
  37.2 18.7 %collective-permute-start.4 = (bf16[256,1024]{1,0:T(8,128)(2,1)}, bf16[256,1024]{1,0:T(8,128)(2,1)}, u32[]{:S(2)}, u32[]{:S(2)}) collective-permute-start(bf16[256,1024]{1,0:T(8,128)(2,1)} %get-tuple-element.1290), channel_id=1, source_target_pairs={{0,8},{1,9},{2,10},{3,11},{4,12},{5,13},{6,14},{7,15}} | collective-permute-start | bytes 1572872 | tf_op jit(solution)/shard_map/ppermute | solution.py:1102
  50.0 20.5 %collective-permute-start.2 = (bf16[256,1024]{1,0:T(8,128)(2,1)}, bf16[256,1024]{1,0:T(8,128)(2,1)S(1)}, u32[]{:S(2)}, u32[]{:S(2)}) collective-permute-start(bf16[256,1024]{1,0:T(8,128)(2,1)} %get-tuple-element.1287), channel_id=1, source_target_pairs={{0,8},{8,16},{1,9},{9,17},{2,10},{10,18},{3,11},{11,19},{4,12},{12... | collective-permute-start | bytes 1572872 | tf_op jit(solution)/shard_map/ppermute | solution.py:1102
  67.7 13.0 %collective-permute-start.5 = (bf16[256,1024]{1,0:T(8,128)(2,1)}, bf16[256,1024]{1,0:T(8,128)(2,1)}, u32[]{:S(2)}, u32[]{:S(2)}) collective-permute-start(bf16[256,1024]{1,0:T(8,128)(2,1)} %get-tuple-element.1291), channel_id=1, source_target_pairs={{0,8},{8,16},{1,9},{9,17},{2,10},{10,18},{3,11},{11,19},{4,12},{12... | collective-permute-start | bytes 1572872 | tf_op jit(solution)/shard_map/ppermute | solution.py:1102
  70.6 17.4 %collective-permute-start.3 = (bf16[256,1024]{1,0:T(8,128)(2,1)}, bf16[256,1024]{1,0:T(8,128)(2,1)}, u32[]{:S(2)}, u32[]{:S(2)}) collective-permute-start(bf16[256,1024]{1,0:T(8,128)(2,1)} %get-tuple-element.1288), channel_id=1, source_target_pairs={{8,16},{16,24},{9,17},{17,25},{10,18},{18,26},{11,19},{19,27},{12,... | collective-permute-start | bytes 1572872 | tf_op jit(solution)/shard_map/ppermute | solution.py:1102
  86.5 13.0 %collective-permute-start.6 = (bf16[256,1024]{1,0:T(8,128)(2,1)}, bf16[256,1024]{1,0:T(8,128)(2,1)}, u32[]{:S(2)}, u32[]{:S(2)}) collective-permute-start(bf16[256,1024]{1,0:T(8,128)(2,1)} %get-tuple-element.1295), channel_id=1, source_target_pairs={{8,16},{16,24},{9,17},{17,25},{10,18},{18,26},{11,19},{19,27},{12,... | collective-permute-start | bytes 1572872 | tf_op jit(solution)/shard_map/ppermute | solution.py:1102
  98.0 2.9 collective-permute-start.7
  99.5 15.4 %collective-permute-start.8 = (bf16[256,1024]{1,0:T(8,128)(2,1)}, bf16[256,1024]{1,0:T(8,128)(2,1)}, u32[]{:S(2)}, u32[]{:S(2)}) collective-permute-start(bf16[256,1024]{1,0:T(8,128)(2,1)} %get-tuple-element.1300), channel_id=1, source_target_pairs={{16,24},{24,16},{17,25},{25,17},{18,26},{26,18},{19,27},{27,19},{2... | collective-permute-start | bytes 1572872 | tf_op jit(solution)/shard_map/ppermute | solution.py:1102
  113.5 2.9 collective-permute-start.14
  115.0 11.4 %collective-permute-start.13 = (bf16[256,1024]{1,0:T(8,128)(2,1)}, bf16[256,1024]{1,0:T(8,128)(2,1)}, u32[]{:S(2)}, u32[]{:S(2)}) collective-permute-start(bf16[256,1024]{1,0:T(8,128)(2,1)} %get-tuple-element.1303), channel_id=1, source_target_pairs={{24,16},{16,8},{25,17},{17,9},{26,18},{18,10},{27,19},{19,11},{28,... | collective-permute-start | bytes 1572872 | tf_op jit(solution)/shard_map/ppermute | solution.py:1102
  124.8 2.8 collective-permute-start.16
  126.3 83.5 %collective-permute-start.15 = (bf16[256,1024]{1,0:T(8,128)(2,1)}, bf16[256,1024]{1,0:T(8,128)(2,1)}, u32[]{:S(2)}, u32[]{:S(2)}) collective-permute-start(bf16[256,1024]{1,0:T(8,128)(2,1)} %get-tuple-element.1310), channel_id=1, source_target_pairs={{16,8},{8,0},{17,9},{9,1},{18,10},{10,2},{19,11},{11,3},{20,12},{1... | collective-permute-start | bytes 1572872 | tf_op jit(solution)/shard_map/ppermute | solution.py:1102
  127.6 82.2 %copy-start.45 = (f32[256,128]{1,0:T(8,128)S(1)}, f32[256,128]{1,0:T(8,128)}, u32[]{:S(2)}) copy-start(f32[256,128]{1,0:T(8,128)} %get-tuple-element.1312) | copy-start | bytes 393220
  135.2 93.0 %collective-permute-start.17 = (bf16[256,1024]{1,0:T(8,128)(2,1)}, bf16[256,1024]{1,0:T(8,128)(2,1)}, u32[]{:S(2)}, u32[]{:S(2)}) collective-permute-start(bf16[256,1024]{1,0:T(8,128)(2,1)} %get-tuple-element.1320), channel_id=1, source_target_pairs={{16,8},{8,0},{17,9},{9,1},{18,10},{10,2},{19,11},{11,3},{20,12},{1... | collective-permute-start | bytes 1572872 | tf_op jit(solution)/shard_map/ppermute | solution.py:1102
  209.9 18.3 %copy-start.46 = (f32[256,128]{1,0:T(8,128)S(1)}, f32[256,128]{1,0:T(8,128)}, u32[]{:S(2)}) copy-start(f32[256,128]{1,0:T(8,128)} %get-tuple-element.1322) | copy-start | bytes 393220
  210.1 2.6 copy-start.8
  210.1 2.6 copy-start.29
  219.6 29.9 %collective-permute-start.18 = (bf16[256,1024]{1,0:T(8,128)(2,1)}, bf16[256,1024]{1,0:T(8,128)(2,1)}, u32[]{:S(2)}, u32[]{:S(2)}) collective-permute-start(bf16[256,1024]{1,0:T(8,128)(2,1)} %get-tuple-element.1328), channel_id=1, source_target_pairs={{8,0},{9,1},{10,2},{11,3},{12,4},{13,5},{14,6},{15,7}} | collective-permute-start | bytes 1572872 | tf_op jit(solution)/shard_map/ppermute | solution.py:1102
  228.2 21.4 %copy-start.43 = (f32[256,128]{1,0:T(8,128)S(1)}, f32[256,128]{1,0:T(8,128)}, u32[]{:S(2)}) copy-start(f32[256,128]{1,0:T(8,128)} %get-tuple-element.1330) | copy-start | bytes 393220
  228.4 2.7 copy-start.9
  228.4 2.7 copy-start.12
  228.4 2.7 copy-start.30
  228.4 2.7 copy-start.49
  228.5 2.7 copy-start.51
  248.3 24.2 %collective-permute-start.19 = (bf16[256,1024]{1,0:T(8,128)(2,1)}, bf16[256,1024]{1,0:T(8,128)(2,1)}, u32[]{:S(2)}, u32[]{:S(2)}) collective-permute-start(bf16[256,1024]{1,0:T(8,128)(2,1)} %get-tuple-element.1355), channel_id=1, source_target_pairs={{8,0},{9,1},{10,2},{11,3},{12,4},{13,5},{14,6},{15,7}} | collective-permute-start | bytes 1572872 | tf_op jit(solution)/shard_map/ppermute | solution.py:1102
  249.8 2.7 copy-start.10
  249.9 2.7 copy-start.13
  249.9 2.7 copy-start.24
  249.9 2.7 copy-start.27
  249.9 2.7 copy-start.50
  272.5 192.4 %reduce-scatter.5.cloned.1.call-start = ((), (), s32[]{:S(2)}) async-start(), calls=%async_computation.3 | async-start | bytes 9879552 | tf_op jit(solution)/shard_map/reduce_scatter | solution.py:1216
  279.8 2.4 copy-start.2
  282.5 2.8 copy-start.11
  282.5 2.8 copy-start.14
  282.5 3.0 copy-start.25
  282.5 3.2 copy-start.28
  282.6 3.5 copy-start.42
  303.7 11.5 %slice-start = ((s8[5636096]{0:T(1024)(128)(4,1)}), s8[4194304]{0:T(1024)(128)(4,1)S(1)}, s32[]{:S(2)}) async-start(s8[5636096]{0:T(1024)(128)(4,1)} %bitcast.65), calls=%async_computation.4 | async-start | bytes 8388608 | tf_op jit(solution)/shard_map/cond
  308.3 6.9 %slice-start.1 = ((s8[5636096]{0:T(1024)(128)(4,1)}), s8[1441792]{0:T(1024)(128)(4,1)S(1)}, s32[]{:S(2)}) async-start(s8[5636096]{0:T(1024)(128)(4,1)} %bitcast.65), calls=%async_computation.5 | async-start | bytes 2883584 | tf_op jit(solution)/shard_map/cond
  370.6 1.2 copy-start.32
  373.2 1.2 copy-start.35
  373.2 1.2 copy-start.36
  373.2 1.2 copy-start.37
  373.2 1.2 copy-start.38
  373.2 1.2 copy-start.39
  373.2 1.2 copy-start.40
  373.2 1.2 copy-start.41
  374.4 15.1 %collective-permute-start.9 = (bf16[512,1024]{1,0:T(8,128)(2,1)}, bf16[512,1024]{1,0:T(8,128)(2,1)}, u32[]{:S(2)}, u32[]{:S(2)}) collective-permute-start(bf16[512,1024]{1,0:T(8,128)(2,1)} %get-tuple-element.1859), channel_id=1, source_target_pairs={{0,1},{1,0},{2,3},{3,2},{4,5},{5,4},{6,7},{7,6},{8,9},{9,8},{10,11... | collective-permute-start | bytes 3145736 | tf_op jit(solution)/shard_map/ppermute | solution.py:887
  388.7 7.0 %collective-permute-start.20 = (bf16[512,1024]{1,0:T(8,128)(2,1)S(1)}, bf16[512,1024]{1,0:T(8,128)(2,1)S(1)}, u32[]{:S(2)}, u32[]{:S(2)}) collective-permute-start(bf16[512,1024]{1,0:T(8,128)(2,1)S(1)} %get-tuple-element.1854), channel_id=1, source_target_pairs={{0,1},{1,0},{2,3},{3,2},{4,5},{5,4},{6,7},{7,6},{8,9},{9,8},{10,11... | collective-permute-start | bytes 3145736 | tf_op jit(solution)/shard_map/ppermute | solution.py:887
  392.3 15.5 %collective-permute-start.10 = (bf16[2,512,256]{2,1,0:T(8,128)(2,1)S(1)}, bf16[2,512,256]{2,1,0:T(8,128)(2,1)S(1)}, u32[]{:S(2)}, u32[]{:S(2)}) collective-permute-start(bf16[2,512,256]{2,1,0:T(8,128)(2,1)S(1)} %get-tuple-element.1857), channel_id=1, source_target_pairs={{24,16},{25,17},{26,18},{27,19},{28,20},{29,21},{30,22},{31,23}} | collective-permute-start | bytes 1572872 | tf_op jit(solution)/shard_map/ppermute | solution.py:1049
  393.0 18.2 %collective-permute-start.11 = (bf16[2,512,256]{2,1,0:T(8,128)(2,1)}, bf16[2,512,256]{2,1,0:T(8,128)(2,1)}, u32[]{:S(2)}, u32[]{:S(2)}) collective-permute-start(bf16[2,512,256]{2,1,0:T(8,128)(2,1)} %get-tuple-element.1856), channel_id=1, source_target_pairs={{24,8},{25,9},{26,10},{27,11},{28,12},{29,13},{30,14},{31,15}} | collective-permute-start | bytes 1572872 | tf_op jit(solution)/shard_map/ppermute | solution.py:1049
  394.5 16.7 %collective-permute-start.12 = (bf16[2,512,256]{2,1,0:T(8,128)(2,1)S(1)}, bf16[2,512,256]{2,1,0:T(8,128)(2,1)}, u32[]{:S(2)}, u32[]{:S(2)}) collective-permute-start(bf16[2,512,256]{2,1,0:T(8,128)(2,1)S(1)} %get-tuple-element.1855), channel_id=1, source_target_pairs={{24,0},{25,1},{26,2},{27,3},{28,4},{29,5},{30,6},{31,7}} | collective-permute-start | bytes 1572872 | tf_op jit(solution)/shard_map/ppermute | solution.py:1049
  396.1 1.3 copy-start.5
  397.4 12.4 %copy-start.52 = (u32[32]{0:T(128)S(1)}, u32[32]{0:T(128)}, u32[]{:S(2)}) copy-start(u32[32]{0:T(128)} %constant.86) | copy-start | bytes 388
  398.7 29.5 %collective-permute-start.21 = (bf16[2,512,256]{2,1,0:T(8,128)(2,1)}, bf16[2,512,256]{2,1,0:T(8,128)(2,1)}, u32[]{:S(2)}, u32[]{:S(2)}) collective-permute-start(bf16[2,512,256]{2,1,0:T(8,128)(2,1)} %get-tuple-element.1852), channel_id=1, source_target_pairs={{0,24},{1,25},{2,26},{3,27},{4,28},{5,29},{6,30},{7,31}} | collective-permute-start | bytes 1572872 | tf_op jit(solution)/shard_map/ppermute | solution.py:1049
  405.7 22.5 %collective-permute-start.22 = (bf16[2,512,256]{2,1,0:T(8,128)(2,1)}, bf16[2,512,256]{2,1,0:T(8,128)(2,1)}, u32[]{:S(2)}, u32[]{:S(2)}) collective-permute-start(bf16[2,512,256]{2,1,0:T(8,128)(2,1)} %get-tuple-element.1851), channel_id=1, source_target_pairs={{0,16},{1,17},{2,18},{3,19},{4,20},{5,21},{6,22},{7,23}} | collective-permute-start | bytes 1572872 | tf_op jit(solution)/shard_map/ppermute | solution.py:1049
  407.8 20.4 %collective-permute-start.23 = (bf16[2,512,256]{2,1,0:T(8,128)(2,1)}, bf16[2,512,256]{2,1,0:T(8,128)(2,1)}, u32[]{:S(2)}, u32[]{:S(2)}) collective-permute-start(bf16[2,512,256]{2,1,0:T(8,128)(2,1)} %get-tuple-element.1850), channel_id=1, source_target_pairs={{0,8},{1,9},{2,10},{3,11},{4,12},{5,13},{6,14},{7,15}} | collective-permute-start | bytes 1572872 | tf_op jit(solution)/shard_map/ppermute | solution.py:1049
  428.2 38.7 %copy-start.6 = (bf16[128,4224]{1,0:T(8,128)(2,1)S(1)}, bf16[128,4224]{1,0:T(8,128)(2,1)}, u32[]{:S(2)}) copy-start(bf16[128,4224]{1,0:T(8,128)(2,1)} %reduce-scatter.3.cloned.1.call-done) | copy-start | bytes 3244036
  468.6 2.4 copy-start.1
  (5 other events, 5.4 us)
Sparse Core Ops, SparseCore 0:
  272.7 97.8 reduce-scatter.2
  372.9 91.9 reduce-scatter.4
